TPU v7x, 512 devices: a whole 4x4x16 slice. The times are simulated.
512 devices in a mesh: dp: 32 (over z_lo, y), tensor: 16 (over x, z_hi, core).
Axes of the slice: x: 4, y: 4, z: 16 (z_hi: 2, z_lo: 8; z = z_hi * 8 + z_lo), core: 2. Of those that a mesh axis runs over, the one named last changes fastest.
Arguments:
- tokens: bfloat16 [15360, 4096], P('dp'), may hold values from -6 to 6
- gate_weight: bfloat16 [4096, 14336], P('dp', 'tensor'), may hold values from -0.09375 to 0.09375
- up_weight: bfloat16 [4096, 14336], P('dp', 'tensor'), may hold values from -0.09375 to 0.09375
- out_grad: bfloat16 [15360, 4096], P('dp', 'tensor'), may hold values from -6 to 6
- in_factor: bfloat16 [14336, 64], P('tensor'), may hold values from -0.046875 to 0.046875
- out_factor: bfloat16 [4096, 64], P('tensor'), may hold values from -0.09375 to 0.09375
- queries: bfloat16 [1024, 4096], P('dp', 'tensor'), may hold values from -6 to 6
Outputs:
- scores: float32 [1024, 96], P('dp')
All inputs are finite; a program needn't handle non-finite values.
Results may differ from a plain program's by a relative error of at most 0.003.
Values may be sent and summed in bfloat16 or wider, within the bound.
No kernel may reach another device: no remote copies, remote signals or barrier semaphores. Data moves between devices by JAX's collectives and lax.ppermute only.
A program may use at most 64 MiB of HBM per device.

v0:
```python
import jax
import jax.numpy as jnp
from jax import lax
from jax.sharding import PartitionSpec as P

LEN = 160


damping = 0.1


def solve_kernel(kernel, cross):
    factor = jnp.linalg.cholesky(kernel)
    lower_solved = lax.linalg.triangular_solve(factor, cross.T, left_side=True, lower=True)
    result = lax.linalg.triangular_solve(
        factor, lower_solved, left_side=True, lower=True, transpose_a=True
    )
    return result.T


def seq_outer(left, right, local_seqs):
    left_seqs = left.reshape(local_seqs, LEN, left.shape[1])
    right_seqs = right.reshape(local_seqs, LEN, right.shape[1])
    outer = jnp.einsum("sti,stj->sij", left_seqs, right_seqs, precision=lax.Precision.HIGHEST)
    return outer.reshape(local_seqs, -1) / jnp.sqrt(jnp.float32(LEN))


def shards(tokens, gate_weight, up_weight, out_grad, in_factor, out_factor, queries):
    rows = tokens.shape[0]
    first = jnp.dot(
        tokens,
        lax.all_gather(gate_weight, "dp", axis=0, tiled=True),
        preferred_element_type=jnp.float32,
    )
    second = jnp.dot(
        tokens,
        lax.all_gather(up_weight, "dp", axis=0, tiled=True),
        preferred_element_type=jnp.float32,
    )
    hidden = (jax.nn.silu(first) * second).astype(jnp.bfloat16)
    in_part = jnp.dot(hidden, in_factor, preferred_element_type=jnp.float32)
    out_part = jnp.dot(out_grad, out_factor, preferred_element_type=jnp.float32)
    rank = in_factor.shape[1]
    local_seqs = rows // LEN
    block_cols = queries.shape[1]
    total_feat = rank * rank
    query_rows = queries.astype(jnp.float32)
    in_proj, out_proj = lax.psum((in_part, out_part), "tensor")
    fragment = seq_outer(in_proj, out_proj, local_seqs)
    features = lax.all_gather(fragment, "dp", axis=0, tiled=True)
    kernel = jnp.dot(features, features.T, precision=lax.Precision.HIGHEST)
    start = lax.axis_index("tensor") * block_cols
    block = lax.dynamic_slice_in_dim(features, start, block_cols, 1)
    cross = lax.psum(jnp.dot(query_rows, block.T, precision=lax.Precision.HIGHEST), "tensor")
    count = kernel.shape[0]
    kernel = kernel / total_feat + damping * jnp.eye(count, dtype=jnp.float32)
    cross = cross / jnp.sqrt(jnp.float32(total_feat))
    return solve_kernel(kernel, cross)


def solution(mesh):
    in_specs = (
        P("dp", None),
        P("dp", "tensor"),
        P("dp", "tensor"),
        P("dp", "tensor"),
        P("tensor", None),
        P("tensor", None),
        P("dp", "tensor"),
    )
    out_specs = P("dp", None)
    return jax.shard_map(shards, mesh=mesh, in_specs=in_specs, out_specs=out_specs, check_vma=False)
```

profile of v0, /device:TPU:1, one launch (start us, length us, event | category | flops | bytes accessed | tf_op | source)
XLA Modules:
  0.0 1118.7 jit_solution(16442771558223949600)
XLA Ops:
  6.5 0.0 copy-start
  6.5 0.0 all-gather.5.cloned.1.call-start
  6.5 0.7 all-gather.5.cloned.1.call-update
  7.3 0.0 all-gather.7.cloned.1.call-start
  7.3 0.7 all-gather.7.cloned.1.call-update
  8.0 0.0 all-reduce.3.cloned.1.call-start
  8.1 0.0 copy-done
  8.1 1.0 fusion.16
  9.0 0.2 reshape.21
  9.2 0.7 copy.17
  9.9 0.0 copy-start.2
  9.9 221.5 %all-gather.5.cloned.1.call-done = bf16[4096,896]{1,0:T(8,128)(2,1)} async-done(((bf16[128,896]{1,0:T(8,128)(2,1)}), bf16[4096,896]{1,0:T(8,128)(2,1)}) %all-gather.5.cloned.1.call-update) | async-done | bytes 7340048 | tf_op jit(solution)/shard_map/all_gather | solution.py:32
  231.5 9.3 fusion.15
  240.8 226.4 %all-gather.7.cloned.1.call-done = bf16[4096,896]{1,0:T(8,128)(2,1)} async-done(((bf16[128,896]{1,0:T(8,128)(2,1)}), bf16[4096,896]{1,0:T(8,128)(2,1)}) %all-gather.7.cloned.1.call-update) | async-done | bytes 7340048 | tf_op jit(solution)/shard_map/all_gather | solution.py:37
  467.2 0.0 copy-done.2
  467.2 8.8 fusion
  476.0 0.2 reshape.20
  476.1 0.7 copy.16
  476.9 0.0 all-reduce.3.cloned.1.call-update
  476.9 0.2 all-gather.9.cloned.1.call-start
  477.1 273.0 %all-reduce.3.cloned.1.call-done = (f32[3,160,64]{1,2,0:T(8,128)}, f32[3,160,64]{1,2,0:T(8,128)}) async-done(((f32[3,160,64]{1,2,0:T(8,128)}, f32[3,160,64]{1,2,0:T(8,128)}), (f32[3,160,64]{1,2,0:T(8,128)}, f32[3,160,64]{1,2,0:T(8,128)})) %all-reduce.3.cloned.1.call-update) | async-done | bytes 245776 | tf_op jit(solution)/shard_map/psum | solution.py:48
  750.1 1.3 convolution_multiply_fusion
  751.5 0.7 reshape.22
  752.2 0.0 all-gather.9.cloned.1.call-update
  752.2 203.6 %all-gather.9.cloned.1.call-done = f32[32,3,4096]{2,1,0:T(4,128)} async-done(((f32[1,3,4096]{2,1,0:T(4,128)}), f32[32,3,4096]{2,1,0:T(4,128)}) %all-gather.9.cloned.1.call-update) | async-done | bytes 1572880 | tf_op jit(solution)/shard_map/all_gather | solution.py:50
  955.9 2.0 reshape.23
  957.9 0.0 copy-start.1
  957.9 1.4 convolution_multiply_fusion.1
  959.3 0.1 copy.19
  959.4 8.8 cholesky.16
  968.2 0.6 compare_reduce_fusion
  968.9 0.7 fusion.3
  969.5 7.4 custom-call.8
  976.9 0.0 copy-done.1
  976.9 0.2 convolution_bitcast_fusion
  977.1 134.1 %psum.23 = f32[32,96]{1,0:T(8,128)S(1)} all-reduce(f32[32,96]{1,0:T(8,128)S(1)} %convolution_bitcast_fusion), channel_id=1, replica_groups=mesh['dp'=32,'tensor'=16] {'tensor'}, use_global_device_ids=true, to_apply=%region_4.5 | all-reduce | flops 3072 | bytes 24576 | tf_op jit(solution)/shard_map/psum | solution.py:54
  1111.2 0.1 fusion.6
  1111.4 0.8 fusion.4
  (2 shorter events, 0.1 us)
Async XLA Ops:
  6.5 1.5 copy-start
  6.5 224.9 %all-gather.5.cloned.1.call-start = ((), (), s32[]{:S(2)}) async-start(), calls=%async_computation | async-start | bytes 7569408 | tf_op jit(solution)/shard_map/all_gather | solution.py:32
  7.3 459.9 %all-gather.7.cloned.1.call-start = ((), (), s32[]{:S(2)}) async-start(), calls=%async_computation.1 | async-start | bytes 7569408 | tf_op jit(solution)/shard_map/all_gather | solution.py:37
  8.0 742.1 %all-reduce.3.cloned.1.call-start = ((), (), s32[]{:S(2)}) async-start(), calls=%async_computation.3 | async-start | bytes 786432 | tf_op jit(solution)/shard_map/psum | solution.py:48
  9.9 457.3 %copy-start.2 = (bf16[896,64]{0,1:T(8,128)(2,1)S(1)}, bf16[896,64]{0,1:T(8,128)(2,1)}, u32[]{:S(2)}) copy-start(bf16[896,64]{0,1:T(8,128)(2,1)} %param.11) | copy-start | bytes 344068
  476.9 479.0 %all-gather.9.cloned.1.call-start = ((), (), s32[]{:S(2)}) async-start(), calls=%async_computation.2 | async-start | bytes 2162688 | tf_op jit(solution)/shard_map/all_gather | solution.py:50
  957.9 19.0 %copy-start.1 = (bf16[32,256]{1,0:T(8,128)(2,1)S(1)}, bf16[32,256]{1,0:T(8,128)(2,1)}, u32[]{:S(2)}) copy-start(bf16[32,256]{1,0:T(8,128)(2,1)} %param.13) | copy-start | bytes 49156
Sparse Core Ops, SparseCore 0:
  9.4 221.9 all-gather.4
  233.5 233.5 all-gather.6
  477.0 273.0 all-reduce.2
  752.3 203.4 all-gather.8
where the time goes:
time: 1130 us; the launch traced here: 1120 us
  waiting for transfers between devices  926 us (82%)
  blocking collectives  134 us (12%)
  matrix products  22.9 us (2%)
  other arithmetic  17.5 us (2%)
  between operations  13.3 us (1%)
    psum x1, waiting for transfers between devices, shards(): in_proj, out_proj = lax.psum((in_part, out_part), 'tensor')  273 us
    all_gather x1, waiting for transfers between devices, shards(): lax.all_gather(up_weight, 'dp', axis=0, tiled=True)  226 us
    all_gather x1, waiting for transfers between devices, shards(): lax.all_gather(gate_weight, 'dp', axis=0, tiled=True)  222 us
    all_gather x1, waiting for transfers between devices, shards(): features = lax.all_gather(fragment, 'dp', axis=0, tiled=True)  204 us
    psum x1, blocking collectives, shards(): lax.psum(jnp.dot(query_rows, block.T, precision=lax.Precision.HIGHEST), '...  134 us
  transfers between devices with their start and end apart: 4, of which 4 were waited for; matrix products, arithmetic and copies ran while one was open for 1% of the time, Pallas kernels for 0%

commit v1 on v0

v1 whole, which is shorter than its diff:
```python
import functools

import jax
import jax.numpy as jnp
from jax import lax
from jax.experimental import pallas as pl
from jax.experimental.pallas import tpu as pltpu
from jax.sharding import Mesh, PartitionSpec as P

LEN = 160
DAMPING = 0.1
ZL, Y, X, ZH, C = 8, 4, 4, 2, 2
PLANE = ("y", "x", "c")
HIGHEST = lax.Precision.HIGHEST


def solve_body(features_ref, queries_ref, out_ref):
    blocks, count, width = features_ref.shape
    total = blocks * width
    features = jnp.concatenate([features_ref[d] for d in range(blocks)], axis=1)
    both = jnp.concatenate([features, queries_ref[...]], axis=0)
    system = lax.dot_general(
        features, both, (((1,), (1,)), ((), ())), preferred_element_type=jnp.float32
    )
    row = lax.broadcasted_iota(jnp.int32, system.shape, 0)
    lane = lax.broadcasted_iota(jnp.int32, system.shape, 1)
    system = jnp.where(
        lane < count,
        system / total + jnp.where(row == lane, DAMPING, 0.0),
        system / (total**0.5),
    )
    groups = [system[8 * g : 8 * g + 8] for g in range(count // 8)]
    inner = lax.broadcasted_iota(jnp.int32, groups[0].shape, 0)
    for k in range(count):
        g, r = k // 8, k % 8
        pivot_row = groups[g][r : r + 1]
        scaled = pivot_row / pivot_row[:, k : k + 1]
        updated = [block - block[:, k : k + 1] * scaled for block in groups]
        updated[g] = jnp.where(inner == r, scaled, updated[g])
        groups = updated
    width = system.shape[1]
    groups += [jnp.zeros_like(groups[0])] * (width // 8 - len(groups))
    solved = jnp.concatenate(groups, axis=0).T
    out_ref[...] = solved[count:, :count]


def solve(features, queries):
    count = features.shape[1]
    return pl.pallas_call(
        solve_body,
        out_shape=jax.ShapeDtypeStruct((queries.shape[0], count), jnp.float32),
        compiler_params=pltpu.CompilerParams(vmem_limit_bytes=32 * 2**20),
        name="solve",
    )(features, queries)


def share(x, axes, count):
    return lax.all_to_all(
        jnp.broadcast_to(x[None], (count,) + x.shape), axes, 0, 0, tiled=True
    )


def layer_kernel(place_ref, factor_ref, *refs):
    chains = 2 * ZL - 1
    blocks = refs[:chains]
    all_tokens, out_ref, weights, tokens, token_sems = refs[chains:]
    z = place_ref[0]
    hidden = blocks[0].shape[1] // 2
    half = all_tokens.shape[1]

    def token_copies(p):
        for c in range(2):
            yield pltpu.make_async_copy(
                all_tokens.at[2 * p + c], tokens.at[p, pl.ds(c * half, half)], token_sems.at[p, c]
            )

    for p in range(Y):
        for copy in token_copies(p):
            copy.start()

    gap = jnp.zeros((256 - hidden, 128), jnp.bfloat16)

    def place_block(at, owner):
        for k in range(Y):
            block = blocks[at][k]
            wide = jnp.concatenate([block[:hidden], gap, block[hidden:], gap], axis=0)
            weights[pl.ds(pl.multiple_of((owner * Y + k) * 128, 128), 128), :] = wide.T

    place_block(0, z)
    for s in range(1, ZL):
        @pl.when(z >= s)
        def _():
            place_block(s, z - s)

        @pl.when(z + s < ZL)
        def _():
            place_block(s + ZL - 1, z + s)

    def part(p, carry):
        for copy in token_copies(p):
            copy.wait()
        both = jnp.dot(tokens[p], weights[...], preferred_element_type=jnp.float32)
        gate, up = both[:, :256], both[:, 256:]
        value = (gate / (1.0 + jnp.exp(-gate)) * up).astype(jnp.bfloat16)
        proj = lax.dot_general(
            factor_ref[...], value, (((1,), (1,)), ((), ())),
            preferred_element_type=jnp.float32,
        )
        space = jnp.zeros((proj.shape[0], 256 - half), jnp.float32)
        proj = jnp.concatenate([proj[:, :half], space, proj[:, half:], space], axis=1)
        lanes = pl.ds(pl.multiple_of(p * 512, 512), 512)
        for d in range(out_ref.shape[0]):
            out_ref[d, :, lanes] = proj[2 * d : 2 * d + 2]
        return carry

    lax.fori_loop(0, Y, part, 0)


def layer(place, factor, blocks, tokens):
    _, half, depth = tokens.shape
    cols = blocks[0].shape[1]
    rank = factor.shape[0]
    vmem = pl.BlockSpec(memory_space=pltpu.VMEM)
    return pl.pallas_call(
        layer_kernel,
        out_shape=jax.ShapeDtypeStruct((rank // 2, 2, Y * 512), jnp.float32),
        in_specs=[pl.BlockSpec(memory_space=pltpu.SMEM)]
        + [vmem] * (1 + len(blocks))
        + [pl.BlockSpec(memory_space=pl.ANY)],
        out_specs=vmem,
        scratch_shapes=[
            pltpu.VMEM((depth, 512), jnp.bfloat16),
            pltpu.VMEM((Y, 2 * half, depth), jnp.bfloat16),
            pltpu.SemaphoreType.DMA((Y, 2)),
        ],
        compiler_params=pltpu.CompilerParams(vmem_limit_bytes=44 * 2**20),
        cost_estimate=pl.CostEstimate(
            flops=4 * Y * half * cols * depth,
            bytes_accessed=2 * depth * (cols + 2 * Y * half),
            transcendentals=0,
        ),
        name="layer",
    )(place, factor, *blocks, tokens)


def tie(value, *after):
    return lax.optimization_barrier((value,) + after)[0]


class Chain:
    def __init__(self, block):
        self.ups, self.downs = [block], [block]

    def step(self):
        s = len(self.ups)
        up, down = self.ups[-1], self.downs[-1]
        if s > 2:
            up, down = tie(up, self.downs[-2]), tie(down, self.ups[-2])
        self.ups.append(lax.ppermute(up, "zl", [(z, z + 1) for z in range(s - 1, ZL - 1)]))
        self.downs.append(lax.ppermute(down, "zl", [(z, z - 1) for z in range(1, ZL + 1 - s)]))

    def hold(self, value):
        self.ups[-1], value = lax.optimization_barrier((self.ups[-1], value))
        return value

    def blocks(self):
        return self.ups + self.downs[1:]


def weight_quarters(gate_weight, up_weight):
    depth, cols = gate_weight.shape
    return jnp.concatenate(
        [w.T.reshape(Y, cols // Y, depth) for w in (gate_weight, up_weight)], axis=1
    )


def out_partial(out_grad, out_factor):
    half = out_grad.shape[0] // 2
    grads = jnp.pad(out_grad.reshape(2, half, -1), ((0, 0), (0, 256 - half), (0, 0)))
    return lax.dot_general(
        out_factor, grads.reshape(512, -1), (((0,), (1,)), ((), ())),
        preferred_element_type=jnp.float32,
    )


def scatter_out_share_queries(out, queries):
    count = X * C
    rank, lanes = out.shape
    ours = queries.astype(jnp.float32).reshape(-1, lanes)
    sent = jnp.concatenate(
        [out.reshape(count, rank // count, lanes), jnp.broadcast_to(ours, (count,) + ours.shape)],
        axis=1,
    )
    got = lax.all_to_all(sent, ("x", "c"), 0, 0, tiled=True)
    full = got[:, rank // count :].reshape((count,) + queries.shape).astype(queries.dtype)
    return got[:, : rank // count].sum(0), full


def shards(tokens, gate_weight, up_weight, out_grad, in_factor, out_factor, queries):
    rows = tokens.shape[0]
    rank = in_factor.shape[1]
    half = rows // 2
    z, y, c = (lax.axis_index(name) for name in ("zl", "y", "c"))
    mine = lax.dynamic_slice_in_dim(tokens, c * half, half, 0)
    plane_tokens = lax.all_gather(mine, ("y", "c"))
    quarter = in_factor.shape[0] // Y
    factor = lax.dynamic_slice_in_dim(in_factor, y * quarter, quarter, 0).T
    factor = jnp.pad(factor, ((0, 0), (0, 256 - quarter)))

    quarters = weight_quarters(gate_weight, up_weight)
    chain = Chain(lax.all_to_all(quarters, "y", 0, 0, tiled=True))
    out = out_partial(out_grad, out_factor)
    for s in range(1, ZL):
        chain.step()
        if s == 1:
            out = tie(out, chain.ups[-1])
            out, plane_queries = scatter_out_share_queries(out, queries)
        if s == 3:
            out, plane_queries = chain.hold((out, plane_queries))
        if s == 6:
            plane_tokens = chain.hold(plane_tokens)
    out = lax.all_gather(tie(out, plane_tokens), "zh").sum(0)
    query_rows = lax.all_gather(tie(plane_queries, out), "zh")
    out = share(out, PLANE, Y * X * C)
    out = out.reshape(Y, rank, -1).transpose(1, 0, 2).reshape(rank, -1)

    place = jnp.stack([z]).astype(jnp.int32)
    in_part = layer(place, factor, chain.blocks(), plane_tokens)
    query_rows = tie(query_rows, in_part)
    query_rows = query_rows.reshape((ZH, X, C) + queries.shape).transpose(3, 1, 0, 2, 4)
    query_rows = query_rows.reshape(queries.shape[0], -1)
    in_proj = lax.all_to_all(in_part, PLANE, 0, 0, tiled=True).sum(0)

    seqs = Y * rows // LEN
    lane = jnp.arange(in_proj.shape[1])
    token = lane // 256 * half + lane % 256
    mask = (token // LEN)[None, :] == jnp.arange(seqs)[:, None]
    spread = jnp.where(mask[:, None, :], in_proj[None], 0.0).reshape(2 * seqs, -1)
    fragment = jnp.dot(spread, out.T, precision=HIGHEST) / jnp.sqrt(jnp.float32(LEN))
    fragment = fragment.reshape(seqs, 2 * rank)
    columns = share(fragment, ("zh", "zl"), ZH * ZL)
    columns = columns.reshape(ZH, ZL * seqs, 2 * rank).sum(0).astype(jnp.bfloat16)
    features = share(columns, PLANE, Y * X * C)
    return solve(features, query_rows)


def solution(mesh):
    fine = Mesh(mesh.devices.reshape(ZL, Y, X, ZH, C), ("zl", "y", "x", "zh", "c"))
    dp, tensor = ("zl", "y"), ("x", "zh", "c")
    in_specs = (
        P(dp, None),
        P(dp, tensor),
        P(dp, tensor),
        P(dp, tensor),
        P(tensor, None),
        P(tensor, None),
        P(dp, tensor),
    )
    return jax.shard_map(
        shards, mesh=fine, in_specs=in_specs, out_specs=P(dp, None), check_vma=False
    )
```

time: 1130 us -> 242 us (0.21)
  the two profiles are of different devices: /device:TPU:1 before, /device:TPU:66 now
where the time goes in v1:
time: 242 us; the launch traced here: 241 us
  blocking collectives  77.5 us (32%)
  starting transfers between devices  54.5 us (23%)
  waiting for transfers between devices  52.1 us (22%)
  Pallas kernels  23.5 us (10%)
  local copies, waits for them, and re-layouts  16.9 us (7%)
  between operations  13.8 us (6%)
    ppermute x7, waiting for transfers between devices, step(): lax.ppermute(down, 'zl', [(z, z - 1) for z in range(1, ZL + 1 - s)])  31.3 us
    all_to_all x1, blocking collectives, share(): lax.all_to_all(jnp.broadcast_to(x[None], (count,) + x.shape), axes, 0, 0,...  28 us
    all_gather x1, blocking collectives, shards(): query_rows = lax.all_gather(tie(plane_queries, out), 'zh')  23.2 us
    ppermute x7, starting transfers between devices, step(): lax.ppermute(up, 'zl', [(z, z + 1) for z in range(s - 1, ZL - 1)])  17.7 us
    pallas_call x1, Pallas kernels, layer(): pl.pallas_call(layer_kernel, out_shape=jax.ShapeDtypeStruct((rank // 2, 2...  14.2 us
    ppermute x7, starting transfers between devices, step(): lax.ppermute(down, 'zl', [(z, z - 1) for z in range(1, ZL + 1 - s)])  13.8 us
    all_gather x1, blocking collectives, shards(): out = lax.all_gather(tie(out, plane_tokens), 'zh').sum(0)  13.2 us
    all_to_all x1, blocking collectives, shards(): chain = Chain(lax.all_to_all(quarters, 'y', 0, 0, tiled=True))  13 us
  transfers between devices with their start and end apart: 19, of which 9 were waited for; matrix products, arithmetic and copies ran while one was open for 3% of the time, Pallas kernels for 6%

profile of v1, /device:TPU:66, one launch (start us, length us, event | category | flops | bytes accessed | tf_op | source)
XLA Modules:
  0.0 241.0 jit_solution(14914775848358391019)
XLA Ops:
  6.6 3.1 %constant_dynamic-slice_fusion = bf16[240,4096]{1,0:T(8,128)(2,1)} fusion(bf16[480,4096]{1,0:T(8,128)(2,1)} %param.7, s32[]{:T(128)S(6)} %select_n.51), kind=kLoop, calls=%fused_computation.27 | loop fusion | bytes 3932164 | tf_op jit(solution)/shard_map/dynamic_slice | solution.py:204
  9.7 0.0 all-gather.5.cloned.1.call-update
  9.7 0.2 copy.22
  9.9 0.2 copy.21
  10.1 13.0 %all_to_all.30.refs_0_ = bf16[4,448,128]{2,1,0:T(8,128)(2,1)S(1)} all-to-all(bf16[4,448,128]{2,1,0:T(8,128)(2,1)S(1)} %pad_maximum_fusion), channel_id=1, replica_groups=mesh['zl'=8,'y'=4,'x'=4,'zh'=2,'c'=2] {'y'}, dimensions={0} | all-to-all | bytes 917504 | tf_op jit(solution)/shard_map/all_to_all | solution.py:211
  23.2 3.8 %collective-permute-start = (bf16[4,448,128]{2,1,0:T(8,128)(2,1)S(1)}, bf16[4,448,128]{2,1,0:T(8,128)(2,1)S(1)}, u32[]{:S(2)}, u32[]{:S(2)}) collective-permute-start(bf16[4,448,128]{2,1,0:T(8,128)(2,1)S(1)} %all_to_all.30.refs_0_), channel_id=1, source_target_pairs={{0,64},{64,128},{128,192},{192,256},{256,320},{320,384},{384,448},... | collective-permute-start | bytes 1376264 | tf_op jit(solution)/shard_map/ppermute | solution.py:159
  27.0 2.0 collective-permute-start.2
  29.0 6.8 %collective-permute-done.refs_1_ = bf16[4,448,128]{2,1,0:T(8,128)(2,1)S(1)} collective-permute-done((bf16[4,448,128]{2,1,0:T(8,128)(2,1)S(1)}, bf16[4,448,128]{2,1,0:T(8,128)(2,1)S(1)}, u32[]{:S(2)}, u32[]{:S(2)}) %collective-permute-start) | collective-permute-done | bytes 458784 | tf_op jit(solution)/shard_map/ppermute | solution.py:159
  35.8 4.5 %collective-permute-start.1 = (bf16[4,448,128]{2,1,0:T(8,128)(2,1)S(1)}, bf16[4,448,128]{2,1,0:T(8,128)(2,1)S(1)}, u32[]{:S(2)}, u32[]{:S(2)}) collective-permute-start(bf16[4,448,128]{2,1,0:T(8,128)(2,1)S(1)} %collective-permute-done.refs_1_), channel_id=1, source_target_pairs={{64,128},{128,192},{192,256},{256,320},{320,384},{384,448},{65,129... | collective-permute-start | bytes 1376264 | tf_op jit(solution)/shard_map/ppermute | solution.py:159
  40.3 0.5 collective-permute-done.2.refs_8_
  40.8 1.9 collective-permute-start.4
  42.8 0.2 convolution_bitcast_fusion
  43.0 0.8 pad_maximum_fusion.1
  43.8 4.8 %all-to-all-start.1 = ((f32[8,24,512]{2,1,0:T(8,128)}), f32[8,24,512]{2,1,0:T(8,128)}, u32[]{:S(2)}, u32[]{:S(2)}) async-start(f32[8,24,512]{2,1,0:T(8,128)} %pad_maximum_fusion.1), calls=%async_computation.1 | async-start | bytes 786432 | tf_op jit(solution)/shard_map/all_to_all | solution.py:194
  48.6 0.0 collective-permute-done.1.refs_2_
  48.6 5.2 %collective-permute-start.3 = (bf16[4,448,128]{2,1,0:T(8,128)(2,1)S(1)}, bf16[4,448,128]{2,1,0:T(8,128)(2,1)S(1)}, u32[]{:S(2)}, u32[]{:S(2)}) collective-permute-start(bf16[4,448,128]{2,1,0:T(8,128)(2,1)S(1)} %collective-permute-done.1.refs_2_), channel_id=1, source_target_pairs={{128,192},{192,256},{256,320},{320,384},{384,448},{129,193},{193,2... | collective-permute-start | bytes 1376264 | tf_op jit(solution)/shard_map/ppermute | solution.py:159
  53.8 1.9 collective-permute-start.6
  55.7 0.5 all-to-all-done.1
  56.2 1.6 slice.13
  57.8 1.0 convert_element_type.16
  58.8 0.9 slice_reduce_fusion
  59.7 4.1 %collective-permute-done.3.refs_3_ = bf16[4,448,128]{2,1,0:T(8,128)(2,1)S(1)} collective-permute-done((bf16[4,448,128]{2,1,0:T(8,128)(2,1)S(1)}, bf16[4,448,128]{2,1,0:T(8,128)(2,1)S(1)}, u32[]{:S(2)}, u32[]{:S(2)}) %collective-permute-start.3) | collective-permute-done | bytes 458784 | tf_op jit(solution)/shard_map/ppermute | solution.py:159
  63.8 5.6 %collective-permute-done.6.refs_10_ = bf16[4,448,128]{2,1,0:T(8,128)(2,1)S(1)} collective-permute-done((bf16[4,448,128]{2,1,0:T(8,128)(2,1)S(1)}, bf16[4,448,128]{2,1,0:T(8,128)(2,1)S(1)}, u32[]{:S(2)}, u32[]{:S(2)}) %collective-permute-start.6) | collective-permute-done | bytes 458784 | tf_op jit(solution)/shard_map/ppermute | solution.py:160
  69.4 1.9 collective-permute-start.8
  71.4 0.7 collective-permute-start.5
  72.1 12.0 %collective-permute-done.8.refs_11_ = bf16[4,448,128]{2,1,0:T(8,128)(2,1)S(1)} collective-permute-done((bf16[4,448,128]{2,1,0:T(8,128)(2,1)S(1)}, bf16[4,448,128]{2,1,0:T(8,128)(2,1)S(1)}, u32[]{:S(2)}, u32[]{:S(2)}) %collective-permute-start.8) | collective-permute-done | bytes 458784 | tf_op jit(solution)/shard_map/ppermute | solution.py:160
  84.1 1.9 collective-permute-start.10
  86.0 0.8 copy-done.1
  86.7 0.7 collective-permute-start.7
  87.4 0.8 copy-done.3
  88.2 9.0 %collective-permute-done.10.refs_12_ = bf16[4,448,128]{2,1,0:T(8,128)(2,1)S(1)} collective-permute-done((bf16[4,448,128]{2,1,0:T(8,128)(2,1)S(1)}, bf16[4,448,128]{2,1,0:T(8,128)(2,1)S(1)}, u32[]{:S(2)}, u32[]{:S(2)}) %collective-permute-start.10) | collective-permute-done | bytes 458784 | tf_op jit(solution)/shard_map/ppermute | solution.py:160
  97.2 2.7 %collective-permute-start.12 = (bf16[4,448,128]{2,1,0:T(8,128)(2,1)S(1)}, bf16[4,448,128]{2,1,0:T(8,128)(2,1)}, u32[]{:S(2)}, u32[]{:S(2)}) collective-permute-start(bf16[4,448,128]{2,1,0:T(8,128)(2,1)S(1)} %collective-permute-done.10.refs_12_), channel_id=1, source_target_pairs={{64,0},{128,64},{65,1},{129,65},{66,2},{130,66},{67,3},{131,67},{6... | collective-permute-start | bytes 1376264 | tf_op jit(solution)/shard_map/ppermute | solution.py:160
  99.9 0.8 copy-done.5
  100.7 0.0 collective-permute-done.7.refs_5_
  100.7 1.4 collective-permute-start.9
  102.1 0.8 copy-done.7
  102.9 4.2 %collective-permute-done.12.refs_13_ = bf16[4,448,128]{2,1,0:T(8,128)(2,1)} collective-permute-done((bf16[4,448,128]{2,1,0:T(8,128)(2,1)S(1)}, bf16[4,448,128]{2,1,0:T(8,128)(2,1)}, u32[]{:S(2)}, u32[]{:S(2)}) %collective-permute-start.12) | collective-permute-done | bytes 458784 | tf_op jit(solution)/shard_map/ppermute | solution.py:160
  107.1 1.4 collective-permute-start.13
  108.5 1.4 collective-permute-start.11
  110.0 0.1 dynamic-slice_bitcast_fusion
  110.1 13.2 %all-gather.1 = f32[16,512]{1,0:T(8,128)S(1)} all-gather(f32[8,512]{1,0:T(8,128)S(1)} %slice_reduce_fusion), channel_id=3, replica_groups=mesh['zl'=8,'y'=4,'x'=4,'zh'=2,'c'=2] {'zh'}, dimensions={0}, use_global_device_ids=true | all-gather | bytes 49152 | tf_op jit(solution)/shard_map/all_gather | solution.py:222
  123.3 0.9 broadcast_in_dim.50
  124.2 5.6 %all-to-all-start.3 = ((f32[32,8,512]{2,1,0:T(8,128)}), f32[32,8,512]{2,1,0:T(8,128)}, u32[]{:S(2)}, u32[]{:S(2)}) async-start(f32[32,8,512]{2,1,0:T(8,128)} %broadcast_in_dim.50), calls=%async_computation.3 | async-start | bytes 1048576 | tf_op jit(solution)/shard_map/all_to_all | solution.py:58
  129.8 0.0 collective-permute-done.13.refs_14_
  129.8 1.0 copy-done.2
  130.8 1.0 copy-done.4
  131.8 1.0 copy-done.6
  132.9 1.0 copy-done.8
  133.9 14.2 %layer.1 = f32[32,2,2048]{2,1,0:T(2,128)} custom-call(s32[1]{0:T(128)} %bitcast.place_ref, bf16[64,256]{1,0:T(8,128)(2,1)S(1)} %pad.8.factor_ref, bf16[4,448,128]{2,1,0:T(8,128)(2,1)S(1)} %all_to_all.30.refs_0_, bf16[4,448,128]{2,1,0:T(8,128)(2,1)S(1)} %collective-permute-done.refs_1_, bf16[4,448,128]{2,1,0:T(8,128)(2,1)S(1)} %collective-permute-done.1.refs_2_, ...), custom_call_target="tpu_custom_call" | custom-call | flops 7046430720 | bytes 19398656 | tf_op jit(solution)/shard_map/layer/pallas_call | solution.py:124
  148.1 7.4 %all-to-all-start.2 = ((f32[32,2,2048]{2,1,0:T(2,128)}), f32[32,2,2048]{2,1,0:T(2,128)S(1)}, u32[]{:S(2)}, u32[]{:S(2)}) async-start(f32[32,2,2048]{2,1,0:T(2,128)} %layer.1), calls=%async_computation.2 | async-start | bytes 1048576 | tf_op jit(solution)/shard_map/all_to_all | solution.py:232
  155.5 1.1 copy.25
  156.6 9.4 %all-to-all-done.2 = f32[32,2,2048]{2,1,0:T(2,128)S(1)} async-done(((f32[32,2,2048]{2,1,0:T(2,128)}), f32[32,2,2048]{2,1,0:T(2,128)S(1)}, u32[]{:S(2)}, u32[]{:S(2)}) %all-to-all-start.2) | async-done | bytes 524320 | tf_op jit(solution)/shard_map/all_to_all | solution.py:232
  166.0 0.2 reduce_sum.37
  166.1 0.1 broadcast_select_fusion
  166.2 0.1 select_n.53
  166.4 0.5 convolution_multiply_fusion
  166.9 0.1 broadcast_in_dim.51
  167.0 28.0 %all_to_all.31 = f32[16,12,128]{2,1,0:T(8,128)S(1)} all-to-all(f32[16,12,128]{2,1,0:T(8,128)S(1)} %broadcast_in_dim.52), channel_id=1, replica_groups=mesh['zl'=8,'y'=4,'x'=4,'zh'=2,'c'=2] {'zh','zl'}, dimensions={0} | all-to-all | bytes 196608 | tf_op jit(solution)/shard_map/all_to_all | solution.py:58
  195.0 1.0 broadcast_in_dim.53
  196.0 5.2 %all-to-all-start.5 = ((bf16[32,96,128]{2,1,0:T(8,128)(2,1)}), bf16[32,96,128]{2,1,0:T(8,128)(2,1)S(1)}, u32[]{:S(2)}, u32[]{:S(2)}) async-start(bf16[32,96,128]{2,1,0:T(8,128)(2,1)} %broadcast_in_dim.53), calls=%async_computation.5 | async-start | bytes 1572864 | tf_op jit(solution)/shard_map/all_to_all | solution.py:58
  201.2 23.2 %all-gather.2 = bf16[16,32,256]{2,1,0:T(8,128)(2,1)S(1)} all-gather(bf16[8,32,256]{2,1,0:T(8,128)(2,1)S(1)} %convert_element_type.16), channel_id=4, replica_groups=mesh['zl'=8,'y'=4,'x'=4,'zh'=2,'c'=2] {'zh'}, dimensions={0}, use_global_device_ids=true | all-gather | bytes 393216 | tf_op jit(solution)/shard_map/all_gather | solution.py:223
  224.4 0.3 copy.24
  224.7 0.2 reshape.115.queries_ref
  224.9 9.3 %solve.1 = f32[32,96]{1,0:T(8,128)} custom-call(bf16[32,96,128]{2,1,0:T(8,128)(2,1)S(1)} %all-to-all-done.5.features_ref, bf16[32,4096]{1,0:T(8,128)(2,1)S(1)} %reshape.115.queries_ref), custom_call_target="tpu_custom_call" | custom-call | tf_op jit(solution)/shard_map/solve/pallas_call | solution.py:49
  (39 shorter events, 0.2 us)
Async XLA Ops:
  6.5 103.4 %copy-start = (bf16[896,64]{0,1:T(8,128)(2,1)S(1)}, bf16[896,64]{0,1:T(8,128)(2,1)}, u32[]{:S(2)}) copy-start(bf16[896,64]{0,1:T(8,128)(2,1)} %param.11) | copy-start | bytes 344068
  6.5 3.2 %copy-start.10 = (bf16[128,896]{1,0:T(8,128)(2,1)S(1)}, bf16[128,896]{1,0:T(8,128)(2,1)}, u32[]{:S(2)}) copy-start(bf16[128,896]{1,0:T(8,128)(2,1)} %param.9) | copy-start | bytes 688132
  6.5 3.4 %copy-start.11 = (bf16[128,896]{1,0:T(8,128)(2,1)S(1)}, bf16[128,896]{1,0:T(8,128)(2,1)}, u32[]{:S(2)}) copy-start(bf16[128,896]{1,0:T(8,128)(2,1)} %param.8) | copy-start | bytes 688132
  6.5 102.0 %all-gather.5.cloned.1.call-start = ((), (), s32[]{:S(2)}) async-start(), calls=%async_computation.6 | async-start | bytes 17694720 | tf_op jit(solution)/shard_map/all_gather | solution.py:205
  6.6 36.1 %copy-start.13 = (bf16[32,256]{1,0:T(8,128)(2,1)S(1)}, bf16[32,256]{1,0:T(8,128)(2,1)}, u32[]{:S(2)}) copy-start(bf16[32,256]{1,0:T(8,128)(2,1)} %param.13) | copy-start | bytes 49156
  6.6 36.2 %copy-start.9 = (bf16[480,256]{1,0:T(8,128)(2,1)S(1)}, bf16[480,256]{1,0:T(8,128)(2,1)}, u32[]{:S(2)}) copy-start(bf16[480,256]{1,0:T(8,128)(2,1)} %param.10) | copy-start | bytes 737284
  6.6 36.2 %copy-start.12 = (bf16[256,64]{0,1:T(8,128)(2,1)S(1)}, bf16[256,64]{0,1:T(8,128)(2,1)}, u32[]{:S(2)}) copy-start(bf16[256,64]{0,1:T(8,128)(2,1)} %param.12) | copy-start | bytes 98308
  23.2 12.7 %collective-permute-start = (bf16[4,448,128]{2,1,0:T(8,128)(2,1)S(1)}, bf16[4,448,128]{2,1,0:T(8,128)(2,1)S(1)}, u32[]{:S(2)}, u32[]{:S(2)}) collective-permute-start(bf16[4,448,128]{2,1,0:T(8,128)(2,1)S(1)} %all_to_all.30.refs_0_), channel_id=1, source_target_pairs={{0,64},{64,128},{128,192},{192,256},{256,320},{320,384},{384,448},... | collective-permute-start | bytes 1376264 | tf_op jit(solution)/shard_map/ppermute | solution.py:159
  27.0 13.8 %collective-permute-start.2 = (bf16[4,448,128]{2,1,0:T(8,128)(2,1)S(1)}, bf16[4,448,128]{2,1,0:T(8,128)(2,1)S(1)}, u32[]{:S(2)}, u32[]{:S(2)}) collective-permute-start(bf16[4,448,128]{2,1,0:T(8,128)(2,1)S(1)} %all_to_all.30.refs_0_), channel_id=1, source_target_pairs={{64,0},{128,64},{192,128},{256,192},{320,256},{384,320},{448,384},... | collective-permute-start | bytes 1376264 | tf_op jit(solution)/shard_map/ppermute | solution.py:160
  35.8 12.8 %collective-permute-start.1 = (bf16[4,448,128]{2,1,0:T(8,128)(2,1)S(1)}, bf16[4,448,128]{2,1,0:T(8,128)(2,1)S(1)}, u32[]{:S(2)}, u32[]{:S(2)}) collective-permute-start(bf16[4,448,128]{2,1,0:T(8,128)(2,1)S(1)} %collective-permute-done.refs_1_), channel_id=1, source_target_pairs={{64,128},{128,192},{192,256},{256,320},{320,384},{384,448},{65,129... | collective-permute-start | bytes 1376264 | tf_op jit(solution)/shard_map/ppermute | solution.py:159
  40.8 13.0 %collective-permute-start.4 = (bf16[4,448,128]{2,1,0:T(8,128)(2,1)S(1)}, bf16[4,448,128]{2,1,0:T(8,128)(2,1)S(1)}, u32[]{:S(2)}, u32[]{:S(2)}) collective-permute-start(bf16[4,448,128]{2,1,0:T(8,128)(2,1)S(1)} %collective-permute-done.2.refs_8_), channel_id=1, source_target_pairs={{64,0},{128,64},{192,128},{256,192},{320,256},{384,320},{65,1},{12... | collective-permute-start | bytes 1376264 | tf_op jit(solution)/shard_map/ppermute | solution.py:160
  43.8 12.4 %all-to-all-start.1 = ((f32[8,24,512]{2,1,0:T(8,128)}), f32[8,24,512]{2,1,0:T(8,128)}, u32[]{:S(2)}, u32[]{:S(2)}) async-start(f32[8,24,512]{2,1,0:T(8,128)} %pad_maximum_fusion.1), calls=%async_computation.1 | async-start | bytes 786432 | tf_op jit(solution)/shard_map/all_to_all | solution.py:194
  48.6 15.2 %collective-permute-start.3 = (bf16[4,448,128]{2,1,0:T(8,128)(2,1)S(1)}, bf16[4,448,128]{2,1,0:T(8,128)(2,1)S(1)}, u32[]{:S(2)}, u32[]{:S(2)}) collective-permute-start(bf16[4,448,128]{2,1,0:T(8,128)(2,1)S(1)} %collective-permute-done.1.refs_2_), channel_id=1, source_target_pairs={{128,192},{192,256},{256,320},{320,384},{384,448},{129,193},{193,2... | collective-permute-start | bytes 1376264 | tf_op jit(solution)/shard_map/ppermute | solution.py:159
  53.8 15.7 %collective-permute-start.6 = (bf16[4,448,128]{2,1,0:T(8,128)(2,1)S(1)}, bf16[4,448,128]{2,1,0:T(8,128)(2,1)S(1)}, u32[]{:S(2)}, u32[]{:S(2)}) collective-permute-start(bf16[4,448,128]{2,1,0:T(8,128)(2,1)S(1)} %collective-permute-done.4.refs_9_), channel_id=1, source_target_pairs={{64,0},{128,64},{192,128},{256,192},{320,256},{65,1},{129,65},{193... | collective-permute-start | bytes 1376264 | tf_op jit(solution)/shard_map/ppermute | solution.py:160
  69.4 14.6 %collective-permute-start.8 = (bf16[4,448,128]{2,1,0:T(8,128)(2,1)S(1)}, bf16[4,448,128]{2,1,0:T(8,128)(2,1)S(1)}, u32[]{:S(2)}, u32[]{:S(2)}) collective-permute-start(bf16[4,448,128]{2,1,0:T(8,128)(2,1)S(1)} %collective-permute-done.6.refs_10_), channel_id=1, source_target_pairs={{64,0},{128,64},{192,128},{256,192},{65,1},{129,65},{193,129},{257... | collective-permute-start | bytes 1376264 | tf_op jit(solution)/shard_map/ppermute | solution.py:160
  71.4 15.4 %collective-permute-start.5 = (bf16[4,448,128]{2,1,0:T(8,128)(2,1)S(1)}, bf16[4,448,128]{2,1,0:T(8,128)(2,1)S(1)}, u32[]{:S(2)}, u32[]{:S(2)}) collective-permute-start(bf16[4,448,128]{2,1,0:T(8,128)(2,1)S(1)} %collective-permute-done.3.refs_3_), channel_id=1, source_target_pairs={{192,256},{256,320},{320,384},{384,448},{193,257},{257,321},{321,3... | collective-permute-start | bytes 1376264 | tf_op jit(solution)/shard_map/ppermute | solution.py:159
  84.1 13.2 %collective-permute-start.10 = (bf16[4,448,128]{2,1,0:T(8,128)(2,1)S(1)}, bf16[4,448,128]{2,1,0:T(8,128)(2,1)S(1)}, u32[]{:S(2)}, u32[]{:S(2)}) collective-permute-start(bf16[4,448,128]{2,1,0:T(8,128)(2,1)S(1)} %collective-permute-done.8.refs_11_), channel_id=1, source_target_pairs={{64,0},{128,64},{192,128},{65,1},{129,65},{193,129},{66,2},{130,66... | collective-permute-start | bytes 1376264 | tf_op jit(solution)/shard_map/ppermute | solution.py:160
  86.0 0.8 copy-start.1
  86.7 14.0 %collective-permute-start.7 = (bf16[4,448,128]{2,1,0:T(8,128)(2,1)S(1)}, bf16[4,448,128]{2,1,0:T(8,128)(2,1)S(1)}, u32[]{:S(2)}, u32[]{:S(2)}) collective-permute-start(bf16[4,448,128]{2,1,0:T(8,128)(2,1)S(1)} %collective-permute-done.5.refs_4_), channel_id=1, source_target_pairs={{256,320},{320,384},{384,448},{257,321},{321,385},{385,449},{258,3... | collective-permute-start | bytes 1376264 | tf_op jit(solution)/shard_map/ppermute | solution.py:159
  87.4 0.8 copy-start.3
  97.2 9.8 %collective-permute-start.12 = (bf16[4,448,128]{2,1,0:T(8,128)(2,1)S(1)}, bf16[4,448,128]{2,1,0:T(8,128)(2,1)}, u32[]{:S(2)}, u32[]{:S(2)}) collective-permute-start(bf16[4,448,128]{2,1,0:T(8,128)(2,1)S(1)} %collective-permute-done.10.refs_12_), channel_id=1, source_target_pairs={{64,0},{128,64},{65,1},{129,65},{66,2},{130,66},{67,3},{131,67},{6... | collective-permute-start | bytes 1376264 | tf_op jit(solution)/shard_map/ppermute | solution.py:160
  99.9 0.8 copy-start.5
  100.7 7.8 %collective-permute-start.9 = (bf16[4,448,128]{2,1,0:T(8,128)(2,1)S(1)}, bf16[4,448,128]{2,1,0:T(8,128)(2,1)}, u32[]{:S(2)}, u32[]{:S(2)}) collective-permute-start(bf16[4,448,128]{2,1,0:T(8,128)(2,1)S(1)} %collective-permute-done.7.refs_5_), channel_id=1, source_target_pairs={{320,384},{384,448},{321,385},{385,449},{322,386},{386,450},{323,3... | collective-permute-start | bytes 1376264 | tf_op jit(solution)/shard_map/ppermute | solution.py:159
  102.1 0.8 copy-start.7
  107.1 22.7 %collective-permute-start.13 = (bf16[4,448,128]{2,1,0:T(8,128)(2,1)}, bf16[4,448,128]{2,1,0:T(8,128)(2,1)}, u32[]{:S(2)}, u32[]{:S(2)}) collective-permute-start(bf16[4,448,128]{2,1,0:T(8,128)(2,1)} %collective-permute-done.12.refs_13_), channel_id=1, source_target_pairs={{64,0},{65,1},{66,2},{67,3},{68,4},{69,5},{70,6},{71,7},{72,8},{73... | collective-permute-start | bytes 1376264 | tf_op jit(solution)/shard_map/ppermute | solution.py:160
  108.5 21.3 %collective-permute-start.11 = (bf16[4,448,128]{2,1,0:T(8,128)(2,1)}, bf16[4,448,128]{2,1,0:T(8,128)(2,1)}, u32[]{:S(2)}, u32[]{:S(2)}) collective-permute-start(bf16[4,448,128]{2,1,0:T(8,128)(2,1)} %collective-permute-done.9.refs_6_), channel_id=1, source_target_pairs={{384,448},{385,449},{386,450},{387,451},{388,452},{389,453},{390,4... | collective-permute-start | bytes 1376264 | tf_op jit(solution)/shard_map/ppermute | solution.py:159
  124.2 23.9 %all-to-all-start.3 = ((f32[32,8,512]{2,1,0:T(8,128)}), f32[32,8,512]{2,1,0:T(8,128)}, u32[]{:S(2)}, u32[]{:S(2)}) async-start(f32[32,8,512]{2,1,0:T(8,128)} %broadcast_in_dim.50), calls=%async_computation.3 | async-start | bytes 1048576 | tf_op jit(solution)/shard_map/all_to_all | solution.py:58
  129.8 1.0 copy-start.2
  130.8 1.0 copy-start.4
  131.8 1.0 copy-start.6
  132.9 1.0 copy-start.8
  148.1 17.9 %all-to-all-start.2 = ((f32[32,2,2048]{2,1,0:T(2,128)}), f32[32,2,2048]{2,1,0:T(2,128)S(1)}, u32[]{:S(2)}, u32[]{:S(2)}) async-start(f32[32,2,2048]{2,1,0:T(2,128)} %layer.1), calls=%async_computation.2 | async-start | bytes 1048576 | tf_op jit(solution)/shard_map/all_to_all | solution.py:232
  196.0 28.9 %all-to-all-start.5 = ((bf16[32,96,128]{2,1,0:T(8,128)(2,1)}), bf16[32,96,128]{2,1,0:T(8,128)(2,1)S(1)}, u32[]{:S(2)}, u32[]{:S(2)}) async-start(bf16[32,96,128]{2,1,0:T(8,128)(2,1)} %broadcast_in_dim.53), calls=%async_computation.5 | async-start | bytes 1572864 | tf_op jit(solution)/shard_map/all_to_all | solution.py:58
Sparse Core Ops, SparseCore 0:
  9.8 91.9 all-gather.4

commit v2 on v1

--- a/solution.py
+++ b/solution.py
@@ -29,15 +29,28 @@
         system / total + jnp.where(row == lane, DAMPING, 0.0),
         system / (total**0.5),
     )
+    on_diagonal = jnp.where(row == lane, system, 0.0)
+    row_scale = lax.rsqrt(jnp.sum(on_diagonal, axis=1, keepdims=True))
+    lane_scale = jnp.sum(jnp.where(row == lane, row_scale, 0.0), axis=0, keepdims=True)
+    system = system * row_scale * jnp.where(lane < count, lane_scale, 1.0)
     groups = [system[8 * g : 8 * g + 8] for g in range(count // 8)]
     inner = lax.broadcasted_iota(jnp.int32, groups[0].shape, 0)
-    for k in range(count):
+    for k in range(0, count, 2):
         g, r = k // 8, k % 8
-        pivot_row = groups[g][r : r + 1]
-        scaled = pivot_row / pivot_row[:, k : k + 1]
-        updated = [block - block[:, k : k + 1] * scaled for block in groups]
-        updated[g] = jnp.where(inner == r, scaled, updated[g])
+        p, q = groups[g][r : r + 1], groups[g][r + 1 : r + 2]
+        a, b, c, d = p[:, k : k + 1], p[:, k + 1 : k + 2], q[:, k : k + 1], q[:, k + 1 : k + 2]
+        inverse = 1.0 / (a * d - b * c)
+        first = (d * inverse) * p - (b * inverse) * q
+        second = (a * inverse) * q - (c * inverse) * p
+        updated = [
+            block - block[:, k : k + 1] * first - block[:, k + 1 : k + 2] * second
+            for block in groups
+        ]
+        updated[g] = jnp.where(
+            inner == r, first, jnp.where(inner == r + 1, second, updated[g])
+        )
         groups = updated
+    groups = [block * row_scale[8 * g : 8 * g + 8] for g, block in enumerate(groups)]
     width = system.shape[1]
     groups += [jnp.zeros_like(groups[0])] * (width // 8 - len(groups))
     solved = jnp.concatenate(groups, axis=0).T
@@ -133,7 +146,7 @@
             pltpu.VMEM((Y, 2 * half, depth), jnp.bfloat16),
             pltpu.SemaphoreType.DMA((Y, 2)),
         ],
-        compiler_params=pltpu.CompilerParams(vmem_limit_bytes=44 * 2**20),
+        compiler_params=pltpu.CompilerParams(vmem_limit_bytes=38 * 2**20),
         cost_estimate=pl.CostEstimate(
             flops=4 * Y * half * cols * depth,
             bytes_accessed=2 * depth * (cols + 2 * Y * half),
@@ -159,9 +172,9 @@
         self.ups.append(lax.ppermute(up, "zl", [(z, z + 1) for z in range(s - 1, ZL - 1)]))
         self.downs.append(lax.ppermute(down, "zl", [(z, z - 1) for z in range(1, ZL + 1 - s)]))
 
-    def hold(self, value):
-        self.ups[-1], value = lax.optimization_barrier((self.ups[-1], value))
-        return value
+    def after(self, *values):
+        self.ups[-1] = tie(self.ups[-1], *values)
+        self.downs[-1] = tie(self.downs[-1], *values)
 
     def blocks(self):
         return self.ups + self.downs[1:]
@@ -183,17 +196,37 @@
     )
 
 
-def scatter_out_share_queries(out, queries):
-    count = X * C
-    rank, lanes = out.shape
-    ours = queries.astype(jnp.float32).reshape(-1, lanes)
+def exchange_z(out, queries):
+    rows, cols = queries.shape
+    high = lax.reduce_precision(out, 8, 7)
     sent = jnp.concatenate(
-        [out.reshape(count, rank // count, lanes), jnp.broadcast_to(ours, (count,) + ours.shape)],
-        axis=1,
-    )
-    got = lax.all_to_all(sent, ("x", "c"), 0, 0, tiled=True)
-    full = got[:, rank // count :].reshape((count,) + queries.shape).astype(queries.dtype)
-    return got[:, : rank // count].sum(0), full
+        [v.astype(jnp.bfloat16) for v in (high, out - high)] + [queries.reshape(-1, out.shape[1])]
+    )
+    got = lax.all_gather(sent, "zh")
+    count = out.shape[0]
+    parts = got[:, : 2 * count].astype(jnp.float32)
+    out = (parts[:, :count] + parts[:, count:]).sum(0)
+    return out, got[:, 2 * count :].reshape(ZH, rows, cols)
+
+
+def share_plane(out, queries):
+    high = lax.reduce_precision(out, 8, 7)
+    sent = jnp.concatenate(
+        [v.astype(jnp.bfloat16) for v in (high, out - high)]
+        + [queries.reshape(-1, out.shape[1])]
+    )
+    return share(sent, PLANE, Y * X * C)
+
+
+def unpack_plane(got, count, rows, cols):
+    lanes = got.shape[2]
+    parts = got[:, : 2 * count].astype(jnp.float32)
+    out = (parts[:, :count] + parts[:, count:]).reshape(Y, X * C * count, lanes)
+    here = got.reshape((Y, X * C) + got.shape[1:])
+    here = lax.dynamic_index_in_dim(here, lax.axis_index("y"), 0, keepdims=False)
+    queries = here[:, 2 * count :].reshape(X, C, ZH, rows, cols)
+    queries = queries.transpose(3, 0, 2, 1, 4).reshape(rows, -1)
+    return out.transpose(1, 0, 2).reshape(X * C * count, Y * lanes), queries
 
 
 def shards(tokens, gate_weight, up_weight, out_grad, in_factor, out_factor, queries):
@@ -212,24 +245,24 @@
     out = out_partial(out_grad, out_factor)
     for s in range(1, ZL):
         chain.step()
-        if s == 1:
+        if s == 2:
+            out = tie(out, chain.ups[-1]).reshape(X * C, rank // (X * C), -1)
+            out = lax.all_to_all(out, ("x", "c"), 0, 0, tiled=True).sum(0)
+        if s == 4:
+            chain.after(out)
             out = tie(out, chain.ups[-1])
-            out, plane_queries = scatter_out_share_queries(out, queries)
-        if s == 3:
-            out, plane_queries = chain.hold((out, plane_queries))
+            out, query_rows = exchange_z(out, queries)
         if s == 6:
-            plane_tokens = chain.hold(plane_tokens)
-    out = lax.all_gather(tie(out, plane_tokens), "zh").sum(0)
-    query_rows = lax.all_gather(tie(plane_queries, out), "zh")
-    out = share(out, PLANE, Y * X * C)
-    out = out.reshape(Y, rank, -1).transpose(1, 0, 2).reshape(rank, -1)
+            chain.after(out, query_rows)
+            out = tie(out, chain.ups[-1])
+            shared = share_plane(out, query_rows)
 
     place = jnp.stack([z]).astype(jnp.int32)
     in_part = layer(place, factor, chain.blocks(), plane_tokens)
-    query_rows = tie(query_rows, in_part)
-    query_rows = query_rows.reshape((ZH, X, C) + queries.shape).transpose(3, 1, 0, 2, 4)
-    query_rows = query_rows.reshape(queries.shape[0], -1)
-    in_proj = lax.all_to_all(in_part, PLANE, 0, 0, tiled=True).sum(0)
+    shared, in_part = lax.optimization_barrier((shared, in_part))
+    out, query_rows = unpack_plane(shared, rank // (X * C), *queries.shape)
+    in_proj = lax.all_to_all(in_part, PLANE, 0, 0, tiled=True)
+    in_proj = in_proj.sum(0)
 
     seqs = Y * rows // LEN
     lane = jnp.arange(in_proj.shape[1])

time: 242 us -> 239 us (0.988)
  the two profiles are of different devices: /device:TPU:66 before, /device:TPU:1 now
where the time goes in v2:
time: 239 us; the launch traced here: 238 us
  waiting for transfers between devices  72.6 us (30%)
  blocking collectives  67.5 us (28%)
  starting transfers between devices  41.6 us (17%)
  Pallas kernels  30.4 us (13%)
  between operations  13.8 us (6%)
  local copies, waits for them, and re-layouts  9.57 us (4%)
    ppermute x7, waiting for transfers between devices, step(): lax.ppermute(down, 'zl', [(z, z - 1) for z in range(1, ZL + 1 - s)])  43.3 us
    all_to_all x1, blocking collectives, share(): lax.all_to_all(jnp.broadcast_to(x[None], (count,) + x.shape), axes, 0, 0,...  30.3 us
    pallas_call x1, Pallas kernels, solve(): pl.pallas_call(solve_body, out_shape=jax.ShapeDtypeStruct((queries.shape[...  15.7 us
    pallas_call x1, Pallas kernels, layer(): pl.pallas_call(layer_kernel, out_shape=jax.ShapeDtypeStruct((rank // 2, 2...  14.7 us
    all_to_all x1, blocking collectives, shards(): out = lax.all_to_all(out, ('x', 'c'), 0, 0, tiled=True).sum(0)  13.5 us
    all_to_all x2, starting transfers between devices, share(): lax.all_to_all(jnp.broadcast_to(x[None], (count,) + x.shape), axes, 0, 0,...  13.2 us
    all_to_all x2, waiting for transfers between devices, share(): lax.all_to_all(jnp.broadcast_to(x[None], (count,) + x.shape), axes, 0, 0,...  12.7 us
    all_gather x1, blocking collectives, exchange_z(): got = lax.all_gather(sent, 'zh')  12.3 us
  transfers between devices with their start and end apart: 18, of which 8 were waited for; matrix products, arithmetic and copies ran while one was open for 3% of the time, Pallas kernels for 6%

profile of v2, /device:TPU:1, one launch (start us, length us, event | category | flops | bytes accessed | tf_op | source)
XLA Modules:
  0.0 237.8 jit_solution(13933352065760276292)
XLA Ops:
  6.5 0.0 copy-start
  6.5 3.0 %constant_dynamic-slice_fusion = bf16[240,4096]{1,0:T(8,128)(2,1)} fusion(bf16[480,4096]{1,0:T(8,128)(2,1)} %param.7, s32[]{:T(128)S(6)} %select_n.55), kind=kLoop, calls=%fused_computation.37 | loop fusion | bytes 3932164 | tf_op jit(solution)/shard_map/dynamic_slice | solution.py:237
  9.6 0.0 all-gather.4.cloned.1.call-update
  9.6 0.0 copy-start.3
  9.6 0.9 copy-done.1
  10.5 0.2 copy.13
  10.7 0.2 copy.14
  10.9 11.4 %all_to_all.30.refs_0_ = bf16[4,448,128]{2,1,0:T(8,128)(2,1)S(1)} all-to-all(bf16[4,448,128]{2,1,0:T(8,128)(2,1)S(1)} %pad_maximum_fusion), channel_id=1, replica_groups=mesh['zl'=8,'y'=4,'x'=4,'zh'=2,'c'=2] {'y'}, dimensions={0} | all-to-all | bytes 917504 | tf_op jit(solution)/shard_map/all_to_all | solution.py:244
  22.3 4.5 %collective-permute-start = (bf16[4,448,128]{2,1,0:T(8,128)(2,1)S(1)}, bf16[4,448,128]{2,1,0:T(8,128)(2,1)S(1)}, u32[]{:S(2)}, u32[]{:S(2)}) collective-permute-start(bf16[4,448,128]{2,1,0:T(8,128)(2,1)S(1)} %all_to_all.30.refs_0_), channel_id=1, source_target_pairs={{0,64},{64,128},{128,192},{192,256},{256,320},{320,384},{384,448},... | collective-permute-start | bytes 1376264 | tf_op jit(solution)/shard_map/ppermute | solution.py:172
  26.9 1.3 collective-permute-start.2
  28.2 6.3 %collective-permute-done.refs_1_ = bf16[4,448,128]{2,1,0:T(8,128)(2,1)S(1)} collective-permute-done((bf16[4,448,128]{2,1,0:T(8,128)(2,1)S(1)}, bf16[4,448,128]{2,1,0:T(8,128)(2,1)S(1)}, u32[]{:S(2)}, u32[]{:S(2)}) %collective-permute-start) | collective-permute-done | bytes 458784 | tf_op jit(solution)/shard_map/ppermute | solution.py:172
  34.5 0.7 collective-permute-start.1
  35.2 3.6 %collective-permute-done.2.refs_8_ = bf16[4,448,128]{2,1,0:T(8,128)(2,1)S(1)} collective-permute-done((bf16[4,448,128]{2,1,0:T(8,128)(2,1)S(1)}, bf16[4,448,128]{2,1,0:T(8,128)(2,1)S(1)}, u32[]{:S(2)}, u32[]{:S(2)}) %collective-permute-start.2) | collective-permute-done | bytes 458784 | tf_op jit(solution)/shard_map/ppermute | solution.py:173
  38.8 1.3 collective-permute-start.4
  40.1 0.0 collective-permute-done.1.refs_2_
  40.1 0.7 collective-permute-start.3
  40.8 9.3 %collective-permute-done.4.refs_9_ = bf16[4,448,128]{2,1,0:T(8,128)(2,1)S(1)} collective-permute-done((bf16[4,448,128]{2,1,0:T(8,128)(2,1)S(1)}, bf16[4,448,128]{2,1,0:T(8,128)(2,1)S(1)}, u32[]{:S(2)}, u32[]{:S(2)}) %collective-permute-start.4) | collective-permute-done | bytes 458784 | tf_op jit(solution)/shard_map/ppermute | solution.py:173
  50.1 1.3 collective-permute-start.6
  51.3 0.0 collective-permute-done.3.refs_3_
  51.4 1.5 collective-permute-start.5
  52.8 1.0 pad.8
  53.8 8.8 %collective-permute-done.6.refs_10_ = bf16[4,448,128]{2,1,0:T(8,128)(2,1)S(1)} collective-permute-done((bf16[4,448,128]{2,1,0:T(8,128)(2,1)S(1)}, bf16[4,448,128]{2,1,0:T(8,128)(2,1)S(1)}, u32[]{:S(2)}, u32[]{:S(2)}) %collective-permute-start.6) | collective-permute-done | bytes 458784 | tf_op jit(solution)/shard_map/ppermute | solution.py:173
  62.5 1.3 collective-permute-start.8
  63.8 0.2 convolution_bitcast_fusion
  64.0 13.5 %all_to_all.31 = f32[8,8,512]{2,1,0:T(8,128)S(1)} all-to-all(f32[8,8,512]{2,1,0:T(8,128)S(1)} %bitcast.34), channel_id=1, replica_groups=mesh['zl'=8,'y'=4,'x'=4,'zh'=2,'c'=2] {'x','c'}, dimensions={0} | all-to-all | bytes 262144 | tf_op jit(solution)/shard_map/all_to_all | solution.py:250
  77.5 0.0 collective-permute-done.5.refs_4_
  77.5 1.5 collective-permute-start.7
  79.0 0.0 copy-done.4
  79.0 0.0 collective-permute-done.8.refs_11_
  79.0 1.3 collective-permute-start.10
  80.3 0.0 collective-permute-done.7.refs_5_
  80.3 1.5 collective-permute-start.9
  81.8 12.3 %all-gather = bf16[64,512]{1,0:T(8,128)(2,1)S(1)} all-gather(bf16[32,512]{1,0:T(8,128)(2,1)S(1)} %pad_maximum_fusion.2), channel_id=2, replica_groups=mesh['zl'=8,'y'=4,'x'=4,'zh'=2,'c'=2] {'zh'}, dimensions={0}, use_global_device_ids=true | all-gather | bytes 98304 | tf_op jit(solution)/shard_map/all_gather | solution.py:205
  94.1 0.0 collective-permute-done.10.refs_12_
  94.1 1.3 collective-permute-start.12
  95.4 0.0 collective-permute-done.9.refs_6_
  95.5 1.3 broadcast_in_dim.44
  96.8 6.3 %all-to-all-start.2 = ((bf16[32,48,512]{2,1,0:T(8,128)(2,1)}), bf16[32,48,512]{2,1,0:T(8,128)(2,1)}, u32[]{:S(2)}, u32[]{:S(2)}) async-start(bf16[32,48,512]{2,1,0:T(8,128)(2,1)} %broadcast_in_dim.44), calls=%async_computation.2 | async-start | bytes 3145728 | tf_op jit(solution)/shard_map/all_to_all | solution.py:71
  103.1 0.1 dynamic-slice_bitcast_fusion.1
  103.2 13.0 %collective-permute-done.12.refs_13_ = bf16[4,448,128]{2,1,0:T(8,128)(2,1)} collective-permute-done((bf16[4,448,128]{2,1,0:T(8,128)(2,1)}, bf16[4,448,128]{2,1,0:T(8,128)(2,1)}, u32[]{:S(2)}, u32[]{:S(2)}) %collective-permute-start.12) | collective-permute-done | bytes 458784 | tf_op jit(solution)/shard_map/ppermute | solution.py:173
  116.1 1.3 collective-permute-start.13
  117.4 1.4 collective-permute-start.11
  118.9 8.7 %collective-permute-done.13.refs_14_ = bf16[4,448,128]{2,1,0:T(8,128)(2,1)} collective-permute-done((bf16[4,448,128]{2,1,0:T(8,128)(2,1)}, bf16[4,448,128]{2,1,0:T(8,128)(2,1)}, u32[]{:S(2)}, u32[]{:S(2)}) %collective-permute-start.13) | collective-permute-done | bytes 458784 | tf_op jit(solution)/shard_map/ppermute | solution.py:173
  127.7 0.0 collective-permute-done.11.refs_7_
  127.7 14.7 %layer.1 = f32[32,2,2048]{2,1,0:T(2,128)} custom-call(s32[1]{0:T(128)} %bitcast.10.place_ref, bf16[64,256]{1,0:T(8,128)(2,1)S(1)} %pad.9.factor_ref, bf16[4,448,128]{2,1,0:T(8,128)(2,1)S(1)} %all_to_all.30.refs_0_, bf16[4,448,128]{2,1,0:T(8,128)(2,1)S(1)} %collective-permute-done.refs_1_, bf16[4,448,128]{2,1,0:T(8,128)(2,1)S(1)} %collective-permute-done.1.refs_2_, ...), custom_call_target="tpu_custom_call" | custom-call | flops 7046430720 | bytes 19398656 | tf_op jit(solution)/shard_map/layer/pallas_call | solution.py:137
  142.4 0.0 all-to-all-done.2
  142.4 7.6 %all-to-all-start.3 = ((f32[32,2,2048]{2,1,0:T(2,128)}), f32[32,2,2048]{2,1,0:T(2,128)S(1)}, u32[]{:S(2)}, u32[]{:S(2)}) async-start(f32[32,2,2048]{2,1,0:T(2,128)} %layer.1), calls=%async_computation.3 | async-start | bytes 1048576 | tf_op jit(solution)/shard_map/all_to_all | solution.py:264
  150.1 1.2 slice_convert_fusion
  151.2 0.1 slice_add_fusion
  151.4 10.2 %all-to-all-done.3 = f32[32,2,2048]{2,1,0:T(2,128)S(1)} async-done(((f32[32,2,2048]{2,1,0:T(2,128)}), f32[32,2,2048]{2,1,0:T(2,128)S(1)}, u32[]{:S(2)}, u32[]{:S(2)}) %all-to-all-start.3) | async-done | bytes 524320 | tf_op jit(solution)/shard_map/all_to_all | solution.py:264
  161.6 0.2 reduce_sum.38
  161.8 0.1 broadcast_select_fusion
  161.9 0.1 select_n.57
  162.0 0.5 convolution_multiply_fusion
  162.6 0.1 broadcast_in_dim.47
  162.7 30.3 %all_to_all.32 = f32[16,12,128]{2,1,0:T(8,128)S(1)} all-to-all(f32[16,12,128]{2,1,0:T(8,128)S(1)} %broadcast_in_dim.48), channel_id=1, replica_groups=mesh['zl'=8,'y'=4,'x'=4,'zh'=2,'c'=2] {'zh','zl'}, dimensions={0} | all-to-all | bytes 196608 | tf_op jit(solution)/shard_map/all_to_all | solution.py:71
  193.0 1.0 broadcast_in_dim.49
  194.0 7.0 %all-to-all-start.5 = ((bf16[32,96,128]{2,1,0:T(8,128)(2,1)}), bf16[32,96,128]{2,1,0:T(8,128)(2,1)S(1)}, u32[]{:S(2)}, u32[]{:S(2)}) async-start(bf16[32,96,128]{2,1,0:T(8,128)(2,1)} %broadcast_in_dim.49), calls=%async_computation.5 | async-start | bytes 1572864 | tf_op jit(solution)/shard_map/all_to_all | solution.py:71
  201.0 1.0 dynamic-slice_bitcast_fusion
  202.0 0.1 reshape.116
  202.1 0.3 copy.16
  202.4 0.2 reshape.117.queries_ref
  202.6 12.7 %all-to-all-done.5.features_ref = bf16[32,96,128]{2,1,0:T(8,128)(2,1)S(1)} async-done(((bf16[32,96,128]{2,1,0:T(8,128)(2,1)}), bf16[32,96,128]{2,1,0:T(8,128)(2,1)S(1)}, u32[]{:S(2)}, u32[]{:S(2)}) %all-to-all-start.5) | async-done | bytes 786464 | tf_op jit(solution)/shard_map/all_to_all | solution.py:71
  215.3 15.7 %solve.1 = f32[32,96]{1,0:T(8,128)} custom-call(bf16[32,96,128]{2,1,0:T(8,128)(2,1)S(1)} %all-to-all-done.5.features_ref, bf16[32,4096]{1,0:T(8,128)(2,1)S(1)} %reshape.117.queries_ref), custom_call_target="tpu_custom_call" | custom-call | tf_op jit(solution)/shard_map/solve/pallas_call | solution.py:62
  (25 shorter events, 0.2 us)
Async XLA Ops:
  6.5 96.5 %copy-start = (bf16[896,64]{0,1:T(8,128)(2,1)S(1)}, bf16[896,64]{0,1:T(8,128)(2,1)}, u32[]{:S(2)}) copy-start(bf16[896,64]{0,1:T(8,128)(2,1)} %param.11) | copy-start | bytes 344068
  6.5 121.1 %all-gather.4.cloned.1.call-start = ((), (), s32[]{:S(2)}) async-start(), calls=%async_computation.6 | async-start | bytes 17694720 | tf_op jit(solution)/shard_map/all_gather | solution.py:238
  9.6 0.9 copy-start.1
  9.6 1.1 copy-start.2
  9.6 54.2 %copy-start.3 = (bf16[256,64]{0,1:T(8,128)(2,1)S(1)}, bf16[256,64]{0,1:T(8,128)(2,1)}, u32[]{:S(2)}) copy-start(bf16[256,64]{0,1:T(8,128)(2,1)} %param.12) | copy-start | bytes 98308
  10.5 68.5 %copy-start.4 = (bf16[32,256]{1,0:T(8,128)(2,1)S(1)}, bf16[32,256]{1,0:T(8,128)(2,1)}, u32[]{:S(2)}) copy-start(bf16[32,256]{1,0:T(8,128)(2,1)} %param.13) | copy-start | bytes 49156
  22.3 12.2 %collective-permute-start = (bf16[4,448,128]{2,1,0:T(8,128)(2,1)S(1)}, bf16[4,448,128]{2,1,0:T(8,128)(2,1)S(1)}, u32[]{:S(2)}, u32[]{:S(2)}) collective-permute-start(bf16[4,448,128]{2,1,0:T(8,128)(2,1)S(1)} %all_to_all.30.refs_0_), channel_id=1, source_target_pairs={{0,64},{64,128},{128,192},{192,256},{256,320},{320,384},{384,448},... | collective-permute-start | bytes 1376264 | tf_op jit(solution)/shard_map/ppermute | solution.py:172
  26.9 11.9 %collective-permute-start.2 = (bf16[4,448,128]{2,1,0:T(8,128)(2,1)S(1)}, bf16[4,448,128]{2,1,0:T(8,128)(2,1)S(1)}, u32[]{:S(2)}, u32[]{:S(2)}) collective-permute-start(bf16[4,448,128]{2,1,0:T(8,128)(2,1)S(1)} %all_to_all.30.refs_0_), channel_id=1, source_target_pairs={{64,0},{128,64},{192,128},{256,192},{320,256},{384,320},{448,384},... | collective-permute-start | bytes 1376264 | tf_op jit(solution)/shard_map/ppermute | solution.py:173
  34.5 5.6 %collective-permute-start.1 = (bf16[4,448,128]{2,1,0:T(8,128)(2,1)S(1)}, bf16[4,448,128]{2,1,0:T(8,128)(2,1)S(1)}, u32[]{:S(2)}, u32[]{:S(2)}) collective-permute-start(bf16[4,448,128]{2,1,0:T(8,128)(2,1)S(1)} %collective-permute-done.refs_1_), channel_id=1, source_target_pairs={{64,128},{128,192},{192,256},{256,320},{320,384},{384,448},{65,129... | collective-permute-start | bytes 1376264 | tf_op jit(solution)/shard_map/ppermute | solution.py:172
  38.8 11.3 %collective-permute-start.4 = (bf16[4,448,128]{2,1,0:T(8,128)(2,1)S(1)}, bf16[4,448,128]{2,1,0:T(8,128)(2,1)S(1)}, u32[]{:S(2)}, u32[]{:S(2)}) collective-permute-start(bf16[4,448,128]{2,1,0:T(8,128)(2,1)S(1)} %collective-permute-done.2.refs_8_), channel_id=1, source_target_pairs={{64,0},{128,64},{192,128},{256,192},{320,256},{384,320},{65,1},{12... | collective-permute-start | bytes 1376264 | tf_op jit(solution)/shard_map/ppermute | solution.py:173
  40.1 11.3 %collective-permute-start.3 = (bf16[4,448,128]{2,1,0:T(8,128)(2,1)S(1)}, bf16[4,448,128]{2,1,0:T(8,128)(2,1)S(1)}, u32[]{:S(2)}, u32[]{:S(2)}) collective-permute-start(bf16[4,448,128]{2,1,0:T(8,128)(2,1)S(1)} %collective-permute-done.1.refs_2_), channel_id=1, source_target_pairs={{128,192},{192,256},{256,320},{320,384},{384,448},{129,193},{193,2... | collective-permute-start | bytes 1376264 | tf_op jit(solution)/shard_map/ppermute | solution.py:172
  50.1 12.5 %collective-permute-start.6 = (bf16[4,448,128]{2,1,0:T(8,128)(2,1)S(1)}, bf16[4,448,128]{2,1,0:T(8,128)(2,1)S(1)}, u32[]{:S(2)}, u32[]{:S(2)}) collective-permute-start(bf16[4,448,128]{2,1,0:T(8,128)(2,1)S(1)} %collective-permute-done.4.refs_9_), channel_id=1, source_target_pairs={{64,0},{128,64},{192,128},{256,192},{320,256},{65,1},{129,65},{193... | collective-permute-start | bytes 1376264 | tf_op jit(solution)/shard_map/ppermute | solution.py:173
  51.4 26.2 %collective-permute-start.5 = (bf16[4,448,128]{2,1,0:T(8,128)(2,1)S(1)}, bf16[4,448,128]{2,1,0:T(8,128)(2,1)}, u32[]{:S(2)}, u32[]{:S(2)}) collective-permute-start(bf16[4,448,128]{2,1,0:T(8,128)(2,1)S(1)} %collective-permute-done.3.refs_3_), channel_id=1, source_target_pairs={{192,256},{256,320},{320,384},{384,448},{193,257},{257,321},{321,3... | collective-permute-start | bytes 1376264 | tf_op jit(solution)/shard_map/ppermute | solution.py:172
  62.5 16.5 %collective-permute-start.8 = (bf16[4,448,128]{2,1,0:T(8,128)(2,1)S(1)}, bf16[4,448,128]{2,1,0:T(8,128)(2,1)}, u32[]{:S(2)}, u32[]{:S(2)}) collective-permute-start(bf16[4,448,128]{2,1,0:T(8,128)(2,1)S(1)} %collective-permute-done.6.refs_10_), channel_id=1, source_target_pairs={{64,0},{128,64},{192,128},{256,192},{65,1},{129,65},{193,129},{257... | collective-permute-start | bytes 1376264 | tf_op jit(solution)/shard_map/ppermute | solution.py:173
  77.5 2.8 %collective-permute-start.7 = (bf16[4,448,128]{2,1,0:T(8,128)(2,1)}, bf16[4,448,128]{2,1,0:T(8,128)(2,1)}, u32[]{:S(2)}, u32[]{:S(2)}) collective-permute-start(bf16[4,448,128]{2,1,0:T(8,128)(2,1)} %collective-permute-done.5.refs_4_), channel_id=1, source_target_pairs={{256,320},{320,384},{384,448},{257,321},{321,385},{385,449},{258,3... | collective-permute-start | bytes 1376264 | tf_op jit(solution)/shard_map/ppermute | solution.py:172
  79.0 15.1 %collective-permute-start.10 = (bf16[4,448,128]{2,1,0:T(8,128)(2,1)}, bf16[4,448,128]{2,1,0:T(8,128)(2,1)}, u32[]{:S(2)}, u32[]{:S(2)}) collective-permute-start(bf16[4,448,128]{2,1,0:T(8,128)(2,1)} %collective-permute-done.8.refs_11_), channel_id=1, source_target_pairs={{64,0},{128,64},{192,128},{65,1},{129,65},{193,129},{66,2},{130,66... | collective-permute-start | bytes 1376264 | tf_op jit(solution)/shard_map/ppermute | solution.py:173
  80.3 15.1 %collective-permute-start.9 = (bf16[4,448,128]{2,1,0:T(8,128)(2,1)}, bf16[4,448,128]{2,1,0:T(8,128)(2,1)}, u32[]{:S(2)}, u32[]{:S(2)}) collective-permute-start(bf16[4,448,128]{2,1,0:T(8,128)(2,1)} %collective-permute-done.7.refs_5_), channel_id=1, source_target_pairs={{320,384},{384,448},{321,385},{385,449},{322,386},{386,450},{323,3... | collective-permute-start | bytes 1376264 | tf_op jit(solution)/shard_map/ppermute | solution.py:172
  94.1 22.0 %collective-permute-start.12 = (bf16[4,448,128]{2,1,0:T(8,128)(2,1)}, bf16[4,448,128]{2,1,0:T(8,128)(2,1)}, u32[]{:S(2)}, u32[]{:S(2)}) collective-permute-start(bf16[4,448,128]{2,1,0:T(8,128)(2,1)} %collective-permute-done.10.refs_12_), channel_id=1, source_target_pairs={{64,0},{128,64},{65,1},{129,65},{66,2},{130,66},{67,3},{131,67},{6... | collective-permute-start | bytes 1376264 | tf_op jit(solution)/shard_map/ppermute | solution.py:173
  96.8 45.6 %all-to-all-start.2 = ((bf16[32,48,512]{2,1,0:T(8,128)(2,1)}), bf16[32,48,512]{2,1,0:T(8,128)(2,1)}, u32[]{:S(2)}, u32[]{:S(2)}) async-start(bf16[32,48,512]{2,1,0:T(8,128)(2,1)} %broadcast_in_dim.44), calls=%async_computation.2 | async-start | bytes 3145728 | tf_op jit(solution)/shard_map/all_to_all | solution.py:71
  116.1 11.5 %collective-permute-start.13 = (bf16[4,448,128]{2,1,0:T(8,128)(2,1)}, bf16[4,448,128]{2,1,0:T(8,128)(2,1)}, u32[]{:S(2)}, u32[]{:S(2)}) collective-permute-start(bf16[4,448,128]{2,1,0:T(8,128)(2,1)} %collective-permute-done.12.refs_13_), channel_id=1, source_target_pairs={{64,0},{65,1},{66,2},{67,3},{68,4},{69,5},{70,6},{71,7},{72,8},{73... | collective-permute-start | bytes 1376264 | tf_op jit(solution)/shard_map/ppermute | solution.py:173
  117.4 10.2 %collective-permute-start.11 = (bf16[4,448,128]{2,1,0:T(8,128)(2,1)}, bf16[4,448,128]{2,1,0:T(8,128)(2,1)}, u32[]{:S(2)}, u32[]{:S(2)}) collective-permute-start(bf16[4,448,128]{2,1,0:T(8,128)(2,1)} %collective-permute-done.9.refs_6_), channel_id=1, source_target_pairs={{384,448},{385,449},{386,450},{387,451},{388,452},{389,453},{390,4... | collective-permute-start | bytes 1376264 | tf_op jit(solution)/shard_map/ppermute | solution.py:172
  142.4 19.2 %all-to-all-start.3 = ((f32[32,2,2048]{2,1,0:T(2,128)}), f32[32,2,2048]{2,1,0:T(2,128)S(1)}, u32[]{:S(2)}, u32[]{:S(2)}) async-start(f32[32,2,2048]{2,1,0:T(2,128)} %layer.1), calls=%async_computation.3 | async-start | bytes 1048576 | tf_op jit(solution)/shard_map/all_to_all | solution.py:264
  194.0 21.3 %all-to-all-start.5 = ((bf16[32,96,128]{2,1,0:T(8,128)(2,1)}), bf16[32,96,128]{2,1,0:T(8,128)(2,1)S(1)}, u32[]{:S(2)}, u32[]{:S(2)}) async-start(bf16[32,96,128]{2,1,0:T(8,128)(2,1)} %broadcast_in_dim.49), calls=%async_computation.5 | async-start | bytes 1572864 | tf_op jit(solution)/shard_map/all_to_all | solution.py:71
Sparse Core Ops, SparseCore 0:
  9.7 93.9 all-gather.3

commit v3 on v2

--- a/solution.py
+++ b/solution.py
@@ -35,21 +35,38 @@
     system = system * row_scale * jnp.where(lane < count, lane_scale, 1.0)
     groups = [system[8 * g : 8 * g + 8] for g in range(count // 8)]
     inner = lax.broadcasted_iota(jnp.int32, groups[0].shape, 0)
-    for k in range(0, count, 2):
-        g, r = k // 8, k % 8
-        p, q = groups[g][r : r + 1], groups[g][r + 1 : r + 2]
-        a, b, c, d = p[:, k : k + 1], p[:, k + 1 : k + 2], q[:, k : k + 1], q[:, k + 1 : k + 2]
-        inverse = 1.0 / (a * d - b * c)
-        first = (d * inverse) * p - (b * inverse) * q
-        second = (a * inverse) * q - (c * inverse) * p
-        updated = [
-            block - block[:, k : k + 1] * first - block[:, k + 1 : k + 2] * second
-            for block in groups
-        ]
-        updated[g] = jnp.where(
-            inner == r, first, jnp.where(inner == r + 1, second, updated[g])
+    whole = groups[0].shape
+    side = 4
+    for low in range(0, len(groups), side):
+        inside = groups[low : low + side]
+        for k in range(8 * low, 8 * (low + side), 2):
+            g, r = k // 8 - low, k % 8
+            p = jnp.broadcast_to(inside[g][r : r + 1], whole)
+            q = jnp.broadcast_to(inside[g][r + 1 : r + 2], whole)
+            a, b, c, d = (
+                jnp.broadcast_to(v[:, n : n + 1], whole) for v in (p, q) for n in (k, k + 1)
+            )
+            inverse = 1.0 / (a * d - b * c)
+            first = (d * inverse) * p - (b * inverse) * q
+            second = (a * inverse) * q - (c * inverse) * p
+            updated = [
+                block
+                - jnp.broadcast_to(block[:, k : k + 1], whole) * first
+                - jnp.broadcast_to(block[:, k + 1 : k + 2], whole) * second
+                for block in inside
+            ]
+            updated[g] = jnp.where(
+                inner == r, first, jnp.where(inner == r + 1, second, updated[g])
+            )
+            inside = updated
+        rest = jnp.concatenate(groups[:low] + groups[low + side :], axis=0)
+        rest = rest - lax.dot_general(
+            rest[:, 8 * low : 8 * (low + side)], jnp.concatenate(inside, axis=0),
+            (((1,), (0,)), ((), ())),
+            precision=HIGHEST, preferred_element_type=jnp.float32,
         )
-        groups = updated
+        rest = [rest[8 * n : 8 * n + 8] for n in range(len(groups) - side)]
+        groups = rest[:low] + inside + rest[low:]
     groups = [block * row_scale[8 * g : 8 * g + 8] for g, block in enumerate(groups)]
     width = system.shape[1]
     groups += [jnp.zeros_like(groups[0])] * (width // 8 - len(groups))
@@ -156,6 +173,41 @@
     )(place, factor, *blocks, tokens)
 
 
+def half_kernel(place_ref, tokens_ref, half_ref, held, sems):
+    pieces, rows, _ = held.shape
+    start = place_ref[0] * (pieces * rows)
+    loads, stores = [], []
+    for n in range(pieces):
+        here = pl.ds(pl.multiple_of(start + n * rows, 16), rows)
+        loads.append(pltpu.make_async_copy(tokens_ref.at[here], held.at[n], sems.at[0, n]))
+        there = pl.ds(n * rows, rows)
+        stores.append(pltpu.make_async_copy(held.at[n], half_ref.at[there], sems.at[1, n]))
+    for load in loads:
+        load.start()
+    for load, store in zip(loads, stores):
+        load.wait()
+        store.start()
+    for store in stores:
+        store.wait()
+
+
+def core_half(tokens, c):
+    rows, depth = tokens.shape
+    pieces = 3
+    anywhere = pl.BlockSpec(memory_space=pl.ANY)
+    return pl.pallas_call(
+        half_kernel,
+        out_shape=jax.ShapeDtypeStruct((rows // 2, depth), tokens.dtype),
+        in_specs=[pl.BlockSpec(memory_space=pltpu.SMEM), anywhere],
+        out_specs=anywhere,
+        scratch_shapes=[
+            pltpu.VMEM((pieces, rows // 2 // pieces, depth), tokens.dtype),
+            pltpu.SemaphoreType.DMA((2, pieces)),
+        ],
+        name="core_half",
+    )(jnp.reshape(c, (1,)).astype(jnp.int32), tokens)
+
+
 def tie(value, *after):
     return lax.optimization_barrier((value,) + after)[0]
 
@@ -234,7 +286,7 @@
     rank = in_factor.shape[1]
     half = rows // 2
     z, y, c = (lax.axis_index(name) for name in ("zl", "y", "c"))
-    mine = lax.dynamic_slice_in_dim(tokens, c * half, half, 0)
+    mine = core_half(tokens, c)
     plane_tokens = lax.all_gather(mine, ("y", "c"))
     quarter = in_factor.shape[0] // Y
     factor = lax.dynamic_slice_in_dim(in_factor, y * quarter, quarter, 0).T
@@ -246,16 +298,16 @@
     for s in range(1, ZL):
         chain.step()
         if s == 2:
-            out = tie(out, chain.ups[-1]).reshape(X * C, rank // (X * C), -1)
+            out = tie(out, chain.ups[-1], chain.downs[-1]).reshape(X * C, rank // (X * C), -1)
             out = lax.all_to_all(out, ("x", "c"), 0, 0, tiled=True).sum(0)
         if s == 4:
             chain.after(out)
-            out = tie(out, chain.ups[-1])
+            out = tie(out, chain.ups[-1], chain.downs[-1])
             out, query_rows = exchange_z(out, queries)
         if s == 6:
             chain.after(out, query_rows)
-            out = tie(out, chain.ups[-1])
-            shared = share_plane(out, query_rows)
+    out = tie(out, chain.ups[-1], chain.downs[-1])
+    shared = share_plane(out, query_rows)
 
     place = jnp.stack([z]).astype(jnp.int32)
     in_part = layer(place, factor, chain.blocks(), plane_tokens)

time: 239 us -> 239 us (level)
  waiting for transfers between devices: 72.6 us -> 81.8 us
  blocking collectives: 67.5 us -> 60.4 us
  Pallas kernels: 30.4 us -> 25.4 us
  local copies, waits for them, and re-layouts: 9.57 us -> 13.7 us
    ppermute x7, waiting for transfers between devices: 43.3 us -> 54.6 us  [step(): lax.ppermute(down, 'zl', [(z, z - 1) for z in range(1, ZL + 1 - s)])]
    all_to_all x1, blocking collectives: 30.3 us -> 22.2 us  [share(): lax.all_to_all(jnp.broadcast_to(x[None], (count,) + x.shape), axes, 0, 0,...]
    unnamed x10 -> x26, local copies, waits for them, and re-layouts: 0.92 us -> 8.08 us
    pallas_call x1, Pallas kernels: 15.7 us -> 8.82 us  [solve(): pl.pallas_call(solve_body, out_shape=jax.ShapeDtypeStruct((queries.shape[...]
    ppermute x7, waiting for transfers between devices: 6.32 us -> 0.2 us  [step(): lax.ppermute(up, 'zl', [(z, z + 1) for z in range(s - 1, ZL - 1)])]
    all_to_all x2, waiting for transfers between devices: 12.7 us -> 16.6 us  [share(): lax.all_to_all(jnp.broadcast_to(x[None], (count,) + x.shape), axes, 0, 0,...]
    dynamic_slice x1 -> x0, local copies, waits for them, and re-layouts: 3.04 us -> none  [shards(): mine = lax.dynamic_slice_in_dim(tokens, c * half, half, 0)]
    pallas_call x0 -> x1, Pallas kernels: none -> 2.44 us  [core_half(): pl.pallas_call(half_kernel, out_shape=jax.ShapeDtypeStruct((rows // 2, de...]
  transfers between devices with their start and end apart: 18 -> 18, of which waited for: 8 -> 9; matrix products, arithmetic and copies ran while one was open for 3% -> 3% of each run, Pallas kernels for 6% -> 6%
where the time goes in v3:
time: 239 us; the launch traced here: 238 us
  waiting for transfers between devices  81.8 us (34%)
  blocking collectives  60.4 us (25%)
  starting transfers between devices  40.1 us (17%)
  Pallas kernels  25.4 us (11%)
  between operations  13.8 us (6%)
  local copies, waits for them, and re-layouts  13.7 us (6%)
    ppermute x7, waiting for transfers between devices, step(): lax.ppermute(down, 'zl', [(z, z - 1) for z in range(1, ZL + 1 - s)])  54.6 us
    all_to_all x1, blocking collectives, share(): lax.all_to_all(jnp.broadcast_to(x[None], (count,) + x.shape), axes, 0, 0,...  22.2 us
    all_to_all x2, waiting for transfers between devices, share(): lax.all_to_all(jnp.broadcast_to(x[None], (count,) + x.shape), axes, 0, 0,...  16.6 us
    all_to_all x2, starting transfers between devices, share(): lax.all_to_all(jnp.broadcast_to(x[None], (count,) + x.shape), axes, 0, 0,...  14.7 us
    pallas_call x1, Pallas kernels, layer(): pl.pallas_call(layer_kernel, out_shape=jax.ShapeDtypeStruct((rank // 2, 2...  14.2 us
    all_to_all x1, blocking collectives, shards(): out = lax.all_to_all(out, ('x', 'c'), 0, 0, tiled=True).sum(0)  13.6 us
    all_gather x1, blocking collectives, exchange_z(): got = lax.all_gather(sent, 'zh')  13.3 us
    all_to_all x1, blocking collectives, shards(): chain = Chain(lax.all_to_all(quarters, 'y', 0, 0, tiled=True))  11.4 us
  transfers between devices with their start and end apart: 18, of which 9 were waited for; matrix products, arithmetic and copies ran while one was open for 3% of the time, Pallas kernels for 6%

profile of v3, /device:TPU:1, one launch (start us, length us, event | category | flops | bytes accessed | tf_op | source)
XLA Modules:
  0.0 237.6 jit_solution(11300917603861240362)
XLA Ops:
  6.5 2.4 %core_half.1 = bf16[240,4096]{1,0:T(8,128)(2,1)} custom-call(s32[1]{0:T(128)} %bitcast.12.place_ref, bf16[480,4096]{1,0:T(8,128)(2,1)} %tokens_ref.1), custom_call_target="tpu_custom_call" | custom-call | tf_op jit(solution)/shard_map/core_half/pallas_call | solution.py:198
  9.0 0.0 copy-start.9
  9.0 0.0 all-gather.4.cloned.1.call-update
  9.0 0.9 copy-done.9
  9.9 0.2 copy.13
  10.1 0.2 copy.14
  10.3 0.0 copy-start.12
  10.4 11.4 %all_to_all.30.refs_0_ = bf16[4,448,128]{2,1,0:T(8,128)(2,1)S(1)} all-to-all(bf16[4,448,128]{2,1,0:T(8,128)(2,1)S(1)} %pad_maximum_fusion), channel_id=1, replica_groups=mesh['zl'=8,'y'=4,'x'=4,'zh'=2,'c'=2] {'y'}, dimensions={0} | all-to-all | bytes 917504 | tf_op jit(solution)/shard_map/all_to_all | solution.py:296
  21.8 1.3 collective-permute-start.2
  23.0 5.2 %collective-permute-start = (bf16[4,448,128]{2,1,0:T(8,128)(2,1)S(1)}, bf16[4,448,128]{2,1,0:T(8,128)(2,1)S(1)}, u32[]{:S(2)}, u32[]{:S(2)}) collective-permute-start(bf16[4,448,128]{2,1,0:T(8,128)(2,1)S(1)} %all_to_all.30.refs_0_), channel_id=1, source_target_pairs={{0,64},{64,128},{128,192},{192,256},{256,320},{320,384},{384,448},... | collective-permute-start | bytes 1376264 | tf_op jit(solution)/shard_map/ppermute | solution.py:224
  28.2 3.9 %collective-permute-done.2.refs_8_ = bf16[4,448,128]{2,1,0:T(8,128)(2,1)S(1)} collective-permute-done((bf16[4,448,128]{2,1,0:T(8,128)(2,1)S(1)}, bf16[4,448,128]{2,1,0:T(8,128)(2,1)S(1)}, u32[]{:S(2)}, u32[]{:S(2)}) %collective-permute-start.2) | collective-permute-done | bytes 458784 | tf_op jit(solution)/shard_map/ppermute | solution.py:225
  32.1 1.3 collective-permute-start.3
  33.4 0.2 collective-permute-done.refs_1_
  33.6 0.7 collective-permute-start.1
  34.3 12.0 %collective-permute-done.3.refs_9_ = bf16[4,448,128]{2,1,0:T(8,128)(2,1)S(1)} collective-permute-done((bf16[4,448,128]{2,1,0:T(8,128)(2,1)S(1)}, bf16[4,448,128]{2,1,0:T(8,128)(2,1)S(1)}, u32[]{:S(2)}, u32[]{:S(2)}) %collective-permute-start.3) | collective-permute-done | bytes 458784 | tf_op jit(solution)/shard_map/ppermute | solution.py:225
  46.3 1.3 collective-permute-start.6
  47.6 0.7 collective-permute-start.4
  48.3 8.8 %collective-permute-done.6.refs_10_ = bf16[4,448,128]{2,1,0:T(8,128)(2,1)S(1)} collective-permute-done((bf16[4,448,128]{2,1,0:T(8,128)(2,1)S(1)}, bf16[4,448,128]{2,1,0:T(8,128)(2,1)S(1)}, u32[]{:S(2)}, u32[]{:S(2)}) %collective-permute-start.6) | collective-permute-done | bytes 458784 | tf_op jit(solution)/shard_map/ppermute | solution.py:225
  57.1 1.3 collective-permute-start.7
  58.4 1.4 collective-permute-start.5
  59.9 1.0 pad.8
  60.9 0.2 convolution_bitcast_fusion
  61.1 13.6 %all_to_all.31 = f32[8,8,512]{2,1,0:T(8,128)S(1)} all-to-all(f32[8,8,512]{2,1,0:T(8,128)S(1)} %bitcast.35), channel_id=1, replica_groups=mesh['zl'=8,'y'=4,'x'=4,'zh'=2,'c'=2] {'x','c'}, dimensions={0} | all-to-all | bytes 262144 | tf_op jit(solution)/shard_map/all_to_all | solution.py:302
  74.7 1.3 collective-permute-start.10
  76.0 1.4 collective-permute-start.8
  77.4 13.1 %collective-permute-done.10.refs_12_ = bf16[4,448,128]{2,1,0:T(8,128)(2,1)} collective-permute-done((bf16[4,448,128]{2,1,0:T(8,128)(2,1)}, bf16[4,448,128]{2,1,0:T(8,128)(2,1)}, u32[]{:S(2)}, u32[]{:S(2)}) %collective-permute-start.10) | collective-permute-done | bytes 458784 | tf_op jit(solution)/shard_map/ppermute | solution.py:225
  90.6 1.3 collective-permute-start.12
  91.9 0.7 collective-permute-start.9
  92.6 13.3 %all-gather = bf16[64,512]{1,0:T(8,128)(2,1)S(1)} all-gather(bf16[32,512]{1,0:T(8,128)(2,1)S(1)} %pad_maximum_fusion.2), channel_id=2, replica_groups=mesh['zl'=8,'y'=4,'x'=4,'zh'=2,'c'=2] {'zh'}, dimensions={0}, use_global_device_ids=true | all-gather | bytes 98304 | tf_op jit(solution)/shard_map/all_gather | solution.py:257
  105.9 1.3 collective-permute-start.13
  107.2 0.8 copy-done.1
  108.0 0.7 collective-permute-start.11
  108.7 0.8 copy-done.3
  109.4 16.7 %collective-permute-done.13.refs_14_ = bf16[4,448,128]{2,1,0:T(8,128)(2,1)S(1)} collective-permute-done((bf16[4,448,128]{2,1,0:T(8,128)(2,1)S(1)}, bf16[4,448,128]{2,1,0:T(8,128)(2,1)S(1)}, u32[]{:S(2)}, u32[]{:S(2)}) %collective-permute-start.13) | collective-permute-done | bytes 458784 | tf_op jit(solution)/shard_map/ppermute | solution.py:225
  126.1 0.8 copy-done.5
  126.9 0.8 copy-done.7
  127.7 1.3 broadcast_in_dim.44
  129.1 7.8 %all-to-all-start.2 = ((bf16[32,48,512]{2,1,0:T(8,128)(2,1)}), bf16[32,48,512]{2,1,0:T(8,128)(2,1)}, u32[]{:S(2)}, u32[]{:S(2)}) async-start(bf16[32,48,512]{2,1,0:T(8,128)(2,1)} %broadcast_in_dim.44), calls=%async_computation.2 | async-start | bytes 3145728 | tf_op jit(solution)/shard_map/all_to_all | solution.py:88
  136.9 0.1 dynamic-slice_bitcast_fusion.1
  137.0 0.0 all-gather.4.cloned.1.call-done
  137.1 1.0 copy-done.2
  138.1 1.0 copy-done.4
  139.1 1.0 copy-done.6
  140.1 1.0 copy-done.8
  141.1 14.2 %layer.1 = f32[32,2,2048]{2,1,0:T(2,128)} custom-call(s32[1]{0:T(128)} %bitcast.10.place_ref, bf16[64,256]{1,0:T(8,128)(2,1)S(1)} %pad.9.factor_ref, bf16[4,448,128]{2,1,0:T(8,128)(2,1)S(1)} %all_to_all.30.refs_0_, bf16[4,448,128]{2,1,0:T(8,128)(2,1)S(1)} %collective-permute-done.refs_1_, bf16[4,448,128]{2,1,0:T(8,128)(2,1)S(1)} %collective-permute-done.1.refs_2_, ...), custom_call_target="tpu_custom_call" | custom-call | flops 7046430720 | bytes 19398656 | tf_op jit(solution)/shard_map/layer/pallas_call | solution.py:154
  155.3 3.9 %all-to-all-done.2 = bf16[32,48,512]{2,1,0:T(8,128)(2,1)} async-done(((bf16[32,48,512]{2,1,0:T(8,128)(2,1)}), bf16[32,48,512]{2,1,0:T(8,128)(2,1)}, u32[]{:S(2)}, u32[]{:S(2)}) %all-to-all-start.2) | async-done | bytes 1572896 | tf_op jit(solution)/shard_map/all_to_all | solution.py:88
  159.2 5.6 %all-to-all-start.3 = ((f32[32,2,2048]{2,1,0:T(2,128)}), f32[32,2,2048]{2,1,0:T(2,128)S(1)}, u32[]{:S(2)}, u32[]{:S(2)}) async-start(f32[32,2,2048]{2,1,0:T(2,128)} %layer.1), calls=%async_computation.3 | async-start | bytes 1048576 | tf_op jit(solution)/shard_map/all_to_all | solution.py:316
  164.7 1.2 slice_convert_fusion
  165.9 0.1 slice_add_fusion
  166.0 10.4 %all-to-all-done.3 = f32[32,2,2048]{2,1,0:T(2,128)S(1)} async-done(((f32[32,2,2048]{2,1,0:T(2,128)}), f32[32,2,2048]{2,1,0:T(2,128)S(1)}, u32[]{:S(2)}, u32[]{:S(2)}) %all-to-all-start.3) | async-done | bytes 524320 | tf_op jit(solution)/shard_map/all_to_all | solution.py:316
  176.4 0.2 reduce_sum.38
  176.6 0.1 broadcast_select_fusion
  176.7 0.1 select_n.53
  176.8 0.5 convolution_multiply_fusion
  177.4 0.1 broadcast_in_dim.47
  177.5 22.2 %all_to_all.32 = f32[16,12,128]{2,1,0:T(8,128)S(1)} all-to-all(f32[16,12,128]{2,1,0:T(8,128)S(1)} %broadcast_in_dim.48), channel_id=1, replica_groups=mesh['zl'=8,'y'=4,'x'=4,'zh'=2,'c'=2] {'zh','zl'}, dimensions={0} | all-to-all | bytes 196608 | tf_op jit(solution)/shard_map/all_to_all | solution.py:88
  199.7 1.0 broadcast_in_dim.49
  200.7 7.0 %all-to-all-start.5 = ((bf16[32,96,128]{2,1,0:T(8,128)(2,1)}), bf16[32,96,128]{2,1,0:T(8,128)(2,1)S(1)}, u32[]{:S(2)}, u32[]{:S(2)}) async-start(bf16[32,96,128]{2,1,0:T(8,128)(2,1)} %broadcast_in_dim.49), calls=%async_computation.5 | async-start | bytes 1572864 | tf_op jit(solution)/shard_map/all_to_all | solution.py:88
  207.6 1.0 dynamic-slice_bitcast_fusion
  208.7 0.1 reshape.120
  208.8 0.3 copy.16
  209.1 0.2 reshape.121.queries_ref
  209.3 12.7 %all-to-all-done.5.features_ref = bf16[32,96,128]{2,1,0:T(8,128)(2,1)S(1)} async-done(((bf16[32,96,128]{2,1,0:T(8,128)(2,1)}), bf16[32,96,128]{2,1,0:T(8,128)(2,1)S(1)}, u32[]{:S(2)}, u32[]{:S(2)}) %all-to-all-start.5) | async-done | bytes 786464 | tf_op jit(solution)/shard_map/all_to_all | solution.py:88
  222.0 8.8 %solve.1 = f32[32,96]{1,0:T(8,128)} custom-call(bf16[32,96,128]{2,1,0:T(8,128)(2,1)S(1)} %all-to-all-done.5.features_ref, bf16[32,4096]{1,0:T(8,128)(2,1)S(1)} %reshape.121.queries_ref), custom_call_target="tpu_custom_call" | custom-call | tf_op jit(solution)/shard_map/solve/pallas_call | solution.py:79
  (41 shorter events, 0.3 us)
Async XLA Ops:
  6.5 130.3 %copy-start = (bf16[896,64]{0,1:T(8,128)(2,1)S(1)}, bf16[896,64]{0,1:T(8,128)(2,1)}, u32[]{:S(2)}) copy-start(bf16[896,64]{0,1:T(8,128)(2,1)} %param.11) | copy-start | bytes 344068
  6.5 130.5 %all-gather.4.cloned.1.call-start = ((), (), s32[]{:S(2)}) async-start(), calls=%async_computation.6 | async-start | bytes 17694720 | tf_op jit(solution)/shard_map/all_gather | solution.py:290
  9.0 0.9 copy-start.9
  9.0 1.1 copy-start.10
  9.9 50.9 %copy-start.11 = (bf16[256,64]{0,1:T(8,128)(2,1)S(1)}, bf16[256,64]{0,1:T(8,128)(2,1)}, u32[]{:S(2)}) copy-start(bf16[256,64]{0,1:T(8,128)(2,1)} %param.12) | copy-start | bytes 98308
  10.3 67.1 %copy-start.12 = (bf16[32,256]{1,0:T(8,128)(2,1)S(1)}, bf16[32,256]{1,0:T(8,128)(2,1)}, u32[]{:S(2)}) copy-start(bf16[32,256]{1,0:T(8,128)(2,1)} %param.13) | copy-start | bytes 49156
  21.8 10.4 %collective-permute-start.2 = (bf16[4,448,128]{2,1,0:T(8,128)(2,1)S(1)}, bf16[4,448,128]{2,1,0:T(8,128)(2,1)S(1)}, u32[]{:S(2)}, u32[]{:S(2)}) collective-permute-start(bf16[4,448,128]{2,1,0:T(8,128)(2,1)S(1)} %all_to_all.30.refs_0_), channel_id=1, source_target_pairs={{64,0},{128,64},{192,128},{256,192},{320,256},{384,320},{448,384},... | collective-permute-start | bytes 1376264 | tf_op jit(solution)/shard_map/ppermute | solution.py:225
  23.0 10.6 %collective-permute-start = (bf16[4,448,128]{2,1,0:T(8,128)(2,1)S(1)}, bf16[4,448,128]{2,1,0:T(8,128)(2,1)S(1)}, u32[]{:S(2)}, u32[]{:S(2)}) collective-permute-start(bf16[4,448,128]{2,1,0:T(8,128)(2,1)S(1)} %all_to_all.30.refs_0_), channel_id=1, source_target_pairs={{0,64},{64,128},{128,192},{192,256},{256,320},{320,384},{384,448},... | collective-permute-start | bytes 1376264 | tf_op jit(solution)/shard_map/ppermute | solution.py:224
  32.1 14.2 %collective-permute-start.3 = (bf16[4,448,128]{2,1,0:T(8,128)(2,1)S(1)}, bf16[4,448,128]{2,1,0:T(8,128)(2,1)S(1)}, u32[]{:S(2)}, u32[]{:S(2)}) collective-permute-start(bf16[4,448,128]{2,1,0:T(8,128)(2,1)S(1)} %collective-permute-done.2.refs_8_), channel_id=1, source_target_pairs={{64,0},{128,64},{192,128},{256,192},{320,256},{384,320},{65,1},{12... | collective-permute-start | bytes 1376264 | tf_op jit(solution)/shard_map/ppermute | solution.py:225
  33.6 14.0 %collective-permute-start.1 = (bf16[4,448,128]{2,1,0:T(8,128)(2,1)S(1)}, bf16[4,448,128]{2,1,0:T(8,128)(2,1)S(1)}, u32[]{:S(2)}, u32[]{:S(2)}) collective-permute-start(bf16[4,448,128]{2,1,0:T(8,128)(2,1)S(1)} %collective-permute-done.refs_1_), channel_id=1, source_target_pairs={{64,128},{128,192},{192,256},{256,320},{320,384},{384,448},{65,129... | collective-permute-start | bytes 1376264 | tf_op jit(solution)/shard_map/ppermute | solution.py:224
  46.3 10.8 %collective-permute-start.6 = (bf16[4,448,128]{2,1,0:T(8,128)(2,1)S(1)}, bf16[4,448,128]{2,1,0:T(8,128)(2,1)S(1)}, u32[]{:S(2)}, u32[]{:S(2)}) collective-permute-start(bf16[4,448,128]{2,1,0:T(8,128)(2,1)S(1)} %collective-permute-done.3.refs_9_), channel_id=1, source_target_pairs={{64,0},{128,64},{192,128},{256,192},{320,256},{65,1},{129,65},{193... | collective-permute-start | bytes 1376264 | tf_op jit(solution)/shard_map/ppermute | solution.py:225
  47.6 10.8 %collective-permute-start.4 = (bf16[4,448,128]{2,1,0:T(8,128)(2,1)S(1)}, bf16[4,448,128]{2,1,0:T(8,128)(2,1)S(1)}, u32[]{:S(2)}, u32[]{:S(2)}) collective-permute-start(bf16[4,448,128]{2,1,0:T(8,128)(2,1)S(1)} %collective-permute-done.1.refs_2_), channel_id=1, source_target_pairs={{128,192},{192,256},{256,320},{320,384},{384,448},{129,193},{193,2... | collective-permute-start | bytes 1376264 | tf_op jit(solution)/shard_map/ppermute | solution.py:224
  57.1 17.5 %collective-permute-start.7 = (bf16[4,448,128]{2,1,0:T(8,128)(2,1)S(1)}, bf16[4,448,128]{2,1,0:T(8,128)(2,1)}, u32[]{:S(2)}, u32[]{:S(2)}) collective-permute-start(bf16[4,448,128]{2,1,0:T(8,128)(2,1)S(1)} %collective-permute-done.6.refs_10_), channel_id=1, source_target_pairs={{64,0},{128,64},{192,128},{256,192},{65,1},{129,65},{193,129},{257... | collective-permute-start | bytes 1376264 | tf_op jit(solution)/shard_map/ppermute | solution.py:225
  58.4 16.2 %collective-permute-start.5 = (bf16[4,448,128]{2,1,0:T(8,128)(2,1)S(1)}, bf16[4,448,128]{2,1,0:T(8,128)(2,1)}, u32[]{:S(2)}, u32[]{:S(2)}) collective-permute-start(bf16[4,448,128]{2,1,0:T(8,128)(2,1)S(1)} %collective-permute-done.4.refs_3_), channel_id=1, source_target_pairs={{192,256},{256,320},{320,384},{384,448},{193,257},{257,321},{321,3... | collective-permute-start | bytes 1376264 | tf_op jit(solution)/shard_map/ppermute | solution.py:224
  74.7 15.9 %collective-permute-start.10 = (bf16[4,448,128]{2,1,0:T(8,128)(2,1)}, bf16[4,448,128]{2,1,0:T(8,128)(2,1)}, u32[]{:S(2)}, u32[]{:S(2)}) collective-permute-start(bf16[4,448,128]{2,1,0:T(8,128)(2,1)} %collective-permute-done.7.refs_11_), channel_id=1, source_target_pairs={{64,0},{128,64},{192,128},{65,1},{129,65},{193,129},{66,2},{130,66... | collective-permute-start | bytes 1376264 | tf_op jit(solution)/shard_map/ppermute | solution.py:225
  76.0 15.9 %collective-permute-start.8 = (bf16[4,448,128]{2,1,0:T(8,128)(2,1)}, bf16[4,448,128]{2,1,0:T(8,128)(2,1)}, u32[]{:S(2)}, u32[]{:S(2)}) collective-permute-start(bf16[4,448,128]{2,1,0:T(8,128)(2,1)} %collective-permute-done.5.refs_4_), channel_id=1, source_target_pairs={{256,320},{320,384},{384,448},{257,321},{321,385},{385,449},{258,3... | collective-permute-start | bytes 1376264 | tf_op jit(solution)/shard_map/ppermute | solution.py:224
  90.6 15.3 %collective-permute-start.12 = (bf16[4,448,128]{2,1,0:T(8,128)(2,1)}, bf16[4,448,128]{2,1,0:T(8,128)(2,1)S(1)}, u32[]{:S(2)}, u32[]{:S(2)}) collective-permute-start(bf16[4,448,128]{2,1,0:T(8,128)(2,1)} %collective-permute-done.10.refs_12_), channel_id=1, source_target_pairs={{64,0},{128,64},{65,1},{129,65},{66,2},{130,66},{67,3},{131,67},{6... | collective-permute-start | bytes 1376264 | tf_op jit(solution)/shard_map/ppermute | solution.py:225
  91.9 16.1 %collective-permute-start.9 = (bf16[4,448,128]{2,1,0:T(8,128)(2,1)}, bf16[4,448,128]{2,1,0:T(8,128)(2,1)S(1)}, u32[]{:S(2)}, u32[]{:S(2)}) collective-permute-start(bf16[4,448,128]{2,1,0:T(8,128)(2,1)} %collective-permute-done.8.refs_5_), channel_id=1, source_target_pairs={{320,384},{384,448},{321,385},{385,449},{322,386},{386,450},{323,3... | collective-permute-start | bytes 1376264 | tf_op jit(solution)/shard_map/ppermute | solution.py:224
  105.9 20.3 %collective-permute-start.13 = (bf16[4,448,128]{2,1,0:T(8,128)(2,1)S(1)}, bf16[4,448,128]{2,1,0:T(8,128)(2,1)S(1)}, u32[]{:S(2)}, u32[]{:S(2)}) collective-permute-start(bf16[4,448,128]{2,1,0:T(8,128)(2,1)S(1)} %collective-permute-done.12.refs_13_), channel_id=1, source_target_pairs={{64,0},{65,1},{66,2},{67,3},{68,4},{69,5},{70,6},{71,7},{72,8},{73... | collective-permute-start | bytes 1376264 | tf_op jit(solution)/shard_map/ppermute | solution.py:225
  107.2 0.8 copy-start.1
  108.0 19.0 %collective-permute-start.11 = (bf16[4,448,128]{2,1,0:T(8,128)(2,1)S(1)}, bf16[4,448,128]{2,1,0:T(8,128)(2,1)S(1)}, u32[]{:S(2)}, u32[]{:S(2)}) collective-permute-start(bf16[4,448,128]{2,1,0:T(8,128)(2,1)S(1)} %collective-permute-done.9.refs_6_), channel_id=1, source_target_pairs={{384,448},{385,449},{386,450},{387,451},{388,452},{389,453},{390,4... | collective-permute-start | bytes 1376264 | tf_op jit(solution)/shard_map/ppermute | solution.py:224
  108.6 0.8 copy-start.3
  126.1 0.8 copy-start.5
  126.9 0.8 copy-start.7
  129.1 30.1 %all-to-all-start.2 = ((bf16[32,48,512]{2,1,0:T(8,128)(2,1)}), bf16[32,48,512]{2,1,0:T(8,128)(2,1)}, u32[]{:S(2)}, u32[]{:S(2)}) async-start(bf16[32,48,512]{2,1,0:T(8,128)(2,1)} %broadcast_in_dim.44), calls=%async_computation.2 | async-start | bytes 3145728 | tf_op jit(solution)/shard_map/all_to_all | solution.py:88
  137.1 1.0 copy-start.2
  138.1 1.0 copy-start.4
  139.1 1.0 copy-start.6
  140.1 1.0 copy-start.8
  159.2 17.2 %all-to-all-start.3 = ((f32[32,2,2048]{2,1,0:T(2,128)}), f32[32,2,2048]{2,1,0:T(2,128)S(1)}, u32[]{:S(2)}, u32[]{:S(2)}) async-start(f32[32,2,2048]{2,1,0:T(2,128)} %layer.1), calls=%async_computation.3 | async-start | bytes 1048576 | tf_op jit(solution)/shard_map/all_to_all | solution.py:316
  200.7 21.3 %all-to-all-start.5 = ((bf16[32,96,128]{2,1,0:T(8,128)(2,1)}), bf16[32,96,128]{2,1,0:T(8,128)(2,1)S(1)}, u32[]{:S(2)}, u32[]{:S(2)}) async-start(bf16[32,96,128]{2,1,0:T(8,128)(2,1)} %broadcast_in_dim.49), calls=%async_computation.5 | async-start | bytes 1572864 | tf_op jit(solution)/shard_map/all_to_all | solution.py:88
Sparse Core Ops, SparseCore 0:
  9.5 93.9 all-gather.3

commit v4 on v3

--- a/solution.py
+++ b/solution.py
@@ -173,41 +173,6 @@
     )(place, factor, *blocks, tokens)
 
 
-def half_kernel(place_ref, tokens_ref, half_ref, held, sems):
-    pieces, rows, _ = held.shape
-    start = place_ref[0] * (pieces * rows)
-    loads, stores = [], []
-    for n in range(pieces):
-        here = pl.ds(pl.multiple_of(start + n * rows, 16), rows)
-        loads.append(pltpu.make_async_copy(tokens_ref.at[here], held.at[n], sems.at[0, n]))
-        there = pl.ds(n * rows, rows)
-        stores.append(pltpu.make_async_copy(held.at[n], half_ref.at[there], sems.at[1, n]))
-    for load in loads:
-        load.start()
-    for load, store in zip(loads, stores):
-        load.wait()
-        store.start()
-    for store in stores:
-        store.wait()
-
-
-def core_half(tokens, c):
-    rows, depth = tokens.shape
-    pieces = 3
-    anywhere = pl.BlockSpec(memory_space=pl.ANY)
-    return pl.pallas_call(
-        half_kernel,
-        out_shape=jax.ShapeDtypeStruct((rows // 2, depth), tokens.dtype),
-        in_specs=[pl.BlockSpec(memory_space=pltpu.SMEM), anywhere],
-        out_specs=anywhere,
-        scratch_shapes=[
-            pltpu.VMEM((pieces, rows // 2 // pieces, depth), tokens.dtype),
-            pltpu.SemaphoreType.DMA((2, pieces)),
-        ],
-        name="core_half",
-    )(jnp.reshape(c, (1,)).astype(jnp.int32), tokens)
-
-
 def tie(value, *after):
     return lax.optimization_barrier((value,) + after)[0]
 
@@ -261,24 +226,10 @@
     return out, got[:, 2 * count :].reshape(ZH, rows, cols)
 
 
-def share_plane(out, queries):
-    high = lax.reduce_precision(out, 8, 7)
-    sent = jnp.concatenate(
-        [v.astype(jnp.bfloat16) for v in (high, out - high)]
-        + [queries.reshape(-1, out.shape[1])]
-    )
-    return share(sent, PLANE, Y * X * C)
-
-
-def unpack_plane(got, count, rows, cols):
-    lanes = got.shape[2]
-    parts = got[:, : 2 * count].astype(jnp.float32)
-    out = (parts[:, :count] + parts[:, count:]).reshape(Y, X * C * count, lanes)
-    here = got.reshape((Y, X * C) + got.shape[1:])
-    here = lax.dynamic_index_in_dim(here, lax.axis_index("y"), 0, keepdims=False)
-    queries = here[:, 2 * count :].reshape(X, C, ZH, rows, cols)
-    queries = queries.transpose(3, 0, 2, 1, 4).reshape(rows, -1)
-    return out.transpose(1, 0, 2).reshape(X * C * count, Y * lanes), queries
+def share_queries(queries):
+    _, rows, cols = queries.shape
+    got = share(queries, ("x", "c"), X * C).reshape(X, C, ZH, rows, cols)
+    return got.transpose(3, 0, 2, 1, 4).reshape(rows, -1)
 
 
 def shards(tokens, gate_weight, up_weight, out_grad, in_factor, out_factor, queries):
@@ -286,7 +237,7 @@
     rank = in_factor.shape[1]
     half = rows // 2
     z, y, c = (lax.axis_index(name) for name in ("zl", "y", "c"))
-    mine = core_half(tokens, c)
+    mine = lax.dynamic_slice_in_dim(tokens, c * half, half, 0)
     plane_tokens = lax.all_gather(mine, ("y", "c"))
     quarter = in_factor.shape[0] // Y
     factor = lax.dynamic_slice_in_dim(in_factor, y * quarter, quarter, 0).T
@@ -294,25 +245,24 @@
 
     quarters = weight_quarters(gate_weight, up_weight)
     chain = Chain(lax.all_to_all(quarters, "y", 0, 0, tiled=True))
-    out = out_partial(out_grad, out_factor)
+    out = out_partial(out_grad, out_factor).reshape(X * C, rank // (X * C), -1)
     for s in range(1, ZL):
         chain.step()
-        if s == 2:
-            out = tie(out, chain.ups[-1], chain.downs[-1]).reshape(X * C, rank // (X * C), -1)
+        if s == 1:
+            out = tie(out, chain.ups[-1])
             out = lax.all_to_all(out, ("x", "c"), 0, 0, tiled=True).sum(0)
-        if s == 4:
+        if s == 5:
             chain.after(out)
-            out = tie(out, chain.ups[-1], chain.downs[-1])
+            out = tie(out, chain.ups[-1])
             out, query_rows = exchange_z(out, queries)
         if s == 6:
-            chain.after(out, query_rows)
-    out = tie(out, chain.ups[-1], chain.downs[-1])
-    shared = share_plane(out, query_rows)
+            chain.after(out, plane_tokens)
+            out = tie(out, chain.ups[-1])
+            out = share(out, PLANE, Y * X * C)
+    out = out.reshape(Y, rank, -1).transpose(1, 0, 2).reshape(rank, -1)
 
     place = jnp.stack([z]).astype(jnp.int32)
     in_part = layer(place, factor, chain.blocks(), plane_tokens)
-    shared, in_part = lax.optimization_barrier((shared, in_part))
-    out, query_rows = unpack_plane(shared, rank // (X * C), *queries.shape)
     in_proj = lax.all_to_all(in_part, PLANE, 0, 0, tiled=True)
     in_proj = in_proj.sum(0)
 
@@ -323,7 +273,10 @@
     spread = jnp.where(mask[:, None, :], in_proj[None], 0.0).reshape(2 * seqs, -1)
     fragment = jnp.dot(spread, out.T, precision=HIGHEST) / jnp.sqrt(jnp.float32(LEN))
     fragment = fragment.reshape(seqs, 2 * rank)
+    fragment, query_rows = lax.optimization_barrier((fragment, query_rows))
     columns = share(fragment, ("zh", "zl"), ZH * ZL)
+    query_rows = share_queries(query_rows)
+    columns, query_rows = lax.optimization_barrier((columns, query_rows))
     columns = columns.reshape(ZH, ZL * seqs, 2 * rank).sum(0).astype(jnp.bfloat16)
     features = share(columns, PLANE, Y * X * C)
     return solve(features, query_rows)

time: 239 us -> 227 us (0.950)
  blocking collectives: 60.4 us -> 53.9 us
  starting transfers between devices: 40.1 us -> 46.1 us
  local copies, waits for them, and re-layouts: 13.7 us -> 7.94 us
  waiting for transfers between devices: 81.8 us -> 78.6 us
    all_to_all x1 -> x0, blocking collectives: 13.6 us -> none  [shards(): out = lax.all_to_all(out, ('x', 'c'), 0, 0, tiled=True).sum(0)]
    ppermute x7, waiting for transfers between devices: 54.6 us -> 45 us  [step(): lax.ppermute(down, 'zl', [(z, z - 1) for z in range(1, ZL + 1 - s)])]
    all_to_all x0 -> x1, starting transfers between devices: none -> 9.38 us  [shards(): out = lax.all_to_all(out, ('x', 'c'), 0, 0, tiled=True).sum(0)]
    unnamed x26 -> x10, local copies, waits for them, and re-layouts: 8.08 us -> 0.02 us
    all_to_all x1 -> x2, blocking collectives: 22.2 us -> 30.2 us  [share(): lax.all_to_all(jnp.broadcast_to(x[None], (count,) + x.shape), axes, 0, 0,...]
    ppermute x7, waiting for transfers between devices: 0.2 us -> 6.32 us  [step(): lax.ppermute(up, 'zl', [(z, z + 1) for z in range(s - 1, ZL - 1)])]
    all_to_all x0 -> x1, waiting for transfers between devices: none -> 5.3 us  [shards(): out = lax.all_to_all(out, ('x', 'c'), 0, 0, tiled=True).sum(0)]
    all_to_all x2, waiting for transfers between devices: 16.6 us -> 11.5 us  [share(): lax.all_to_all(jnp.broadcast_to(x[None], (count,) + x.shape), axes, 0, 0,...]
  transfers between devices with their start and end apart: 18 -> 19, of which waited for: 9 -> 10; matrix products, arithmetic and copies ran while one was open for 3% -> 2% of each run, Pallas kernels for 6% -> 7%
where the time goes in v4:
time: 227 us; the launch traced here: 226 us
  waiting for transfers between devices  78.6 us (35%)
  blocking collectives  53.9 us (24%)
  starting transfers between devices  46.1 us (20%)
  Pallas kernels  23.5 us (10%)
  between operations  13.8 us (6%)
  local copies, waits for them, and re-layouts  7.94 us (3%)
    ppermute x7, waiting for transfers between devices, step(): lax.ppermute(down, 'zl', [(z, z - 1) for z in range(1, ZL + 1 - s)])  45 us
    all_to_all x2, blocking collectives, share(): lax.all_to_all(jnp.broadcast_to(x[None], (count,) + x.shape), axes, 0, 0,...  30.2 us
    pallas_call x1, Pallas kernels, layer(): pl.pallas_call(layer_kernel, out_shape=jax.ShapeDtypeStruct((rank // 2, 2...  14.7 us
    all_gather x1, blocking collectives, exchange_z(): got = lax.all_gather(sent, 'zh')  12.3 us
    ppermute x7, starting transfers between devices, step(): lax.ppermute(up, 'zl', [(z, z + 1) for z in range(s - 1, ZL - 1)])  11.7 us
    all_to_all x2, waiting for transfers between devices, share(): lax.all_to_all(jnp.broadcast_to(x[None], (count,) + x.shape), axes, 0, 0,...  11.5 us
    all_to_all x1, blocking collectives, shards(): chain = Chain(lax.all_to_all(quarters, 'y', 0, 0, tiled=True))  11.4 us
    all_to_all x1, waiting for transfers between devices, shards(): in_proj = lax.all_to_all(in_part, PLANE, 0, 0, tiled=True)  10.5 us
  transfers between devices with their start and end apart: 19, of which 10 were waited for; matrix products, arithmetic and copies ran while one was open for 2% of the time, Pallas kernels for 7%

profile of v4, /device:TPU:1, one launch (start us, length us, event | category | flops | bytes accessed | tf_op | source)
XLA Modules:
  0.0 225.7 jit_solution(16119609754409986402)
XLA Ops:
  6.5 0.0 copy-start
  6.6 3.1 %constant_dynamic-slice_fusion = bf16[240,4096]{1,0:T(8,128)(2,1)} fusion(bf16[480,4096]{1,0:T(8,128)(2,1)} %param.7, s32[]{:T(128)S(6)} %select_n.51), kind=kLoop, calls=%fused_computation.30 | loop fusion | bytes 3932164 | tf_op jit(solution)/shard_map/dynamic_slice | solution.py:240
  9.6 0.0 all-gather.4.cloned.1.call-update
  9.7 0.2 copy.14
  9.9 0.0 copy-done.2
  9.9 0.2 copy.13
  10.1 11.4 %all_to_all.35.refs_0_ = bf16[4,448,128]{2,1,0:T(8,128)(2,1)S(1)} all-to-all(bf16[4,448,128]{2,1,0:T(8,128)(2,1)S(1)} %pad_maximum_fusion), channel_id=1, replica_groups=mesh['zl'=8,'y'=4,'x'=4,'zh'=2,'c'=2] {'y'}, dimensions={0} | all-to-all | bytes 917504 | tf_op jit(solution)/shard_map/all_to_all | solution.py:247
  21.5 4.5 %collective-permute-start = (bf16[4,448,128]{2,1,0:T(8,128)(2,1)S(1)}, bf16[4,448,128]{2,1,0:T(8,128)(2,1)S(1)}, u32[]{:S(2)}, u32[]{:S(2)}) collective-permute-start(bf16[4,448,128]{2,1,0:T(8,128)(2,1)S(1)} %all_to_all.35.refs_0_), channel_id=1, source_target_pairs={{0,64},{64,128},{128,192},{192,256},{256,320},{320,384},{384,448},... | collective-permute-start | bytes 1376264 | tf_op jit(solution)/shard_map/ppermute | solution.py:189
  26.0 1.3 collective-permute-start.2
  27.3 6.3 %collective-permute-done.refs_1_ = bf16[4,448,128]{2,1,0:T(8,128)(2,1)S(1)} collective-permute-done((bf16[4,448,128]{2,1,0:T(8,128)(2,1)S(1)}, bf16[4,448,128]{2,1,0:T(8,128)(2,1)S(1)}, u32[]{:S(2)}, u32[]{:S(2)}) %collective-permute-start) | collective-permute-done | bytes 458784 | tf_op jit(solution)/shard_map/ppermute | solution.py:189
  33.6 0.7 collective-permute-start.1
  34.3 3.5 %collective-permute-done.2.refs_8_ = bf16[4,448,128]{2,1,0:T(8,128)(2,1)S(1)} collective-permute-done((bf16[4,448,128]{2,1,0:T(8,128)(2,1)S(1)}, bf16[4,448,128]{2,1,0:T(8,128)(2,1)S(1)}, u32[]{:S(2)}, u32[]{:S(2)}) %collective-permute-start.2) | collective-permute-done | bytes 458784 | tf_op jit(solution)/shard_map/ppermute | solution.py:190
  37.8 1.3 collective-permute-start.4
  39.1 0.0 collective-permute-done.1.refs_2_
  39.1 0.7 collective-permute-start.3
  39.8 9.2 %collective-permute-done.4.refs_9_ = bf16[4,448,128]{2,1,0:T(8,128)(2,1)S(1)} collective-permute-done((bf16[4,448,128]{2,1,0:T(8,128)(2,1)S(1)}, bf16[4,448,128]{2,1,0:T(8,128)(2,1)S(1)}, u32[]{:S(2)}, u32[]{:S(2)}) %collective-permute-start.4) | collective-permute-done | bytes 458784 | tf_op jit(solution)/shard_map/ppermute | solution.py:190
  49.0 1.3 collective-permute-start.6
  50.3 0.0 collective-permute-done.3.refs_3_
  50.3 1.4 collective-permute-start.5
  51.7 9.9 %collective-permute-done.6.refs_10_ = bf16[4,448,128]{2,1,0:T(8,128)(2,1)S(1)} collective-permute-done((bf16[4,448,128]{2,1,0:T(8,128)(2,1)S(1)}, bf16[4,448,128]{2,1,0:T(8,128)(2,1)S(1)}, u32[]{:S(2)}, u32[]{:S(2)}) %collective-permute-start.6) | collective-permute-done | bytes 458784 | tf_op jit(solution)/shard_map/ppermute | solution.py:190
  61.7 1.3 collective-permute-start.8
  63.0 0.0 collective-permute-done.5.refs_4_
  63.0 1.5 collective-permute-start.7
  64.5 7.4 %collective-permute-done.8.refs_11_ = bf16[4,448,128]{2,1,0:T(8,128)(2,1)} collective-permute-done((bf16[4,448,128]{2,1,0:T(8,128)(2,1)S(1)}, bf16[4,448,128]{2,1,0:T(8,128)(2,1)}, u32[]{:S(2)}, u32[]{:S(2)}) %collective-permute-start.8) | collective-permute-done | bytes 458784 | tf_op jit(solution)/shard_map/ppermute | solution.py:190
  71.9 1.3 collective-permute-start.10
  73.2 1.0 pad.9
  74.2 0.9 convolution_bitcast_fusion
  75.0 9.4 %all-to-all-start.1 = ((f32[8,8,512]{2,1,0:T(8,128)}), f32[8,8,512]{2,1,0:T(8,128)S(1)}, u32[]{:S(2)}, u32[]{:S(2)}) async-start(f32[8,8,512]{2,1,0:T(8,128)} %convolution_bitcast_fusion), calls=%async_computation.1 | async-start | bytes 262144 | tf_op jit(solution)/shard_map/all_to_all | solution.py:253
  84.4 5.3 %all-to-all-done.1 = f32[8,8,512]{2,1,0:T(8,128)S(1)} async-done(((f32[8,8,512]{2,1,0:T(8,128)}), f32[8,8,512]{2,1,0:T(8,128)S(1)}, u32[]{:S(2)}, u32[]{:S(2)}) %all-to-all-start.1) | async-done | bytes 131104 | tf_op jit(solution)/shard_map/all_to_all | solution.py:253
  89.7 0.0 collective-permute-done.7.refs_5_
  89.7 1.5 collective-permute-start.9
  91.2 0.0 collective-permute-done.10.refs_12_
  91.2 1.3 collective-permute-start.12
  92.5 12.3 %all-gather = bf16[64,512]{1,0:T(8,128)(2,1)S(1)} all-gather(bf16[32,512]{1,0:T(8,128)(2,1)S(1)} %pad_maximum_fusion.1), channel_id=2, replica_groups=mesh['zl'=8,'y'=4,'x'=4,'zh'=2,'c'=2] {'zh'}, dimensions={0}, use_global_device_ids=true | all-gather | bytes 98304 | tf_op jit(solution)/shard_map/all_gather | solution.py:222
  104.8 0.0 collective-permute-done.9.refs_6_
  104.9 0.0 all-gather.4.cloned.1.call-done
  104.9 1.4 collective-permute-start.11
  106.3 0.2 collective-permute-done.12.refs_13_
  106.5 1.3 collective-permute-start.13
  107.8 0.0 copy-done
  107.8 0.1 dynamic-slice_bitcast_fusion
  107.9 0.9 broadcast_in_dim.31
  108.8 6.6 %all-to-all-start.3 = ((f32[32,8,512]{2,1,0:T(8,128)}), f32[32,8,512]{2,1,0:T(8,128)}, u32[]{:S(2)}, u32[]{:S(2)}) async-start(f32[32,8,512]{2,1,0:T(8,128)} %broadcast_in_dim.31), calls=%async_computation.3 | async-start | bytes 1048576 | tf_op jit(solution)/shard_map/all_to_all | solution.py:88
  115.4 0.0 collective-permute-done.11.refs_7_
  115.4 14.7 %collective-permute-done.13.refs_14_ = bf16[4,448,128]{2,1,0:T(8,128)(2,1)} collective-permute-done((bf16[4,448,128]{2,1,0:T(8,128)(2,1)}, bf16[4,448,128]{2,1,0:T(8,128)(2,1)}, u32[]{:S(2)}, u32[]{:S(2)}) %collective-permute-start.13) | collective-permute-done | bytes 458784 | tf_op jit(solution)/shard_map/ppermute | solution.py:190
  130.2 14.7 %layer.1 = f32[32,2,2048]{2,1,0:T(2,128)} custom-call(s32[1]{0:T(128)} %bitcast.place_ref, bf16[64,256]{1,0:T(8,128)(2,1)S(1)} %pad.8.factor_ref, bf16[4,448,128]{2,1,0:T(8,128)(2,1)S(1)} %all_to_all.35.refs_0_, bf16[4,448,128]{2,1,0:T(8,128)(2,1)S(1)} %collective-permute-done.refs_1_, bf16[4,448,128]{2,1,0:T(8,128)(2,1)S(1)} %collective-permute-done.1.refs_2_, ...), custom_call_target="tpu_custom_call" | custom-call | flops 7046430720 | bytes 19398656 | tf_op jit(solution)/shard_map/layer/pallas_call | solution.py:154
  144.9 0.0 all-to-all-done.3
  144.9 5.9 %all-to-all-start.2 = ((f32[32,2,2048]{2,1,0:T(2,128)}), f32[32,2,2048]{2,1,0:T(2,128)S(1)}, u32[]{:S(2)}, u32[]{:S(2)}) async-start(f32[32,2,2048]{2,1,0:T(2,128)} %layer.1), calls=%async_computation.2 | async-start | bytes 1048576 | tf_op jit(solution)/shard_map/all_to_all | solution.py:266
  150.9 1.1 copy.17
  152.0 10.5 %all-to-all-done.2 = f32[32,2,2048]{2,1,0:T(2,128)S(1)} async-done(((f32[32,2,2048]{2,1,0:T(2,128)}), f32[32,2,2048]{2,1,0:T(2,128)S(1)}, u32[]{:S(2)}, u32[]{:S(2)}) %all-to-all-start.2) | async-done | bytes 524320 | tf_op jit(solution)/shard_map/all_to_all | solution.py:266
  162.5 0.2 reduce_sum.38
  162.6 0.1 broadcast_select_fusion
  162.8 0.1 select_n.53
  162.9 0.5 convolution_multiply_fusion
  163.4 0.1 reshape.114
  163.5 9.4 %all_to_all.36 = bf16[8,2,32,256]{3,2,1,0:T(8,128)(2,1)S(1)} all-to-all(bf16[8,2,32,256]{3,2,1,0:T(8,128)(2,1)S(1)} %broadcast_in_dim.33), channel_id=1, replica_groups=mesh['zl'=8,'y'=4,'x'=4,'zh'=2,'c'=2] {'x','c'}, dimensions={0} | all-to-all | bytes 524288 | tf_op jit(solution)/shard_map/all_to_all | solution.py:88
  172.9 0.7 broadcast_in_dim.32
  173.6 3.5 %all-to-all-start.4 = ((f32[16,12,128]{2,1,0:T(8,128)}), f32[16,12,128]{2,1,0:T(8,128)S(1)}, u32[]{:S(2)}, u32[]{:S(2)}) async-start(f32[16,12,128]{2,1,0:T(8,128)} %broadcast_in_dim.32), calls=%async_computation.4 | async-start | bytes 262144 | tf_op jit(solution)/shard_map/all_to_all | solution.py:88
  177.1 0.3 copy.16
  177.3 0.2 reshape.117.queries_ref
  177.5 11.4 %all-to-all-done.4 = f32[16,12,128]{2,1,0:T(8,128)S(1)} async-done(((f32[16,12,128]{2,1,0:T(8,128)}), f32[16,12,128]{2,1,0:T(8,128)S(1)}, u32[]{:S(2)}, u32[]{:S(2)}) %all-to-all-start.4) | async-done | bytes 98336 | tf_op jit(solution)/shard_map/all_to_all | solution.py:88
  189.0 0.1 broadcast_in_dim.54
  189.1 20.9 %all_to_all.37.features_ref = bf16[32,96,128]{2,1,0:T(8,128)(2,1)S(1)} all-to-all(bf16[32,96,128]{2,1,0:T(8,128)(2,1)S(1)} %broadcast_in_dim.54), channel_id=1, replica_groups=mesh['zl'=8,'y'=4,'x'=4,'zh'=2,'c'=2] {'y','x','c'}, dimensions={0} | all-to-all | bytes 1572864 | tf_op jit(solution)/shard_map/all_to_all | solution.py:88
  210.0 8.8 %solve.1 = f32[32,96]{1,0:T(8,128)} custom-call(bf16[32,96,128]{2,1,0:T(8,128)(2,1)S(1)} %all_to_all.37.features_ref, bf16[32,4096]{1,0:T(8,128)(2,1)S(1)} %reshape.117.queries_ref), custom_call_target="tpu_custom_call" | custom-call | tf_op jit(solution)/shard_map/solve/pallas_call | solution.py:79
  (22 shorter events, 0.2 us)
Async XLA Ops:
  6.5 101.3 %copy-start = (bf16[896,64]{0,1:T(8,128)(2,1)S(1)}, bf16[896,64]{0,1:T(8,128)(2,1)}, u32[]{:S(2)}) copy-start(bf16[896,64]{0,1:T(8,128)(2,1)} %param.11) | copy-start | bytes 344068
  6.5 3.1 %copy-start.1 = (bf16[128,896]{1,0:T(8,128)(2,1)S(1)}, bf16[128,896]{1,0:T(8,128)(2,1)}, u32[]{:S(2)}) copy-start(bf16[128,896]{1,0:T(8,128)(2,1)} %param.9) | copy-start | bytes 688132
  6.5 3.3 %copy-start.2 = (bf16[128,896]{1,0:T(8,128)(2,1)S(1)}, bf16[128,896]{1,0:T(8,128)(2,1)}, u32[]{:S(2)}) copy-start(bf16[128,896]{1,0:T(8,128)(2,1)} %param.8) | copy-start | bytes 688132
  6.5 98.3 %all-gather.4.cloned.1.call-start = ((), (), s32[]{:S(2)}) async-start(), calls=%async_computation.7 | async-start | bytes 17694720 | tf_op jit(solution)/shard_map/all_gather | solution.py:241
  6.6 67.6 %copy-start.3 = (bf16[256,64]{0,1:T(8,128)(2,1)S(1)}, bf16[256,64]{0,1:T(8,128)(2,1)}, u32[]{:S(2)}) copy-start(bf16[256,64]{0,1:T(8,128)(2,1)} %param.12) | copy-start | bytes 98308
  9.6 74.8 %copy-start.4 = (bf16[32,256]{1,0:T(8,128)(2,1)S(1)}, bf16[32,256]{1,0:T(8,128)(2,1)}, u32[]{:S(2)}) copy-start(bf16[32,256]{1,0:T(8,128)(2,1)} %param.13) | copy-start | bytes 49156
  21.5 12.2 %collective-permute-start = (bf16[4,448,128]{2,1,0:T(8,128)(2,1)S(1)}, bf16[4,448,128]{2,1,0:T(8,128)(2,1)S(1)}, u32[]{:S(2)}, u32[]{:S(2)}) collective-permute-start(bf16[4,448,128]{2,1,0:T(8,128)(2,1)S(1)} %all_to_all.35.refs_0_), channel_id=1, source_target_pairs={{0,64},{64,128},{128,192},{192,256},{256,320},{320,384},{384,448},... | collective-permute-start | bytes 1376264 | tf_op jit(solution)/shard_map/ppermute | solution.py:189
  26.0 11.8 %collective-permute-start.2 = (bf16[4,448,128]{2,1,0:T(8,128)(2,1)S(1)}, bf16[4,448,128]{2,1,0:T(8,128)(2,1)S(1)}, u32[]{:S(2)}, u32[]{:S(2)}) collective-permute-start(bf16[4,448,128]{2,1,0:T(8,128)(2,1)S(1)} %all_to_all.35.refs_0_), channel_id=1, source_target_pairs={{64,0},{128,64},{192,128},{256,192},{320,256},{384,320},{448,384},... | collective-permute-start | bytes 1376264 | tf_op jit(solution)/shard_map/ppermute | solution.py:190
  33.6 5.5 %collective-permute-start.1 = (bf16[4,448,128]{2,1,0:T(8,128)(2,1)S(1)}, bf16[4,448,128]{2,1,0:T(8,128)(2,1)S(1)}, u32[]{:S(2)}, u32[]{:S(2)}) collective-permute-start(bf16[4,448,128]{2,1,0:T(8,128)(2,1)S(1)} %collective-permute-done.refs_1_), channel_id=1, source_target_pairs={{64,128},{128,192},{192,256},{256,320},{320,384},{384,448},{65,129... | collective-permute-start | bytes 1376264 | tf_op jit(solution)/shard_map/ppermute | solution.py:189
  37.8 11.2 %collective-permute-start.4 = (bf16[4,448,128]{2,1,0:T(8,128)(2,1)S(1)}, bf16[4,448,128]{2,1,0:T(8,128)(2,1)S(1)}, u32[]{:S(2)}, u32[]{:S(2)}) collective-permute-start(bf16[4,448,128]{2,1,0:T(8,128)(2,1)S(1)} %collective-permute-done.2.refs_8_), channel_id=1, source_target_pairs={{64,0},{128,64},{192,128},{256,192},{320,256},{384,320},{65,1},{12... | collective-permute-start | bytes 1376264 | tf_op jit(solution)/shard_map/ppermute | solution.py:190
  39.1 11.2 %collective-permute-start.3 = (bf16[4,448,128]{2,1,0:T(8,128)(2,1)S(1)}, bf16[4,448,128]{2,1,0:T(8,128)(2,1)S(1)}, u32[]{:S(2)}, u32[]{:S(2)}) collective-permute-start(bf16[4,448,128]{2,1,0:T(8,128)(2,1)S(1)} %collective-permute-done.1.refs_2_), channel_id=1, source_target_pairs={{128,192},{192,256},{256,320},{320,384},{384,448},{129,193},{193,2... | collective-permute-start | bytes 1376264 | tf_op jit(solution)/shard_map/ppermute | solution.py:189
  49.0 12.7 %collective-permute-start.6 = (bf16[4,448,128]{2,1,0:T(8,128)(2,1)S(1)}, bf16[4,448,128]{2,1,0:T(8,128)(2,1)S(1)}, u32[]{:S(2)}, u32[]{:S(2)}) collective-permute-start(bf16[4,448,128]{2,1,0:T(8,128)(2,1)S(1)} %collective-permute-done.4.refs_9_), channel_id=1, source_target_pairs={{64,0},{128,64},{192,128},{256,192},{320,256},{65,1},{129,65},{193... | collective-permute-start | bytes 1376264 | tf_op jit(solution)/shard_map/ppermute | solution.py:190
  50.3 12.7 %collective-permute-start.5 = (bf16[4,448,128]{2,1,0:T(8,128)(2,1)S(1)}, bf16[4,448,128]{2,1,0:T(8,128)(2,1)}, u32[]{:S(2)}, u32[]{:S(2)}) collective-permute-start(bf16[4,448,128]{2,1,0:T(8,128)(2,1)S(1)} %collective-permute-done.3.refs_3_), channel_id=1, source_target_pairs={{192,256},{256,320},{320,384},{384,448},{193,257},{257,321},{321,3... | collective-permute-start | bytes 1376264 | tf_op jit(solution)/shard_map/ppermute | solution.py:189
  61.7 10.2 %collective-permute-start.8 = (bf16[4,448,128]{2,1,0:T(8,128)(2,1)S(1)}, bf16[4,448,128]{2,1,0:T(8,128)(2,1)}, u32[]{:S(2)}, u32[]{:S(2)}) collective-permute-start(bf16[4,448,128]{2,1,0:T(8,128)(2,1)S(1)} %collective-permute-done.6.refs_10_), channel_id=1, source_target_pairs={{64,0},{128,64},{192,128},{256,192},{65,1},{129,65},{193,129},{257... | collective-permute-start | bytes 1376264 | tf_op jit(solution)/shard_map/ppermute | solution.py:190
  63.0 26.7 %collective-permute-start.7 = (bf16[4,448,128]{2,1,0:T(8,128)(2,1)}, bf16[4,448,128]{2,1,0:T(8,128)(2,1)}, u32[]{:S(2)}, u32[]{:S(2)}) collective-permute-start(bf16[4,448,128]{2,1,0:T(8,128)(2,1)} %collective-permute-done.5.refs_4_), channel_id=1, source_target_pairs={{256,320},{320,384},{384,448},{257,321},{321,385},{385,449},{258,3... | collective-permute-start | bytes 1376264 | tf_op jit(solution)/shard_map/ppermute | solution.py:189
  71.9 19.3 %collective-permute-start.10 = (bf16[4,448,128]{2,1,0:T(8,128)(2,1)}, bf16[4,448,128]{2,1,0:T(8,128)(2,1)}, u32[]{:S(2)}, u32[]{:S(2)}) collective-permute-start(bf16[4,448,128]{2,1,0:T(8,128)(2,1)} %collective-permute-done.8.refs_11_), channel_id=1, source_target_pairs={{64,0},{128,64},{192,128},{65,1},{129,65},{193,129},{66,2},{130,66... | collective-permute-start | bytes 1376264 | tf_op jit(solution)/shard_map/ppermute | solution.py:190
  75.0 14.7 %all-to-all-start.1 = ((f32[8,8,512]{2,1,0:T(8,128)}), f32[8,8,512]{2,1,0:T(8,128)S(1)}, u32[]{:S(2)}, u32[]{:S(2)}) async-start(f32[8,8,512]{2,1,0:T(8,128)} %convolution_bitcast_fusion), calls=%async_computation.1 | async-start | bytes 262144 | tf_op jit(solution)/shard_map/all_to_all | solution.py:253
  89.7 15.1 %collective-permute-start.9 = (bf16[4,448,128]{2,1,0:T(8,128)(2,1)}, bf16[4,448,128]{2,1,0:T(8,128)(2,1)}, u32[]{:S(2)}, u32[]{:S(2)}) collective-permute-start(bf16[4,448,128]{2,1,0:T(8,128)(2,1)} %collective-permute-done.7.refs_5_), channel_id=1, source_target_pairs={{320,384},{384,448},{321,385},{385,449},{322,386},{386,450},{323,3... | collective-permute-start | bytes 1376264 | tf_op jit(solution)/shard_map/ppermute | solution.py:189
  91.2 15.3 %collective-permute-start.12 = (bf16[4,448,128]{2,1,0:T(8,128)(2,1)}, bf16[4,448,128]{2,1,0:T(8,128)(2,1)}, u32[]{:S(2)}, u32[]{:S(2)}) collective-permute-start(bf16[4,448,128]{2,1,0:T(8,128)(2,1)} %collective-permute-done.10.refs_12_), channel_id=1, source_target_pairs={{64,0},{128,64},{65,1},{129,65},{66,2},{130,66},{67,3},{131,67},{6... | collective-permute-start | bytes 1376264 | tf_op jit(solution)/shard_map/ppermute | solution.py:190
  104.9 10.5 %collective-permute-start.11 = (bf16[4,448,128]{2,1,0:T(8,128)(2,1)}, bf16[4,448,128]{2,1,0:T(8,128)(2,1)}, u32[]{:S(2)}, u32[]{:S(2)}) collective-permute-start(bf16[4,448,128]{2,1,0:T(8,128)(2,1)} %collective-permute-done.9.refs_6_), channel_id=1, source_target_pairs={{384,448},{385,449},{386,450},{387,451},{388,452},{389,453},{390,4... | collective-permute-start | bytes 1376264 | tf_op jit(solution)/shard_map/ppermute | solution.py:189
  106.5 23.7 %collective-permute-start.13 = (bf16[4,448,128]{2,1,0:T(8,128)(2,1)}, bf16[4,448,128]{2,1,0:T(8,128)(2,1)}, u32[]{:S(2)}, u32[]{:S(2)}) collective-permute-start(bf16[4,448,128]{2,1,0:T(8,128)(2,1)} %collective-permute-done.12.refs_13_), channel_id=1, source_target_pairs={{64,0},{65,1},{66,2},{67,3},{68,4},{69,5},{70,6},{71,7},{72,8},{73... | collective-permute-start | bytes 1376264 | tf_op jit(solution)/shard_map/ppermute | solution.py:190
  108.8 36.1 %all-to-all-start.3 = ((f32[32,8,512]{2,1,0:T(8,128)}), f32[32,8,512]{2,1,0:T(8,128)}, u32[]{:S(2)}, u32[]{:S(2)}) async-start(f32[32,8,512]{2,1,0:T(8,128)} %broadcast_in_dim.31), calls=%async_computation.3 | async-start | bytes 1048576 | tf_op jit(solution)/shard_map/all_to_all | solution.py:88
  144.9 17.6 %all-to-all-start.2 = ((f32[32,2,2048]{2,1,0:T(2,128)}), f32[32,2,2048]{2,1,0:T(2,128)S(1)}, u32[]{:S(2)}, u32[]{:S(2)}) async-start(f32[32,2,2048]{2,1,0:T(2,128)} %layer.1), calls=%async_computation.2 | async-start | bytes 1048576 | tf_op jit(solution)/shard_map/all_to_all | solution.py:266
  173.6 15.4 %all-to-all-start.4 = ((f32[16,12,128]{2,1,0:T(8,128)}), f32[16,12,128]{2,1,0:T(8,128)S(1)}, u32[]{:S(2)}, u32[]{:S(2)}) async-start(f32[16,12,128]{2,1,0:T(8,128)} %broadcast_in_dim.32), calls=%async_computation.4 | async-start | bytes 262144 | tf_op jit(solution)/shard_map/all_to_all | solution.py:88
Sparse Core Ops, SparseCore 0:
  9.8 93.9 all-gather.3

commit v5 on v4

--- a/solution.py
+++ b/solution.py
@@ -189,9 +189,11 @@
         self.ups.append(lax.ppermute(up, "zl", [(z, z + 1) for z in range(s - 1, ZL - 1)]))
         self.downs.append(lax.ppermute(down, "zl", [(z, z - 1) for z in range(1, ZL + 1 - s)]))
 
-    def after(self, *values):
-        self.ups[-1] = tie(self.ups[-1], *values)
-        self.downs[-1] = tie(self.downs[-1], *values)
+    def join(self, value):
+        self.ups[-1], self.downs[-1], value = lax.optimization_barrier(
+            (self.ups[-1], self.downs[-1], value)
+        )
+        return value
 
     def blocks(self):
         return self.ups + self.downs[1:]
@@ -226,10 +228,24 @@
     return out, got[:, 2 * count :].reshape(ZH, rows, cols)
 
 
-def share_queries(queries):
-    _, rows, cols = queries.shape
-    got = share(queries, ("x", "c"), X * C).reshape(X, C, ZH, rows, cols)
-    return got.transpose(3, 0, 2, 1, 4).reshape(rows, -1)
+def share_plane(out, queries):
+    high = lax.reduce_precision(out, 8, 7)
+    sent = jnp.concatenate(
+        [v.astype(jnp.bfloat16) for v in (high, out - high)]
+        + [queries.reshape(-1, out.shape[1])]
+    )
+    return lax.all_gather(sent, PLANE)
+
+
+def unpack_plane(got, count, rows, cols):
+    lanes = got.shape[2]
+    parts = got[:, : 2 * count].astype(jnp.float32)
+    out = (parts[:, :count] + parts[:, count:]).reshape(Y, X * C * count, lanes)
+    here = got.reshape((Y, X * C) + got.shape[1:])
+    here = lax.dynamic_index_in_dim(here, lax.axis_index("y"), 0, keepdims=False)
+    queries = here[:, 2 * count :].reshape(X, C, ZH, rows, cols)
+    queries = queries.transpose(3, 0, 2, 1, 4).reshape(rows, -1)
+    return out.transpose(1, 0, 2).reshape(X * C * count, Y * lanes), queries
 
 
 def shards(tokens, gate_weight, up_weight, out_grad, in_factor, out_factor, queries):
@@ -248,22 +264,22 @@
     out = out_partial(out_grad, out_factor).reshape(X * C, rank // (X * C), -1)
     for s in range(1, ZL):
         chain.step()
-        if s == 1:
-            out = tie(out, chain.ups[-1])
+        if s == 2:
             out = lax.all_to_all(out, ("x", "c"), 0, 0, tiled=True).sum(0)
-        if s == 5:
-            chain.after(out)
-            out = tie(out, chain.ups[-1])
-            out, query_rows = exchange_z(out, queries)
+        if s == 4:
+            out = exchange_z(out, queries)
+        if s < 5:
+            out = chain.join(out)
         if s == 6:
-            chain.after(out, plane_tokens)
-            out = tie(out, chain.ups[-1])
-            out = share(out, PLANE, Y * X * C)
-    out = out.reshape(Y, rank, -1).transpose(1, 0, 2).reshape(rank, -1)
+            plane_tokens = chain.join(plane_tokens)
+    out, query_rows = out
+    shared = share_plane(out, query_rows)
 
     place = jnp.stack([z]).astype(jnp.int32)
     in_part = layer(place, factor, chain.blocks(), plane_tokens)
     in_proj = lax.all_to_all(in_part, PLANE, 0, 0, tiled=True)
+    in_proj, shared = lax.optimization_barrier((in_proj, shared))
+    out, query_rows = unpack_plane(shared, rank // (X * C), *queries.shape)
     in_proj = in_proj.sum(0)
 
     seqs = Y * rows // LEN
@@ -273,10 +289,7 @@
     spread = jnp.where(mask[:, None, :], in_proj[None], 0.0).reshape(2 * seqs, -1)
     fragment = jnp.dot(spread, out.T, precision=HIGHEST) / jnp.sqrt(jnp.float32(LEN))
     fragment = fragment.reshape(seqs, 2 * rank)
-    fragment, query_rows = lax.optimization_barrier((fragment, query_rows))
     columns = share(fragment, ("zh", "zl"), ZH * ZL)
-    query_rows = share_queries(query_rows)
-    columns, query_rows = lax.optimization_barrier((columns, query_rows))
     columns = columns.reshape(ZH, ZL * seqs, 2 * rank).sum(0).astype(jnp.bfloat16)
     features = share(columns, PLANE, Y * X * C)
     return solve(features, query_rows)

time: 227 us -> 235 us (1.035)
  waiting for transfers between devices: 78.6 us -> 91.8 us
  starting transfers between devices: 46.1 us -> 36.3 us
  local copies, waits for them, and re-layouts: 7.94 us -> 12.7 us
    ppermute x7, waiting for transfers between devices: 45 us -> 61.6 us  [step(): lax.ppermute(down, 'zl', [(z, z - 1) for z in range(1, ZL + 1 - s)])]
    all_to_all x2 -> x1, blocking collectives: 30.2 us -> 17.1 us  [share(): lax.all_to_all(jnp.broadcast_to(x[None], (count,) + x.shape), axes, 0, 0,...]
    all_to_all x0 -> x1, blocking collectives: none -> 12.6 us  [shards(): out = lax.all_to_all(out, ('x', 'c'), 0, 0, tiled=True).sum(0)]
    all_to_all x1 -> x0, starting transfers between devices: 9.38 us -> none  [shards(): out = lax.all_to_all(out, ('x', 'c'), 0, 0, tiled=True).sum(0)]
    unnamed x10 -> x24, local copies, waits for them, and re-layouts: 0.02 us -> 6.25 us
    all_to_all x1 -> x0, waiting for transfers between devices: 5.3 us -> none  [shards(): out = lax.all_to_all(out, ('x', 'c'), 0, 0, tiled=True).sum(0)]
    all_to_all x1, starting transfers between devices: 5.89 us -> 8.97 us  [shards(): in_proj = lax.all_to_all(in_part, PLANE, 0, 0, tiled=True)]
    all_to_all x2 -> x1, starting transfers between devices: 10.2 us -> 8.17 us  [share(): lax.all_to_all(jnp.broadcast_to(x[None], (count,) + x.shape), axes, 0, 0,...]
  transfers between devices with their start and end apart: 19 -> 18, of which waited for: 10 -> 11; matrix products, arithmetic and copies ran while one was open for 2% -> 1% of each run, Pallas kernels for 7% -> 6%
where the time goes in v5:
time: 235 us; the launch traced here: 234 us
  waiting for transfers between devices  91.8 us (39%)
  blocking collectives  53.4 us (23%)
  starting transfers between devices  36.3 us (15%)
  Pallas kernels  23.2 us (10%)
  between operations  13.8 us (6%)
  local copies, waits for them, and re-layouts  12.7 us (5%)
    ppermute x7, waiting for transfers between devices, step(): lax.ppermute(down, 'zl', [(z, z - 1) for z in range(1, ZL + 1 - s)])  61.6 us
    all_to_all x1, blocking collectives, share(): lax.all_to_all(jnp.broadcast_to(x[None], (count,) + x.shape), axes, 0, 0,...  17.1 us
    pallas_call x1, Pallas kernels, layer(): pl.pallas_call(layer_kernel, out_shape=jax.ShapeDtypeStruct((rank // 2, 2...  14.4 us
    all_to_all x1, blocking collectives, shards(): out = lax.all_to_all(out, ('x', 'c'), 0, 0, tiled=True).sum(0)  12.6 us
    all_to_all x1, waiting for transfers between devices, share(): lax.all_to_all(jnp.broadcast_to(x[None], (count,) + x.shape), axes, 0, 0,...  12.6 us
    all_gather x1, blocking collectives, exchange_z(): got = lax.all_gather(sent, 'zh')  12.3 us
    all_to_all x1, blocking collectives, shards(): chain = Chain(lax.all_to_all(quarters, 'y', 0, 0, tiled=True))  11.4 us
    ppermute x7, starting transfers between devices, step(): lax.ppermute(up, 'zl', [(z, z + 1) for z in range(s - 1, ZL - 1)])  10.2 us
  transfers between devices with their start and end apart: 18, of which 11 were waited for; matrix products, arithmetic and copies ran while one was open for 1% of the time, Pallas kernels for 6%

profile of v5, /device:TPU:1, one launch (start us, length us, event | category | flops | bytes accessed | tf_op | source)
XLA Modules:
  0.0 234.3 jit_solution(10056776342476539280)
XLA Ops:
  6.5 3.1 %constant_dynamic-slice_fusion = bf16[240,4096]{1,0:T(8,128)(2,1)} fusion(bf16[480,4096]{1,0:T(8,128)(2,1)} %param.7, s32[]{:T(128)S(6)} %select_n.55), kind=kLoop, calls=%fused_computation.37 | loop fusion | bytes 3932164 | tf_op jit(solution)/shard_map/dynamic_slice | solution.py:256
  9.6 0.0 all-gather.6.cloned.1.call-update
  9.6 0.0 copy-start.10
  9.6 0.0 all-gather.8.cloned.1.call-start
  9.7 0.8 copy-done.8
  10.5 0.2 copy.14
  10.7 0.2 copy.13
  10.9 11.4 %all_to_all.25.refs_0_ = bf16[4,448,128]{2,1,0:T(8,128)(2,1)S(1)} all-to-all(bf16[4,448,128]{2,1,0:T(8,128)(2,1)S(1)} %pad_maximum_fusion), channel_id=1, replica_groups=mesh['zl'=8,'y'=4,'x'=4,'zh'=2,'c'=2] {'y'}, dimensions={0} | all-to-all | bytes 917504 | tf_op jit(solution)/shard_map/all_to_all | solution.py:263
  22.3 4.5 %collective-permute-start = (bf16[4,448,128]{2,1,0:T(8,128)(2,1)S(1)}, bf16[4,448,128]{2,1,0:T(8,128)(2,1)S(1)}, u32[]{:S(2)}, u32[]{:S(2)}) collective-permute-start(bf16[4,448,128]{2,1,0:T(8,128)(2,1)S(1)} %all_to_all.25.refs_0_), channel_id=1, source_target_pairs={{0,64},{64,128},{128,192},{192,256},{256,320},{320,384},{384,448},... | collective-permute-start | bytes 1376264 | tf_op jit(solution)/shard_map/ppermute | solution.py:189
  26.9 1.3 collective-permute-start.1
  28.2 0.2 convolution_bitcast_fusion
  28.4 6.1 %collective-permute-done.refs_1_ = bf16[4,448,128]{2,1,0:T(8,128)(2,1)S(1)} collective-permute-done((bf16[4,448,128]{2,1,0:T(8,128)(2,1)S(1)}, bf16[4,448,128]{2,1,0:T(8,128)(2,1)S(1)}, u32[]{:S(2)}, u32[]{:S(2)}) %collective-permute-start) | collective-permute-done | bytes 458784 | tf_op jit(solution)/shard_map/ppermute | solution.py:189
  34.5 4.2 %collective-permute-done.1.refs_8_ = bf16[4,448,128]{2,1,0:T(8,128)(2,1)S(1)} collective-permute-done((bf16[4,448,128]{2,1,0:T(8,128)(2,1)S(1)}, bf16[4,448,128]{2,1,0:T(8,128)(2,1)S(1)}, u32[]{:S(2)}, u32[]{:S(2)}) %collective-permute-start.1) | collective-permute-done | bytes 458784 | tf_op jit(solution)/shard_map/ppermute | solution.py:190
  38.7 0.7 collective-permute-start.2
  39.4 1.3 collective-permute-start.3
  40.7 12.6 %all_to_all.26 = f32[8,8,512]{2,1,0:T(8,128)S(1)} all-to-all(f32[8,8,512]{2,1,0:T(8,128)S(1)} %convolution_bitcast_fusion), channel_id=1, replica_groups=mesh['zl'=8,'y'=4,'x'=4,'zh'=2,'c'=2] {'x','c'}, dimensions={0} | all-to-all | bytes 262144 | tf_op jit(solution)/shard_map/all_to_all | solution.py:268
  53.3 0.0 collective-permute-done.2.refs_2_
  53.3 1.6 collective-permute-done.3.refs_9_
  54.9 0.7 collective-permute-start.4
  55.6 1.3 collective-permute-start.5
  56.9 15.5 %collective-permute-done.5.refs_10_ = bf16[4,448,128]{2,1,0:T(8,128)(2,1)S(1)} collective-permute-done((bf16[4,448,128]{2,1,0:T(8,128)(2,1)S(1)}, bf16[4,448,128]{2,1,0:T(8,128)(2,1)S(1)}, u32[]{:S(2)}, u32[]{:S(2)}) %collective-permute-start.5) | collective-permute-done | bytes 458784 | tf_op jit(solution)/shard_map/ppermute | solution.py:190
  72.4 1.5 collective-permute-start.6
  73.9 1.3 collective-permute-start.7
  75.2 12.3 %all-gather = bf16[64,512]{1,0:T(8,128)(2,1)S(1)} all-gather(bf16[32,512]{1,0:T(8,128)(2,1)S(1)} %pad_maximum_fusion.2), channel_id=2, replica_groups=mesh['zl'=8,'y'=4,'x'=4,'zh'=2,'c'=2] {'zh'}, dimensions={0}, use_global_device_ids=true | all-gather | bytes 98304 | tf_op jit(solution)/shard_map/all_gather | solution.py:224
  87.6 3.0 %collective-permute-done.7.refs_11_ = bf16[4,448,128]{2,1,0:T(8,128)(2,1)} collective-permute-done((bf16[4,448,128]{2,1,0:T(8,128)(2,1)S(1)}, bf16[4,448,128]{2,1,0:T(8,128)(2,1)}, u32[]{:S(2)}, u32[]{:S(2)}) %collective-permute-start.7) | collective-permute-done | bytes 458784 | tf_op jit(solution)/shard_map/ppermute | solution.py:190
  90.6 0.6 pad_maximum_fusion.1
  91.2 0.0 all-gather.8.cloned.1.call-update
  91.2 0.7 collective-permute-start.8
  91.9 1.3 collective-permute-start.10
  93.3 0.7 collective-permute-start.9
  94.0 0.8 copy-done.1
  94.7 18.1 %collective-permute-done.10.refs_12_ = bf16[4,448,128]{2,1,0:T(8,128)(2,1)S(1)} collective-permute-done((bf16[4,448,128]{2,1,0:T(8,128)(2,1)}, bf16[4,448,128]{2,1,0:T(8,128)(2,1)S(1)}, u32[]{:S(2)}, u32[]{:S(2)}) %collective-permute-start.10) | collective-permute-done | bytes 458784 | tf_op jit(solution)/shard_map/ppermute | solution.py:190
  112.8 1.3 collective-permute-start.11
  114.1 0.8 copy-done.3
  114.9 0.8 copy-done.5
  115.7 7.9 %collective-permute-done.11.refs_13_ = bf16[4,448,128]{2,1,0:T(8,128)(2,1)} collective-permute-done((bf16[4,448,128]{2,1,0:T(8,128)(2,1)S(1)}, bf16[4,448,128]{2,1,0:T(8,128)(2,1)}, u32[]{:S(2)}, u32[]{:S(2)}) %collective-permute-start.11) | collective-permute-done | bytes 458784 | tf_op jit(solution)/shard_map/ppermute | solution.py:190
  123.6 1.4 collective-permute-start.12
  125.0 1.3 collective-permute-start.13
  126.3 0.1 dynamic-slice_bitcast_fusion.1
  126.4 0.0 collective-permute-done.12.refs_7_
  126.4 11.4 %collective-permute-done.13.refs_14_ = bf16[4,448,128]{2,1,0:T(8,128)(2,1)} collective-permute-done((bf16[4,448,128]{2,1,0:T(8,128)(2,1)}, bf16[4,448,128]{2,1,0:T(8,128)(2,1)}, u32[]{:S(2)}, u32[]{:S(2)}) %collective-permute-start.13) | collective-permute-done | bytes 458784 | tf_op jit(solution)/shard_map/ppermute | solution.py:190
  137.8 1.0 copy-done.2
  138.8 1.0 copy-done.4
  139.8 1.0 copy-done.6
  140.8 14.4 %layer.1 = f32[32,2,2048]{2,1,0:T(2,128)} custom-call(s32[1]{0:T(128)} %bitcast.place_ref, bf16[64,256]{1,0:T(8,128)(2,1)S(1)} %pad.8.factor_ref, bf16[4,448,128]{2,1,0:T(8,128)(2,1)S(1)} %all_to_all.25.refs_0_, bf16[4,448,128]{2,1,0:T(8,128)(2,1)S(1)} %collective-permute-done.refs_1_, bf16[4,448,128]{2,1,0:T(8,128)(2,1)S(1)} %collective-permute-done.2.refs_2_, ...), custom_call_target="tpu_custom_call" | custom-call | flops 7046430720 | bytes 19398656 | tf_op jit(solution)/shard_map/layer/pallas_call | solution.py:154
  155.2 9.0 %all-to-all-start.2 = ((f32[32,2,2048]{2,1,0:T(2,128)}), f32[32,2,2048]{2,1,0:T(2,128)S(1)}, u32[]{:S(2)}, u32[]{:S(2)}) async-start(f32[32,2,2048]{2,1,0:T(2,128)} %layer.1), calls=%async_computation.2 | async-start | bytes 1048576 | tf_op jit(solution)/shard_map/all_to_all | solution.py:280
  164.3 1.9 all-gather.8.cloned.1.call-done
  166.2 9.6 %all-to-all-done.2 = f32[32,2,2048]{2,1,0:T(2,128)S(1)} async-done(((f32[32,2,2048]{2,1,0:T(2,128)}), f32[32,2,2048]{2,1,0:T(2,128)S(1)}, u32[]{:S(2)}, u32[]{:S(2)}) %all-to-all-start.2) | async-done | bytes 524320 | tf_op jit(solution)/shard_map/all_to_all | solution.py:280
  175.8 0.2 reduce_sum.38
  175.9 0.1 broadcast_select_fusion
  176.1 0.1 select_n.57
  176.2 1.2 slice_convert_fusion
  177.4 0.1 slice_add_fusion
  177.5 0.5 convolution_multiply_fusion
  178.0 0.1 broadcast_in_dim.40
  178.1 17.1 %all_to_all.27 = f32[16,12,128]{2,1,0:T(8,128)S(1)} all-to-all(f32[16,12,128]{2,1,0:T(8,128)S(1)} %broadcast_in_dim.41), channel_id=1, replica_groups=mesh['zl'=8,'y'=4,'x'=4,'zh'=2,'c'=2] {'zh','zl'}, dimensions={0} | all-to-all | bytes 196608 | tf_op jit(solution)/shard_map/all_to_all | solution.py:88
  195.3 1.0 broadcast_in_dim.42
  196.3 8.2 %all-to-all-start.4 = ((bf16[32,96,128]{2,1,0:T(8,128)(2,1)}), bf16[32,96,128]{2,1,0:T(8,128)(2,1)S(1)}, u32[]{:S(2)}, u32[]{:S(2)}) async-start(bf16[32,96,128]{2,1,0:T(8,128)(2,1)} %broadcast_in_dim.42), calls=%async_computation.4 | async-start | bytes 1572864 | tf_op jit(solution)/shard_map/all_to_all | solution.py:88
  204.5 1.0 dynamic-slice_bitcast_fusion
  205.5 0.1 reshape.119
  205.6 0.3 copy.16
  205.9 0.2 reshape.120.queries_ref
  206.1 12.6 %all-to-all-done.4.features_ref = bf16[32,96,128]{2,1,0:T(8,128)(2,1)S(1)} async-done(((bf16[32,96,128]{2,1,0:T(8,128)(2,1)}), bf16[32,96,128]{2,1,0:T(8,128)(2,1)S(1)}, u32[]{:S(2)}, u32[]{:S(2)}) %all-to-all-start.4) | async-done | bytes 786464 | tf_op jit(solution)/shard_map/all_to_all | solution.py:88
  218.7 8.8 %solve.1 = f32[32,96]{1,0:T(8,128)} custom-call(bf16[32,96,128]{2,1,0:T(8,128)(2,1)S(1)} %all-to-all-done.4.features_ref, bf16[32,4096]{1,0:T(8,128)(2,1)S(1)} %reshape.120.queries_ref), custom_call_target="tpu_custom_call" | custom-call | tf_op jit(solution)/shard_map/solve/pallas_call | solution.py:79
  (41 shorter events, 0.3 us)
Async XLA Ops:
  6.5 119.8 %copy-start = (bf16[896,64]{0,1:T(8,128)(2,1)S(1)}, bf16[896,64]{0,1:T(8,128)(2,1)}, u32[]{:S(2)}) copy-start(bf16[896,64]{0,1:T(8,128)(2,1)} %param.11) | copy-start | bytes 344068
  6.5 117.0 %all-gather.6.cloned.1.call-start = ((), (), s32[]{:S(2)}) async-start(), calls=%async_computation.5 | async-start | bytes 17694720 | tf_op jit(solution)/shard_map/all_gather | solution.py:257
  9.6 0.9 copy-start.8
  9.6 1.1 copy-start.9
  9.6 18.6 %copy-start.7 = (bf16[480,256]{1,0:T(8,128)(2,1)S(1)}, bf16[480,256]{1,0:T(8,128)(2,1)}, u32[]{:S(2)}) copy-start(bf16[480,256]{1,0:T(8,128)(2,1)} %param.10) | copy-start | bytes 737284
  9.6 18.6 %copy-start.10 = (bf16[256,64]{0,1:T(8,128)(2,1)S(1)}, bf16[256,64]{0,1:T(8,128)(2,1)}, u32[]{:S(2)}) copy-start(bf16[256,64]{0,1:T(8,128)(2,1)} %param.12) | copy-start | bytes 98308
  9.6 156.5 %all-gather.8.cloned.1.call-start = ((), (), s32[]{:S(2)}) async-start(), calls=%async_computation.6 | async-start | bytes 1622016 | tf_op jit(solution)/shard_map/all_gather | solution.py:237
  10.5 46.4 %copy-start.11 = (bf16[32,256]{1,0:T(8,128)(2,1)S(1)}, bf16[32,256]{1,0:T(8,128)(2,1)}, u32[]{:S(2)}) copy-start(bf16[32,256]{1,0:T(8,128)(2,1)} %param.13) | copy-start | bytes 49156
  22.3 12.2 %collective-permute-start = (bf16[4,448,128]{2,1,0:T(8,128)(2,1)S(1)}, bf16[4,448,128]{2,1,0:T(8,128)(2,1)S(1)}, u32[]{:S(2)}, u32[]{:S(2)}) collective-permute-start(bf16[4,448,128]{2,1,0:T(8,128)(2,1)S(1)} %all_to_all.25.refs_0_), channel_id=1, source_target_pairs={{0,64},{64,128},{128,192},{192,256},{256,320},{320,384},{384,448},... | collective-permute-start | bytes 1376264 | tf_op jit(solution)/shard_map/ppermute | solution.py:189
  26.9 11.8 %collective-permute-start.1 = (bf16[4,448,128]{2,1,0:T(8,128)(2,1)S(1)}, bf16[4,448,128]{2,1,0:T(8,128)(2,1)S(1)}, u32[]{:S(2)}, u32[]{:S(2)}) collective-permute-start(bf16[4,448,128]{2,1,0:T(8,128)(2,1)S(1)} %all_to_all.25.refs_0_), channel_id=1, source_target_pairs={{64,0},{128,64},{192,128},{256,192},{320,256},{384,320},{448,384},... | collective-permute-start | bytes 1376264 | tf_op jit(solution)/shard_map/ppermute | solution.py:190
  38.7 14.6 %collective-permute-start.2 = (bf16[4,448,128]{2,1,0:T(8,128)(2,1)S(1)}, bf16[4,448,128]{2,1,0:T(8,128)(2,1)S(1)}, u32[]{:S(2)}, u32[]{:S(2)}) collective-permute-start(bf16[4,448,128]{2,1,0:T(8,128)(2,1)S(1)} %collective-permute-done.refs_1_), channel_id=1, source_target_pairs={{64,128},{128,192},{192,256},{256,320},{320,384},{384,448},{65,129... | collective-permute-start | bytes 1376264 | tf_op jit(solution)/shard_map/ppermute | solution.py:189
  39.4 15.5 %collective-permute-start.3 = (bf16[4,448,128]{2,1,0:T(8,128)(2,1)S(1)}, bf16[4,448,128]{2,1,0:T(8,128)(2,1)S(1)}, u32[]{:S(2)}, u32[]{:S(2)}) collective-permute-start(bf16[4,448,128]{2,1,0:T(8,128)(2,1)S(1)} %collective-permute-done.1.refs_8_), channel_id=1, source_target_pairs={{64,0},{128,64},{192,128},{256,192},{320,256},{384,320},{65,1},{12... | collective-permute-start | bytes 1376264 | tf_op jit(solution)/shard_map/ppermute | solution.py:190
  54.9 2.0 collective-permute-start.4
  55.6 16.8 %collective-permute-start.5 = (bf16[4,448,128]{2,1,0:T(8,128)(2,1)S(1)}, bf16[4,448,128]{2,1,0:T(8,128)(2,1)S(1)}, u32[]{:S(2)}, u32[]{:S(2)}) collective-permute-start(bf16[4,448,128]{2,1,0:T(8,128)(2,1)S(1)} %collective-permute-done.3.refs_9_), channel_id=1, source_target_pairs={{64,0},{128,64},{192,128},{256,192},{320,256},{65,1},{129,65},{193... | collective-permute-start | bytes 1376264 | tf_op jit(solution)/shard_map/ppermute | solution.py:190
  72.4 15.1 %collective-permute-start.6 = (bf16[4,448,128]{2,1,0:T(8,128)(2,1)S(1)}, bf16[4,448,128]{2,1,0:T(8,128)(2,1)}, u32[]{:S(2)}, u32[]{:S(2)}) collective-permute-start(bf16[4,448,128]{2,1,0:T(8,128)(2,1)S(1)} %collective-permute-done.4.refs_3_), channel_id=1, source_target_pairs={{192,256},{256,320},{320,384},{384,448},{193,257},{257,321},{321,3... | collective-permute-start | bytes 1376264 | tf_op jit(solution)/shard_map/ppermute | solution.py:189
  73.9 16.7 %collective-permute-start.7 = (bf16[4,448,128]{2,1,0:T(8,128)(2,1)S(1)}, bf16[4,448,128]{2,1,0:T(8,128)(2,1)}, u32[]{:S(2)}, u32[]{:S(2)}) collective-permute-start(bf16[4,448,128]{2,1,0:T(8,128)(2,1)S(1)} %collective-permute-done.5.refs_10_), channel_id=1, source_target_pairs={{64,0},{128,64},{192,128},{256,192},{65,1},{129,65},{193,129},{257... | collective-permute-start | bytes 1376264 | tf_op jit(solution)/shard_map/ppermute | solution.py:190
  91.2 2.0 collective-permute-start.8
  91.9 20.9 %collective-permute-start.10 = (bf16[4,448,128]{2,1,0:T(8,128)(2,1)}, bf16[4,448,128]{2,1,0:T(8,128)(2,1)S(1)}, u32[]{:S(2)}, u32[]{:S(2)}) collective-permute-start(bf16[4,448,128]{2,1,0:T(8,128)(2,1)} %collective-permute-done.7.refs_11_), channel_id=1, source_target_pairs={{64,0},{128,64},{192,128},{65,1},{129,65},{193,129},{66,2},{130,66... | collective-permute-start | bytes 1376264 | tf_op jit(solution)/shard_map/ppermute | solution.py:190
  93.3 21.6 %collective-permute-start.9 = (bf16[4,448,128]{2,1,0:T(8,128)(2,1)S(1)}, bf16[4,448,128]{2,1,0:T(8,128)(2,1)S(1)}, u32[]{:S(2)}, u32[]{:S(2)}) collective-permute-start(bf16[4,448,128]{2,1,0:T(8,128)(2,1)S(1)} %collective-permute-done.8.refs_5_), channel_id=1, source_target_pairs={{320,384},{384,448},{321,385},{385,449},{322,386},{386,450},{323,3... | collective-permute-start | bytes 1376264 | tf_op jit(solution)/shard_map/ppermute | solution.py:189
  94.0 0.8 copy-start.1
  112.8 10.8 %collective-permute-start.11 = (bf16[4,448,128]{2,1,0:T(8,128)(2,1)S(1)}, bf16[4,448,128]{2,1,0:T(8,128)(2,1)}, u32[]{:S(2)}, u32[]{:S(2)}) collective-permute-start(bf16[4,448,128]{2,1,0:T(8,128)(2,1)S(1)} %collective-permute-done.10.refs_12_), channel_id=1, source_target_pairs={{64,0},{128,64},{65,1},{129,65},{66,2},{130,66},{67,3},{131,67},{6... | collective-permute-start | bytes 1376264 | tf_op jit(solution)/shard_map/ppermute | solution.py:190
  114.1 0.8 copy-start.3
  114.9 0.8 copy-start.5
  123.6 2.8 %collective-permute-start.12 = (bf16[4,448,128]{2,1,0:T(8,128)(2,1)}, bf16[4,448,128]{2,1,0:T(8,128)(2,1)}, u32[]{:S(2)}, u32[]{:S(2)}) collective-permute-start(bf16[4,448,128]{2,1,0:T(8,128)(2,1)} %copy-done.5), channel_id=1, source_target_pairs={{384,448},{385,449},{386,450},{387,451},{388,452},{389,453},{390,4... | collective-permute-start | bytes 1376264 | tf_op jit(solution)/shard_map/ppermute | solution.py:189
  125.0 12.8 %collective-permute-start.13 = (bf16[4,448,128]{2,1,0:T(8,128)(2,1)}, bf16[4,448,128]{2,1,0:T(8,128)(2,1)}, u32[]{:S(2)}, u32[]{:S(2)}) collective-permute-start(bf16[4,448,128]{2,1,0:T(8,128)(2,1)} %collective-permute-done.11.refs_13_), channel_id=1, source_target_pairs={{64,0},{65,1},{66,2},{67,3},{68,4},{69,5},{70,6},{71,7},{72,8},{73... | collective-permute-start | bytes 1376264 | tf_op jit(solution)/shard_map/ppermute | solution.py:190
  137.8 1.0 copy-start.2
  138.8 1.0 copy-start.4
  139.8 1.0 copy-start.6
  155.2 20.5 %all-to-all-start.2 = ((f32[32,2,2048]{2,1,0:T(2,128)}), f32[32,2,2048]{2,1,0:T(2,128)S(1)}, u32[]{:S(2)}, u32[]{:S(2)}) async-start(f32[32,2,2048]{2,1,0:T(2,128)} %layer.1), calls=%async_computation.2 | async-start | bytes 1048576 | tf_op jit(solution)/shard_map/all_to_all | solution.py:280
  196.3 22.4 %all-to-all-start.4 = ((bf16[32,96,128]{2,1,0:T(8,128)(2,1)}), bf16[32,96,128]{2,1,0:T(8,128)(2,1)S(1)}, u32[]{:S(2)}, u32[]{:S(2)}) async-start(bf16[32,96,128]{2,1,0:T(8,128)(2,1)} %broadcast_in_dim.42), calls=%async_computation.4 | async-start | bytes 1572864 | tf_op jit(solution)/shard_map/all_to_all | solution.py:88
Sparse Core Ops, SparseCore 0:
  9.7 93.9 all-gather.5
  106.9 59.2 all-gather.7

commit v6 on v4

--- a/solution.py
+++ b/solution.py
@@ -226,10 +226,20 @@
     return out, got[:, 2 * count :].reshape(ZH, rows, cols)
 
 
-def share_queries(queries):
-    _, rows, cols = queries.shape
-    got = share(queries, ("x", "c"), X * C).reshape(X, C, ZH, rows, cols)
-    return got.transpose(3, 0, 2, 1, 4).reshape(rows, -1)
+def share_plane(out, queries):
+    high = lax.reduce_precision(out, 8, 7)
+    sent = jnp.concatenate(
+        [v.astype(jnp.bfloat16) for v in (high, out - high)]
+        + [queries.reshape(-1, out.shape[1])]
+    )
+    return lax.all_gather(sent, PLANE)
+
+
+def unpack_queries(got, first, rows, cols):
+    here = got.reshape((Y, X * C) + got.shape[1:])
+    here = lax.dynamic_index_in_dim(here, lax.axis_index("y"), 0, keepdims=False)
+    queries = here[:, first:].reshape(X, C, ZH, rows, cols)
+    return queries.transpose(3, 0, 2, 1, 4).reshape(rows, -1)
 
 
 def shards(tokens, gate_weight, up_weight, out_grad, in_factor, out_factor, queries):
@@ -257,12 +267,14 @@
             out, query_rows = exchange_z(out, queries)
         if s == 6:
             chain.after(out, plane_tokens)
-            out = tie(out, chain.ups[-1])
-            out = share(out, PLANE, Y * X * C)
-    out = out.reshape(Y, rank, -1).transpose(1, 0, 2).reshape(rank, -1)
+    shared = share_plane(out, query_rows)
+    out = tie(out, chain.ups[-1], chain.downs[-1])
+    out = share(out, PLANE, Y * X * C)
 
     place = jnp.stack([z]).astype(jnp.int32)
     in_part = layer(place, factor, chain.blocks(), plane_tokens)
+    in_part, out = lax.optimization_barrier((in_part, out))
+    out = out.reshape(Y, rank, -1).transpose(1, 0, 2).reshape(rank, -1)
     in_proj = lax.all_to_all(in_part, PLANE, 0, 0, tiled=True)
     in_proj = in_proj.sum(0)
 
@@ -273,11 +285,10 @@
     spread = jnp.where(mask[:, None, :], in_proj[None], 0.0).reshape(2 * seqs, -1)
     fragment = jnp.dot(spread, out.T, precision=HIGHEST) / jnp.sqrt(jnp.float32(LEN))
     fragment = fragment.reshape(seqs, 2 * rank)
-    fragment, query_rows = lax.optimization_barrier((fragment, query_rows))
     columns = share(fragment, ("zh", "zl"), ZH * ZL)
-    query_rows = share_queries(query_rows)
-    columns, query_rows = lax.optimization_barrier((columns, query_rows))
+    columns, shared = lax.optimization_barrier((columns, shared))
     columns = columns.reshape(ZH, ZL * seqs, 2 * rank).sum(0).astype(jnp.bfloat16)
+    query_rows = unpack_queries(shared, 2 * rank // (X * C), *queries.shape)
     features = share(columns, PLANE, Y * X * C)
     return solve(features, query_rows)
 

time: 227 us -> 230 us (1.013)
  blocking collectives: 53.9 us -> 23.7 us
  waiting for transfers between devices: 78.6 us -> 99.8 us
  starting transfers between devices: 46.1 us -> 54.6 us
  local copies, waits for them, and re-layouts: 7.94 us -> 10.8 us
    all_to_all x2 -> x0, blocking collectives: 30.2 us -> none  [share(): lax.all_to_all(jnp.broadcast_to(x[None], (count,) + x.shape), axes, 0, 0,...]
    all_to_all x2 -> x3, waiting for transfers between devices: 11.5 us -> 24.6 us  [share(): lax.all_to_all(jnp.broadcast_to(x[None], (count,) + x.shape), axes, 0, 0,...]
    ppermute x7, waiting for transfers between devices: 45 us -> 52.5 us  [step(): lax.ppermute(down, 'zl', [(z, z - 1) for z in range(1, ZL + 1 - s)])]
    all_to_all x2 -> x3, starting transfers between devices: 10.2 us -> 17 us  [share(): lax.all_to_all(jnp.broadcast_to(x[None], (count,) + x.shape), axes, 0, 0,...]
  transfers between devices with their start and end apart: 19 -> 21, of which waited for: 10 -> 10; matrix products, arithmetic and copies ran while one was open for 2% -> 4% of each run, Pallas kernels for 7% -> 6%
where the time goes in v6:
time: 230 us; the launch traced here: 229 us
  waiting for transfers between devices  99.8 us (43%)
  starting transfers between devices  54.6 us (24%)
  blocking collectives  23.7 us (10%)
  Pallas kernels  23.5 us (10%)
  between operations  13.8 us (6%)
  local copies, waits for them, and re-layouts  10.8 us (5%)
    ppermute x7, waiting for transfers between devices, step(): lax.ppermute(down, 'zl', [(z, z - 1) for z in range(1, ZL + 1 - s)])  52.5 us
    all_to_all x3, waiting for transfers between devices, share(): lax.all_to_all(jnp.broadcast_to(x[None], (count,) + x.shape), axes, 0, 0,...  24.6 us
    all_to_all x3, starting transfers between devices, share(): lax.all_to_all(jnp.broadcast_to(x[None], (count,) + x.shape), axes, 0, 0,...  17 us
    pallas_call x1, Pallas kernels, layer(): pl.pallas_call(layer_kernel, out_shape=jax.ShapeDtypeStruct((rank // 2, 2...  14.7 us
    all_gather x1, blocking collectives, exchange_z(): got = lax.all_gather(sent, 'zh')  12.3 us
    ppermute x7, starting transfers between devices, step(): lax.ppermute(up, 'zl', [(z, z + 1) for z in range(s - 1, ZL - 1)])  11.7 us
    all_to_all x1, blocking collectives, shards(): chain = Chain(lax.all_to_all(quarters, 'y', 0, 0, tiled=True))  11.4 us
    all_to_all x1, waiting for transfers between devices, shards(): in_proj = lax.all_to_all(in_part, PLANE, 0, 0, tiled=True)  11 us
  transfers between devices with their start and end apart: 21, of which 10 were waited for; matrix products, arithmetic and copies ran while one was open for 4% of the time, Pallas kernels for 6%

profile of v6, /device:TPU:1, one launch (start us, length us, event | category | flops | bytes accessed | tf_op | source)
XLA Modules:
  0.0 228.7 jit_solution(1663409332529458285)
XLA Ops:
  6.5 3.1 %constant_dynamic-slice_fusion = bf16[240,4096]{1,0:T(8,128)(2,1)} fusion(bf16[480,4096]{1,0:T(8,128)(2,1)} %param.7, s32[]{:T(128)S(6)} %select_n.55), kind=kLoop, calls=%fused_computation.35 | loop fusion | bytes 3932164 | tf_op jit(solution)/shard_map/dynamic_slice | solution.py:250
  9.6 0.0 all-gather.6.cloned.1.call-update
  9.7 0.0 copy-start.3
  9.7 0.9 copy-done.1
  10.6 0.2 copy.14
  10.8 0.2 copy.13
  11.0 11.4 %all_to_all.30.refs_0_ = bf16[4,448,128]{2,1,0:T(8,128)(2,1)S(1)} all-to-all(bf16[4,448,128]{2,1,0:T(8,128)(2,1)S(1)} %pad_maximum_fusion), channel_id=1, replica_groups=mesh['zl'=8,'y'=4,'x'=4,'zh'=2,'c'=2] {'y'}, dimensions={0} | all-to-all | bytes 917504 | tf_op jit(solution)/shard_map/all_to_all | solution.py:257
  22.4 4.5 %collective-permute-start = (bf16[4,448,128]{2,1,0:T(8,128)(2,1)S(1)}, bf16[4,448,128]{2,1,0:T(8,128)(2,1)S(1)}, u32[]{:S(2)}, u32[]{:S(2)}) collective-permute-start(bf16[4,448,128]{2,1,0:T(8,128)(2,1)S(1)} %all_to_all.30.refs_0_), channel_id=1, source_target_pairs={{0,64},{64,128},{128,192},{192,256},{256,320},{320,384},{384,448},... | collective-permute-start | bytes 1376264 | tf_op jit(solution)/shard_map/ppermute | solution.py:189
  26.9 1.3 collective-permute-start.2
  28.2 6.3 %collective-permute-done.refs_1_ = bf16[4,448,128]{2,1,0:T(8,128)(2,1)S(1)} collective-permute-done((bf16[4,448,128]{2,1,0:T(8,128)(2,1)S(1)}, bf16[4,448,128]{2,1,0:T(8,128)(2,1)S(1)}, u32[]{:S(2)}, u32[]{:S(2)}) %collective-permute-start) | collective-permute-done | bytes 458784 | tf_op jit(solution)/shard_map/ppermute | solution.py:189
  34.5 0.7 collective-permute-start.1
  35.2 3.6 %collective-permute-done.2.refs_8_ = bf16[4,448,128]{2,1,0:T(8,128)(2,1)S(1)} collective-permute-done((bf16[4,448,128]{2,1,0:T(8,128)(2,1)S(1)}, bf16[4,448,128]{2,1,0:T(8,128)(2,1)S(1)}, u32[]{:S(2)}, u32[]{:S(2)}) %collective-permute-start.2) | collective-permute-done | bytes 458784 | tf_op jit(solution)/shard_map/ppermute | solution.py:190
  38.8 1.3 collective-permute-start.4
  40.1 0.0 collective-permute-done.1.refs_2_
  40.1 0.7 collective-permute-start.3
  40.8 9.3 %collective-permute-done.4.refs_9_ = bf16[4,448,128]{2,1,0:T(8,128)(2,1)S(1)} collective-permute-done((bf16[4,448,128]{2,1,0:T(8,128)(2,1)S(1)}, bf16[4,448,128]{2,1,0:T(8,128)(2,1)S(1)}, u32[]{:S(2)}, u32[]{:S(2)}) %collective-permute-start.4) | collective-permute-done | bytes 458784 | tf_op jit(solution)/shard_map/ppermute | solution.py:190
  50.1 1.3 collective-permute-start.6
  51.4 1.4 collective-permute-start.5
  52.9 9.7 %collective-permute-done.6.refs_10_ = bf16[4,448,128]{2,1,0:T(8,128)(2,1)S(1)} collective-permute-done((bf16[4,448,128]{2,1,0:T(8,128)(2,1)S(1)}, bf16[4,448,128]{2,1,0:T(8,128)(2,1)S(1)}, u32[]{:S(2)}, u32[]{:S(2)}) %collective-permute-start.6) | collective-permute-done | bytes 458784 | tf_op jit(solution)/shard_map/ppermute | solution.py:190
  62.6 1.3 collective-permute-start.8
  63.9 0.0 collective-permute-done.5.refs_4_
  63.9 1.4 collective-permute-start.7
  65.3 7.4 %collective-permute-done.8.refs_11_ = bf16[4,448,128]{2,1,0:T(8,128)(2,1)} collective-permute-done((bf16[4,448,128]{2,1,0:T(8,128)(2,1)S(1)}, bf16[4,448,128]{2,1,0:T(8,128)(2,1)}, u32[]{:S(2)}, u32[]{:S(2)}) %collective-permute-start.8) | collective-permute-done | bytes 458784 | tf_op jit(solution)/shard_map/ppermute | solution.py:190
  72.8 1.3 collective-permute-start.10
  74.1 1.0 pad.9
  75.0 0.9 convolution_bitcast_fusion
  75.9 9.4 %all-to-all-start.1 = ((f32[8,8,512]{2,1,0:T(8,128)}), f32[8,8,512]{2,1,0:T(8,128)S(1)}, u32[]{:S(2)}, u32[]{:S(2)}) async-start(f32[8,8,512]{2,1,0:T(8,128)} %convolution_bitcast_fusion), calls=%async_computation.1 | async-start | bytes 262144 | tf_op jit(solution)/shard_map/all_to_all | solution.py:263
  85.3 5.3 %all-to-all-done.1 = f32[8,8,512]{2,1,0:T(8,128)S(1)} async-done(((f32[8,8,512]{2,1,0:T(8,128)}), f32[8,8,512]{2,1,0:T(8,128)S(1)}, u32[]{:S(2)}, u32[]{:S(2)}) %all-to-all-start.1) | async-done | bytes 131104 | tf_op jit(solution)/shard_map/all_to_all | solution.py:263
  90.6 1.5 collective-permute-start.9
  92.1 1.3 collective-permute-start.12
  93.4 12.3 %all-gather = bf16[64,512]{1,0:T(8,128)(2,1)S(1)} all-gather(bf16[32,512]{1,0:T(8,128)(2,1)S(1)} %pad_maximum_fusion.2), channel_id=2, replica_groups=mesh['zl'=8,'y'=4,'x'=4,'zh'=2,'c'=2] {'zh'}, dimensions={0}, use_global_device_ids=true | all-gather | bytes 98304 | tf_op jit(solution)/shard_map/all_gather | solution.py:222
  105.7 0.6 pad_maximum_fusion.1
  106.3 0.0 all-gather.8.cloned.1.call-update
  106.4 0.0 collective-permute-done.9.refs_6_
  106.4 0.0 all-gather.6.cloned.1.call-done
  106.4 1.5 collective-permute-start.11
  107.9 1.3 collective-permute-start.13
  109.2 0.1 dynamic-slice_bitcast_fusion.1
  109.3 0.0 collective-permute-done.11.refs_7_
  109.3 22.4 %collective-permute-done.13.refs_14_ = bf16[4,448,128]{2,1,0:T(8,128)(2,1)} collective-permute-done((bf16[4,448,128]{2,1,0:T(8,128)(2,1)}, bf16[4,448,128]{2,1,0:T(8,128)(2,1)}, u32[]{:S(2)}, u32[]{:S(2)}) %collective-permute-start.13) | collective-permute-done | bytes 458784 | tf_op jit(solution)/shard_map/ppermute | solution.py:190
  131.7 0.9 broadcast_in_dim.44
  132.6 6.5 %all-to-all-start.2 = ((f32[32,8,512]{2,1,0:T(8,128)}), f32[32,8,512]{2,1,0:T(8,128)}, u32[]{:S(2)}, u32[]{:S(2)}) async-start(f32[32,8,512]{2,1,0:T(8,128)} %broadcast_in_dim.44), calls=%async_computation.2 | async-start | bytes 1048576 | tf_op jit(solution)/shard_map/all_to_all | solution.py:88
  139.1 14.7 %layer.1 = f32[32,2,2048]{2,1,0:T(2,128)} custom-call(s32[1]{0:T(128)} %bitcast.place_ref, bf16[64,256]{1,0:T(8,128)(2,1)S(1)} %pad.8.factor_ref, bf16[4,448,128]{2,1,0:T(8,128)(2,1)S(1)} %all_to_all.30.refs_0_, bf16[4,448,128]{2,1,0:T(8,128)(2,1)S(1)} %collective-permute-done.refs_1_, bf16[4,448,128]{2,1,0:T(8,128)(2,1)S(1)} %collective-permute-done.1.refs_2_, ...), custom_call_target="tpu_custom_call" | custom-call | flops 7046430720 | bytes 19398656 | tf_op jit(solution)/shard_map/layer/pallas_call | solution.py:154
  153.9 0.0 all-to-all-done.2
  153.9 7.5 %all-to-all-start.3 = ((f32[32,2,2048]{2,1,0:T(2,128)}), f32[32,2,2048]{2,1,0:T(2,128)S(1)}, u32[]{:S(2)}, u32[]{:S(2)}) async-start(f32[32,2,2048]{2,1,0:T(2,128)} %layer.1), calls=%async_computation.3 | async-start | bytes 1048576 | tf_op jit(solution)/shard_map/all_to_all | solution.py:278
  161.4 1.1 copy.17
  162.5 11.0 %all-to-all-done.3 = f32[32,2,2048]{2,1,0:T(2,128)S(1)} async-done(((f32[32,2,2048]{2,1,0:T(2,128)}), f32[32,2,2048]{2,1,0:T(2,128)S(1)}, u32[]{:S(2)}, u32[]{:S(2)}) %all-to-all-start.3) | async-done | bytes 524320 | tf_op jit(solution)/shard_map/all_to_all | solution.py:278
  173.5 0.2 reduce_sum.38
  173.7 0.1 broadcast_select_fusion
  173.8 0.1 select_n.57
  174.0 0.5 convolution_multiply_fusion
  174.5 0.1 broadcast_in_dim.47
  174.6 0.7 broadcast_in_dim.48
  175.2 3.5 %all-to-all-start.4 = ((f32[16,12,128]{2,1,0:T(8,128)}), f32[16,12,128]{2,1,0:T(8,128)S(1)}, u32[]{:S(2)}, u32[]{:S(2)}) async-start(f32[16,12,128]{2,1,0:T(8,128)} %broadcast_in_dim.48), calls=%async_computation.4 | async-start | bytes 262144 | tf_op jit(solution)/shard_map/all_to_all | solution.py:88
  178.7 0.0 all-gather.8.cloned.1.call-done
  178.8 11.9 %all-to-all-done.4 = f32[16,12,128]{2,1,0:T(8,128)S(1)} async-done(((f32[16,12,128]{2,1,0:T(8,128)}), f32[16,12,128]{2,1,0:T(8,128)S(1)}, u32[]{:S(2)}, u32[]{:S(2)}) %all-to-all-start.4) | async-done | bytes 98336 | tf_op jit(solution)/shard_map/all_to_all | solution.py:88
  190.7 1.0 broadcast_in_dim.49
  191.7 7.0 %all-to-all-start.5 = ((bf16[32,96,128]{2,1,0:T(8,128)(2,1)}), bf16[32,96,128]{2,1,0:T(8,128)(2,1)S(1)}, u32[]{:S(2)}, u32[]{:S(2)}) async-start(bf16[32,96,128]{2,1,0:T(8,128)(2,1)} %broadcast_in_dim.49), calls=%async_computation.5 | async-start | bytes 1572864 | tf_op jit(solution)/shard_map/all_to_all | solution.py:88
  198.7 1.0 dynamic-slice_bitcast_fusion
  199.7 0.1 reshape.112
  199.8 0.3 copy.16
  200.1 0.2 reshape.113.queries_ref
  200.3 12.7 %all-to-all-done.5.features_ref = bf16[32,96,128]{2,1,0:T(8,128)(2,1)S(1)} async-done(((bf16[32,96,128]{2,1,0:T(8,128)(2,1)}), bf16[32,96,128]{2,1,0:T(8,128)(2,1)S(1)}, u32[]{:S(2)}, u32[]{:S(2)}) %all-to-all-start.5) | async-done | bytes 786464 | tf_op jit(solution)/shard_map/all_to_all | solution.py:88
  213.0 8.8 %solve.1 = f32[32,96]{1,0:T(8,128)} custom-call(bf16[32,96,128]{2,1,0:T(8,128)(2,1)S(1)} %all-to-all-done.5.features_ref, bf16[32,4096]{1,0:T(8,128)(2,1)S(1)} %reshape.113.queries_ref), custom_call_target="tpu_custom_call" | custom-call | tf_op jit(solution)/shard_map/solve/pallas_call | solution.py:79
  (28 shorter events, 0.2 us)
Async XLA Ops:
  6.5 102.6 %copy-start = (bf16[896,64]{0,1:T(8,128)(2,1)S(1)}, bf16[896,64]{0,1:T(8,128)(2,1)}, u32[]{:S(2)}) copy-start(bf16[896,64]{0,1:T(8,128)(2,1)} %param.11) | copy-start | bytes 344068
  6.5 99.9 %all-gather.6.cloned.1.call-start = ((), (), s32[]{:S(2)}) async-start(), calls=%async_computation.6 | async-start | bytes 17694720 | tf_op jit(solution)/shard_map/all_gather | solution.py:251
  9.6 0.9 copy-start.1
  9.6 1.1 copy-start.2
  9.7 65.4 %copy-start.3 = (bf16[256,64]{0,1:T(8,128)(2,1)S(1)}, bf16[256,64]{0,1:T(8,128)(2,1)}, u32[]{:S(2)}) copy-start(bf16[256,64]{0,1:T(8,128)(2,1)} %param.12) | copy-start | bytes 98308
  10.6 74.7 %copy-start.4 = (bf16[32,256]{1,0:T(8,128)(2,1)S(1)}, bf16[32,256]{1,0:T(8,128)(2,1)}, u32[]{:S(2)}) copy-start(bf16[32,256]{1,0:T(8,128)(2,1)} %param.13) | copy-start | bytes 49156
  22.4 12.2 %collective-permute-start = (bf16[4,448,128]{2,1,0:T(8,128)(2,1)S(1)}, bf16[4,448,128]{2,1,0:T(8,128)(2,1)S(1)}, u32[]{:S(2)}, u32[]{:S(2)}) collective-permute-start(bf16[4,448,128]{2,1,0:T(8,128)(2,1)S(1)} %all_to_all.30.refs_0_), channel_id=1, source_target_pairs={{0,64},{64,128},{128,192},{192,256},{256,320},{320,384},{384,448},... | collective-permute-start | bytes 1376264 | tf_op jit(solution)/shard_map/ppermute | solution.py:189
  26.9 11.9 %collective-permute-start.2 = (bf16[4,448,128]{2,1,0:T(8,128)(2,1)S(1)}, bf16[4,448,128]{2,1,0:T(8,128)(2,1)S(1)}, u32[]{:S(2)}, u32[]{:S(2)}) collective-permute-start(bf16[4,448,128]{2,1,0:T(8,128)(2,1)S(1)} %all_to_all.30.refs_0_), channel_id=1, source_target_pairs={{64,0},{128,64},{192,128},{256,192},{320,256},{384,320},{448,384},... | collective-permute-start | bytes 1376264 | tf_op jit(solution)/shard_map/ppermute | solution.py:190
  34.5 5.6 %collective-permute-start.1 = (bf16[4,448,128]{2,1,0:T(8,128)(2,1)S(1)}, bf16[4,448,128]{2,1,0:T(8,128)(2,1)S(1)}, u32[]{:S(2)}, u32[]{:S(2)}) collective-permute-start(bf16[4,448,128]{2,1,0:T(8,128)(2,1)S(1)} %collective-permute-done.refs_1_), channel_id=1, source_target_pairs={{64,128},{128,192},{192,256},{256,320},{320,384},{384,448},{65,129... | collective-permute-start | bytes 1376264 | tf_op jit(solution)/shard_map/ppermute | solution.py:189
  38.8 11.3 %collective-permute-start.4 = (bf16[4,448,128]{2,1,0:T(8,128)(2,1)S(1)}, bf16[4,448,128]{2,1,0:T(8,128)(2,1)S(1)}, u32[]{:S(2)}, u32[]{:S(2)}) collective-permute-start(bf16[4,448,128]{2,1,0:T(8,128)(2,1)S(1)} %collective-permute-done.2.refs_8_), channel_id=1, source_target_pairs={{64,0},{128,64},{192,128},{256,192},{320,256},{384,320},{65,1},{12... | collective-permute-start | bytes 1376264 | tf_op jit(solution)/shard_map/ppermute | solution.py:190
  40.1 11.3 %collective-permute-start.3 = (bf16[4,448,128]{2,1,0:T(8,128)(2,1)S(1)}, bf16[4,448,128]{2,1,0:T(8,128)(2,1)S(1)}, u32[]{:S(2)}, u32[]{:S(2)}) collective-permute-start(bf16[4,448,128]{2,1,0:T(8,128)(2,1)S(1)} %collective-permute-done.1.refs_2_), channel_id=1, source_target_pairs={{128,192},{192,256},{256,320},{320,384},{384,448},{129,193},{193,2... | collective-permute-start | bytes 1376264 | tf_op jit(solution)/shard_map/ppermute | solution.py:189
  50.1 12.5 %collective-permute-start.6 = (bf16[4,448,128]{2,1,0:T(8,128)(2,1)S(1)}, bf16[4,448,128]{2,1,0:T(8,128)(2,1)S(1)}, u32[]{:S(2)}, u32[]{:S(2)}) collective-permute-start(bf16[4,448,128]{2,1,0:T(8,128)(2,1)S(1)} %collective-permute-done.4.refs_9_), channel_id=1, source_target_pairs={{64,0},{128,64},{192,128},{256,192},{320,256},{65,1},{129,65},{193... | collective-permute-start | bytes 1376264 | tf_op jit(solution)/shard_map/ppermute | solution.py:190
  51.4 12.5 %collective-permute-start.5 = (bf16[4,448,128]{2,1,0:T(8,128)(2,1)S(1)}, bf16[4,448,128]{2,1,0:T(8,128)(2,1)}, u32[]{:S(2)}, u32[]{:S(2)}) collective-permute-start(bf16[4,448,128]{2,1,0:T(8,128)(2,1)S(1)} %collective-permute-done.3.refs_3_), channel_id=1, source_target_pairs={{192,256},{256,320},{320,384},{384,448},{193,257},{257,321},{321,3... | collective-permute-start | bytes 1376264 | tf_op jit(solution)/shard_map/ppermute | solution.py:189
  62.6 10.2 %collective-permute-start.8 = (bf16[4,448,128]{2,1,0:T(8,128)(2,1)S(1)}, bf16[4,448,128]{2,1,0:T(8,128)(2,1)}, u32[]{:S(2)}, u32[]{:S(2)}) collective-permute-start(bf16[4,448,128]{2,1,0:T(8,128)(2,1)S(1)} %collective-permute-done.6.refs_10_), channel_id=1, source_target_pairs={{64,0},{128,64},{192,128},{256,192},{65,1},{129,65},{193,129},{257... | collective-permute-start | bytes 1376264 | tf_op jit(solution)/shard_map/ppermute | solution.py:190
  63.9 26.7 %collective-permute-start.7 = (bf16[4,448,128]{2,1,0:T(8,128)(2,1)}, bf16[4,448,128]{2,1,0:T(8,128)(2,1)}, u32[]{:S(2)}, u32[]{:S(2)}) collective-permute-start(bf16[4,448,128]{2,1,0:T(8,128)(2,1)} %collective-permute-done.5.refs_4_), channel_id=1, source_target_pairs={{256,320},{320,384},{384,448},{257,321},{321,385},{385,449},{258,3... | collective-permute-start | bytes 1376264 | tf_op jit(solution)/shard_map/ppermute | solution.py:189
  72.8 19.3 %collective-permute-start.10 = (bf16[4,448,128]{2,1,0:T(8,128)(2,1)}, bf16[4,448,128]{2,1,0:T(8,128)(2,1)}, u32[]{:S(2)}, u32[]{:S(2)}) collective-permute-start(bf16[4,448,128]{2,1,0:T(8,128)(2,1)} %collective-permute-done.8.refs_11_), channel_id=1, source_target_pairs={{64,0},{128,64},{192,128},{65,1},{129,65},{193,129},{66,2},{130,66... | collective-permute-start | bytes 1376264 | tf_op jit(solution)/shard_map/ppermute | solution.py:190
  75.9 14.7 %all-to-all-start.1 = ((f32[8,8,512]{2,1,0:T(8,128)}), f32[8,8,512]{2,1,0:T(8,128)S(1)}, u32[]{:S(2)}, u32[]{:S(2)}) async-start(f32[8,8,512]{2,1,0:T(8,128)} %convolution_bitcast_fusion), calls=%async_computation.1 | async-start | bytes 262144 | tf_op jit(solution)/shard_map/all_to_all | solution.py:263
  85.3 93.5 %all-gather.8.cloned.1.call-start = ((), (), s32[]{:S(2)}) async-start(), calls=%async_computation.7 | async-start | bytes 1622016 | tf_op jit(solution)/shard_map/all_gather | solution.py:235
  90.6 15.8 %collective-permute-start.9 = (bf16[4,448,128]{2,1,0:T(8,128)(2,1)}, bf16[4,448,128]{2,1,0:T(8,128)(2,1)}, u32[]{:S(2)}, u32[]{:S(2)}) collective-permute-start(bf16[4,448,128]{2,1,0:T(8,128)(2,1)} %collective-permute-done.7.refs_5_), channel_id=1, source_target_pairs={{320,384},{384,448},{321,385},{385,449},{322,386},{386,450},{323,3... | collective-permute-start | bytes 1376264 | tf_op jit(solution)/shard_map/ppermute | solution.py:189
  92.1 15.8 %collective-permute-start.12 = (bf16[4,448,128]{2,1,0:T(8,128)(2,1)}, bf16[4,448,128]{2,1,0:T(8,128)(2,1)}, u32[]{:S(2)}, u32[]{:S(2)}) collective-permute-start(bf16[4,448,128]{2,1,0:T(8,128)(2,1)} %collective-permute-done.10.refs_12_), channel_id=1, source_target_pairs={{64,0},{128,64},{65,1},{129,65},{66,2},{130,66},{67,3},{131,67},{6... | collective-permute-start | bytes 1376264 | tf_op jit(solution)/shard_map/ppermute | solution.py:190
  106.4 2.9 %collective-permute-start.11 = (bf16[4,448,128]{2,1,0:T(8,128)(2,1)}, bf16[4,448,128]{2,1,0:T(8,128)(2,1)}, u32[]{:S(2)}, u32[]{:S(2)}) collective-permute-start(bf16[4,448,128]{2,1,0:T(8,128)(2,1)} %collective-permute-done.9.refs_6_), channel_id=1, source_target_pairs={{384,448},{385,449},{386,450},{387,451},{388,452},{389,453},{390,4... | collective-permute-start | bytes 1376264 | tf_op jit(solution)/shard_map/ppermute | solution.py:189
  107.9 23.9 %collective-permute-start.13 = (bf16[4,448,128]{2,1,0:T(8,128)(2,1)}, bf16[4,448,128]{2,1,0:T(8,128)(2,1)}, u32[]{:S(2)}, u32[]{:S(2)}) collective-permute-start(bf16[4,448,128]{2,1,0:T(8,128)(2,1)} %collective-permute-done.12.refs_13_), channel_id=1, source_target_pairs={{64,0},{65,1},{66,2},{67,3},{68,4},{69,5},{70,6},{71,7},{72,8},{73... | collective-permute-start | bytes 1376264 | tf_op jit(solution)/shard_map/ppermute | solution.py:190
  132.6 21.3 %all-to-all-start.2 = ((f32[32,8,512]{2,1,0:T(8,128)}), f32[32,8,512]{2,1,0:T(8,128)}, u32[]{:S(2)}, u32[]{:S(2)}) async-start(f32[32,8,512]{2,1,0:T(8,128)} %broadcast_in_dim.44), calls=%async_computation.2 | async-start | bytes 1048576 | tf_op jit(solution)/shard_map/all_to_all | solution.py:88
  153.9 19.7 %all-to-all-start.3 = ((f32[32,2,2048]{2,1,0:T(2,128)}), f32[32,2,2048]{2,1,0:T(2,128)S(1)}, u32[]{:S(2)}, u32[]{:S(2)}) async-start(f32[32,2,2048]{2,1,0:T(2,128)} %layer.1), calls=%async_computation.3 | async-start | bytes 1048576 | tf_op jit(solution)/shard_map/all_to_all | solution.py:278
  175.2 15.4 %all-to-all-start.4 = ((f32[16,12,128]{2,1,0:T(8,128)}), f32[16,12,128]{2,1,0:T(8,128)S(1)}, u32[]{:S(2)}, u32[]{:S(2)}) async-start(f32[16,12,128]{2,1,0:T(8,128)} %broadcast_in_dim.48), calls=%async_computation.4 | async-start | bytes 262144 | tf_op jit(solution)/shard_map/all_to_all | solution.py:88
  191.7 21.3 %all-to-all-start.5 = ((bf16[32,96,128]{2,1,0:T(8,128)(2,1)}), bf16[32,96,128]{2,1,0:T(8,128)(2,1)S(1)}, u32[]{:S(2)}, u32[]{:S(2)}) async-start(bf16[32,96,128]{2,1,0:T(8,128)(2,1)} %broadcast_in_dim.49), calls=%async_computation.5 | async-start | bytes 1572864 | tf_op jit(solution)/shard_map/all_to_all | solution.py:88
Sparse Core Ops, SparseCore 0:
  9.8 93.9 all-gather.5
  106.9 65.6 all-gather.7

commit v7 on v6

--- a/solution.py
+++ b/solution.py
@@ -193,6 +193,12 @@
         self.ups[-1] = tie(self.ups[-1], *values)
         self.downs[-1] = tie(self.downs[-1], *values)
 
+    def join(self, value):
+        self.ups[-1], self.downs[-1], value = lax.optimization_barrier(
+            (self.ups[-1], self.downs[-1], value)
+        )
+        return value
+
     def blocks(self):
         return self.ups + self.downs[1:]
 
@@ -258,17 +264,15 @@
     out = out_partial(out_grad, out_factor).reshape(X * C, rank // (X * C), -1)
     for s in range(1, ZL):
         chain.step()
-        if s == 1:
-            out = tie(out, chain.ups[-1])
+        if s == 2:
             out = lax.all_to_all(out, ("x", "c"), 0, 0, tiled=True).sum(0)
-        if s == 5:
-            chain.after(out)
-            out = tie(out, chain.ups[-1])
-            out, query_rows = exchange_z(out, queries)
+        if s < 3:
+            out = chain.join(out)
         if s == 6:
-            chain.after(out, plane_tokens)
+            out = chain.join(out)
+        if s == 7:
+            out, query_rows = chain.join(exchange_z(out, queries))
     shared = share_plane(out, query_rows)
-    out = tie(out, chain.ups[-1], chain.downs[-1])
     out = share(out, PLANE, Y * X * C)
 
     place = jnp.stack([z]).astype(jnp.int32)

time: 230 us -> 240 us (1.043)
  blocking collectives: 23.7 us -> 36.3 us
  waiting for transfers between devices: 99.8 us -> 94.7 us
  local copies, waits for them, and re-layouts: 10.8 us -> 13.4 us
    all_to_all x0 -> x1, blocking collectives: none -> 12.6 us  [shards(): out = lax.all_to_all(out, ('x', 'c'), 0, 0, tiled=True).sum(0)]
    all_to_all x3, starting transfers between devices: 17 us -> 27.9 us  [share(): lax.all_to_all(jnp.broadcast_to(x[None], (count,) + x.shape), axes, 0, 0,...]
    all_to_all x1 -> x0, starting transfers between devices: 9.37 us -> none  [shards(): out = lax.all_to_all(out, ('x', 'c'), 0, 0, tiled=True).sum(0)]
    all_to_all x1 -> x0, waiting for transfers between devices: 5.29 us -> none  [shards(): out = lax.all_to_all(out, ('x', 'c'), 0, 0, tiled=True).sum(0)]
    unnamed x10 -> x20, local copies, waits for them, and re-layouts: 0.92 us -> 4.45 us
    all_gather x1, waiting for transfers between devices: 0.02 us -> 2.69 us  [share_plane(): return lax.all_gather(sent, PLANE)]
    all_to_all x3, waiting for transfers between devices: 24.6 us -> 22 us  [share(): lax.all_to_all(jnp.broadcast_to(x[None], (count,) + x.shape), axes, 0, 0,...]
  transfers between devices with their start and end apart: 21 -> 20, of which waited for: 10 -> 11; matrix products, arithmetic and copies ran while one was open for 4% -> 3% of each run, Pallas kernels for 6% -> 6%
where the time goes in v7:
time: 240 us; the launch traced here: 239 us
  waiting for transfers between devices  94.7 us (39%)
  starting transfers between devices  55.4 us (23%)
  blocking collectives  36.3 us (15%)
  Pallas kernels  23.3 us (10%)
  between operations  13.8 us (6%)
  local copies, waits for them, and re-layouts  13.4 us (6%)
    ppermute x7, waiting for transfers between devices, step(): lax.ppermute(down, 'zl', [(z, z - 1) for z in range(1, ZL + 1 - s)])  53.4 us
    all_to_all x3, starting transfers between devices, share(): lax.all_to_all(jnp.broadcast_to(x[None], (count,) + x.shape), axes, 0, 0,...  27.9 us
    all_to_all x3, waiting for transfers between devices, share(): lax.all_to_all(jnp.broadcast_to(x[None], (count,) + x.shape), axes, 0, 0,...  22 us
    pallas_call x1, Pallas kernels, layer(): pl.pallas_call(layer_kernel, out_shape=jax.ShapeDtypeStruct((rank // 2, 2...  14.5 us
    all_to_all x1, blocking collectives, shards(): out = lax.all_to_all(out, ('x', 'c'), 0, 0, tiled=True).sum(0)  12.6 us
    all_gather x1, blocking collectives, exchange_z(): got = lax.all_gather(sent, 'zh')  12.3 us
    all_to_all x1, blocking collectives, shards(): chain = Chain(lax.all_to_all(quarters, 'y', 0, 0, tiled=True))  11.4 us
    ppermute x7, starting transfers between devices, step(): lax.ppermute(up, 'zl', [(z, z + 1) for z in range(s - 1, ZL - 1)])  10.9 us
  transfers between devices with their start and end apart: 20, of which 11 were waited for; matrix products, arithmetic and copies ran while one was open for 3% of the time, Pallas kernels for 6%

profile of v7, /device:TPU:1, one launch (start us, length us, event | category | flops | bytes accessed | tf_op | source)
XLA Modules:
  0.0 238.7 jit_solution(8793404559591971354)
XLA Ops:
  6.5 3.1 %constant_dynamic-slice_fusion = bf16[240,4096]{1,0:T(8,128)(2,1)} fusion(bf16[480,4096]{1,0:T(8,128)(2,1)} %param.7, s32[]{:T(128)S(6)} %select_n.55), kind=kLoop, calls=%fused_computation.35 | loop fusion | bytes 3932164 | tf_op jit(solution)/shard_map/dynamic_slice | solution.py:256
  9.6 0.0 all-gather.6.cloned.1.call-update
  9.6 0.0 copy-start.8
  9.6 0.0 all-gather.8.cloned.1.call-start
  9.7 0.8 copy-done.6
  10.5 0.2 copy.14
  10.7 0.2 copy.13
  10.9 11.4 %all_to_all.30.refs_0_ = bf16[4,448,128]{2,1,0:T(8,128)(2,1)S(1)} all-to-all(bf16[4,448,128]{2,1,0:T(8,128)(2,1)S(1)} %pad_maximum_fusion), channel_id=1, replica_groups=mesh['zl'=8,'y'=4,'x'=4,'zh'=2,'c'=2] {'y'}, dimensions={0} | all-to-all | bytes 917504 | tf_op jit(solution)/shard_map/all_to_all | solution.py:263
  22.3 4.5 %collective-permute-start = (bf16[4,448,128]{2,1,0:T(8,128)(2,1)S(1)}, bf16[4,448,128]{2,1,0:T(8,128)(2,1)S(1)}, u32[]{:S(2)}, u32[]{:S(2)}) collective-permute-start(bf16[4,448,128]{2,1,0:T(8,128)(2,1)S(1)} %all_to_all.30.refs_0_), channel_id=1, source_target_pairs={{0,64},{64,128},{128,192},{192,256},{256,320},{320,384},{384,448},... | collective-permute-start | bytes 1376264 | tf_op jit(solution)/shard_map/ppermute | solution.py:189
  26.9 1.3 collective-permute-start.1
  28.2 0.2 convolution_bitcast_fusion
  28.4 6.1 %collective-permute-done.refs_1_ = bf16[4,448,128]{2,1,0:T(8,128)(2,1)S(1)} collective-permute-done((bf16[4,448,128]{2,1,0:T(8,128)(2,1)S(1)}, bf16[4,448,128]{2,1,0:T(8,128)(2,1)S(1)}, u32[]{:S(2)}, u32[]{:S(2)}) %collective-permute-start) | collective-permute-done | bytes 458784 | tf_op jit(solution)/shard_map/ppermute | solution.py:189
  34.5 4.2 %collective-permute-done.1.refs_8_ = bf16[4,448,128]{2,1,0:T(8,128)(2,1)S(1)} collective-permute-done((bf16[4,448,128]{2,1,0:T(8,128)(2,1)S(1)}, bf16[4,448,128]{2,1,0:T(8,128)(2,1)S(1)}, u32[]{:S(2)}, u32[]{:S(2)}) %collective-permute-start.1) | collective-permute-done | bytes 458784 | tf_op jit(solution)/shard_map/ppermute | solution.py:190
  38.7 0.7 collective-permute-start.2
  39.4 1.3 collective-permute-start.3
  40.7 12.6 %all_to_all.31 = f32[8,8,512]{2,1,0:T(8,128)S(1)} all-to-all(f32[8,8,512]{2,1,0:T(8,128)S(1)} %convolution_bitcast_fusion), channel_id=1, replica_groups=mesh['zl'=8,'y'=4,'x'=4,'zh'=2,'c'=2] {'x','c'}, dimensions={0} | all-to-all | bytes 262144 | tf_op jit(solution)/shard_map/all_to_all | solution.py:268
  53.3 1.6 collective-permute-done.3.refs_9_
  54.9 0.7 collective-permute-start.4
  55.6 1.3 collective-permute-start.6
  56.9 0.7 collective-permute-start.5
  57.6 14.8 %collective-permute-done.6.refs_10_ = bf16[4,448,128]{2,1,0:T(8,128)(2,1)S(1)} collective-permute-done((bf16[4,448,128]{2,1,0:T(8,128)(2,1)S(1)}, bf16[4,448,128]{2,1,0:T(8,128)(2,1)S(1)}, u32[]{:S(2)}, u32[]{:S(2)}) %collective-permute-start.6) | collective-permute-done | bytes 458784 | tf_op jit(solution)/shard_map/ppermute | solution.py:190
  72.4 1.3 collective-permute-start.8
  73.7 0.0 collective-permute-done.5.refs_4_
  73.7 1.4 collective-permute-start.7
  75.2 0.8 copy-done.1
  76.0 13.2 %collective-permute-done.8.refs_11_ = bf16[4,448,128]{2,1,0:T(8,128)(2,1)S(1)} collective-permute-done((bf16[4,448,128]{2,1,0:T(8,128)(2,1)S(1)}, bf16[4,448,128]{2,1,0:T(8,128)(2,1)S(1)}, u32[]{:S(2)}, u32[]{:S(2)}) %collective-permute-start.8) | collective-permute-done | bytes 458784 | tf_op jit(solution)/shard_map/ppermute | solution.py:190
  89.1 1.3 collective-permute-start.10
  90.4 0.8 copy-done.3
  91.2 1.4 collective-permute-start.9
  92.6 8.9 %collective-permute-done.10.refs_12_ = bf16[4,448,128]{2,1,0:T(8,128)(2,1)} collective-permute-done((bf16[4,448,128]{2,1,0:T(8,128)(2,1)S(1)}, bf16[4,448,128]{2,1,0:T(8,128)(2,1)}, u32[]{:S(2)}, u32[]{:S(2)}) %collective-permute-start.10) | collective-permute-done | bytes 458784 | tf_op jit(solution)/shard_map/ppermute | solution.py:190
  101.5 1.3 collective-permute-start.11
  102.9 10.7 %collective-permute-done.11.refs_13_ = bf16[4,448,128]{2,1,0:T(8,128)(2,1)} collective-permute-done((bf16[4,448,128]{2,1,0:T(8,128)(2,1)}, bf16[4,448,128]{2,1,0:T(8,128)(2,1)}, u32[]{:S(2)}, u32[]{:S(2)}) %collective-permute-start.11) | collective-permute-done | bytes 458784 | tf_op jit(solution)/shard_map/ppermute | solution.py:190
  113.6 1.4 collective-permute-start.12
  115.1 1.3 collective-permute-start.13
  116.4 12.3 %all-gather = bf16[64,512]{1,0:T(8,128)(2,1)S(1)} all-gather(bf16[32,512]{1,0:T(8,128)(2,1)S(1)} %pad_maximum_fusion.2), channel_id=2, replica_groups=mesh['zl'=8,'y'=4,'x'=4,'zh'=2,'c'=2] {'zh'}, dimensions={0}, use_global_device_ids=true | all-gather | bytes 98304 | tf_op jit(solution)/shard_map/all_gather | solution.py:228
  128.7 0.6 pad_maximum_fusion.1
  129.4 0.0 all-gather.8.cloned.1.call-update
  129.4 0.1 dynamic-slice_bitcast_fusion.1
  129.5 0.8 broadcast_in_dim.44
  130.3 9.2 %all-to-all-start.2 = ((f32[32,8,512]{2,1,0:T(8,128)}), f32[32,8,512]{2,1,0:T(8,128)}, u32[]{:S(2)}, u32[]{:S(2)}) async-start(f32[32,8,512]{2,1,0:T(8,128)} %broadcast_in_dim.44), calls=%async_computation.2 | async-start | bytes 1048576 | tf_op jit(solution)/shard_map/all_to_all | solution.py:88
  139.6 0.0 all-gather.6.cloned.1.call-done
  139.6 1.0 copy-done.2
  140.7 1.0 copy-done.4
  141.7 14.5 %layer.1 = f32[32,2,2048]{2,1,0:T(2,128)} custom-call(s32[1]{0:T(128)} %bitcast.place_ref, bf16[64,256]{1,0:T(8,128)(2,1)S(1)} %pad.8.factor_ref, bf16[4,448,128]{2,1,0:T(8,128)(2,1)S(1)} %all_to_all.30.refs_0_, bf16[4,448,128]{2,1,0:T(8,128)(2,1)S(1)} %collective-permute-done.refs_1_, bf16[4,448,128]{2,1,0:T(8,128)(2,1)S(1)} %collective-permute-done.2.refs_2_, ...), custom_call_target="tpu_custom_call" | custom-call | flops 7046430720 | bytes 19398656 | tf_op jit(solution)/shard_map/layer/pallas_call | solution.py:154
  156.2 7.5 %all-to-all-start.3 = ((f32[32,2,2048]{2,1,0:T(2,128)}), f32[32,2,2048]{2,1,0:T(2,128)S(1)}, u32[]{:S(2)}, u32[]{:S(2)}) async-start(f32[32,2,2048]{2,1,0:T(2,128)} %layer.1), calls=%async_computation.3 | async-start | bytes 1048576 | tf_op jit(solution)/shard_map/all_to_all | solution.py:282
  163.7 1.1 copy.17
  164.8 10.4 %all-to-all-done.3 = f32[32,2,2048]{2,1,0:T(2,128)S(1)} async-done(((f32[32,2,2048]{2,1,0:T(2,128)}), f32[32,2,2048]{2,1,0:T(2,128)S(1)}, u32[]{:S(2)}, u32[]{:S(2)}) %all-to-all-start.3) | async-done | bytes 524320 | tf_op jit(solution)/shard_map/all_to_all | solution.py:282
  175.2 0.2 reduce_sum.38
  175.4 0.1 broadcast_select_fusion
  175.5 0.1 select_n.57
  175.6 0.5 convolution_multiply_fusion
  176.2 0.1 broadcast_in_dim.47
  176.2 0.7 broadcast_in_dim.48
  176.9 11.7 %all-to-all-start.4 = ((f32[16,12,128]{2,1,0:T(8,128)}), f32[16,12,128]{2,1,0:T(8,128)S(1)}, u32[]{:S(2)}, u32[]{:S(2)}) async-start(f32[16,12,128]{2,1,0:T(8,128)} %broadcast_in_dim.48), calls=%async_computation.4 | async-start | bytes 262144 | tf_op jit(solution)/shard_map/all_to_all | solution.py:88
  188.7 2.7 %all-gather.8.cloned.1.call-done = bf16[1536,512]{1,0:T(8,128)(2,1)} async-done(((bf16[48,512]{1,0:T(8,128)(2,1)}), bf16[1536,512]{1,0:T(8,128)(2,1)}) %all-gather.8.cloned.1.call-update) | async-done | bytes 1572880 | tf_op jit(solution)/shard_map/all_gather | solution.py:241
  191.4 9.3 %all-to-all-done.4 = f32[16,12,128]{2,1,0:T(8,128)S(1)} async-done(((f32[16,12,128]{2,1,0:T(8,128)}), f32[16,12,128]{2,1,0:T(8,128)S(1)}, u32[]{:S(2)}, u32[]{:S(2)}) %all-to-all-start.4) | async-done | bytes 98336 | tf_op jit(solution)/shard_map/all_to_all | solution.py:88
  200.7 1.0 broadcast_in_dim.49
  201.7 7.0 %all-to-all-start.5 = ((bf16[32,96,128]{2,1,0:T(8,128)(2,1)}), bf16[32,96,128]{2,1,0:T(8,128)(2,1)S(1)}, u32[]{:S(2)}, u32[]{:S(2)}) async-start(bf16[32,96,128]{2,1,0:T(8,128)(2,1)} %broadcast_in_dim.49), calls=%async_computation.5 | async-start | bytes 1572864 | tf_op jit(solution)/shard_map/all_to_all | solution.py:88
  208.7 1.0 dynamic-slice_bitcast_fusion
  209.7 0.1 reshape.120
  209.8 0.3 copy.16
  210.1 0.2 reshape.121.queries_ref
  210.3 12.7 %all-to-all-done.5.features_ref = bf16[32,96,128]{2,1,0:T(8,128)(2,1)S(1)} async-done(((bf16[32,96,128]{2,1,0:T(8,128)(2,1)}), bf16[32,96,128]{2,1,0:T(8,128)(2,1)S(1)}, u32[]{:S(2)}, u32[]{:S(2)}) %all-to-all-start.5) | async-done | bytes 786464 | tf_op jit(solution)/shard_map/all_to_all | solution.py:88
  223.0 8.8 %solve.1 = f32[32,96]{1,0:T(8,128)} custom-call(bf16[32,96,128]{2,1,0:T(8,128)(2,1)S(1)} %all-to-all-done.5.features_ref, bf16[32,4096]{1,0:T(8,128)(2,1)S(1)} %reshape.121.queries_ref), custom_call_target="tpu_custom_call" | custom-call | tf_op jit(solution)/shard_map/solve/pallas_call | solution.py:79
  (39 shorter events, 0.3 us)
Async XLA Ops:
  6.5 122.9 %copy-start = (bf16[896,64]{0,1:T(8,128)(2,1)S(1)}, bf16[896,64]{0,1:T(8,128)(2,1)}, u32[]{:S(2)}) copy-start(bf16[896,64]{0,1:T(8,128)(2,1)} %param.11) | copy-start | bytes 344068
  6.5 133.1 %all-gather.6.cloned.1.call-start = ((), (), s32[]{:S(2)}) async-start(), calls=%async_computation.6 | async-start | bytes 17694720 | tf_op jit(solution)/shard_map/all_gather | solution.py:257
  9.6 0.9 copy-start.6
  9.6 1.1 copy-start.7
  9.6 18.6 %copy-start.5 = (bf16[480,256]{1,0:T(8,128)(2,1)S(1)}, bf16[480,256]{1,0:T(8,128)(2,1)}, u32[]{:S(2)}) copy-start(bf16[480,256]{1,0:T(8,128)(2,1)} %param.10) | copy-start | bytes 737284
  9.6 18.6 %copy-start.8 = (bf16[256,64]{0,1:T(8,128)(2,1)S(1)}, bf16[256,64]{0,1:T(8,128)(2,1)}, u32[]{:S(2)}) copy-start(bf16[256,64]{0,1:T(8,128)(2,1)} %param.12) | copy-start | bytes 98308
  9.6 181.7 %all-gather.8.cloned.1.call-start = ((), (), s32[]{:S(2)}) async-start(), calls=%async_computation.7 | async-start | bytes 1622016 | tf_op jit(solution)/shard_map/all_gather | solution.py:241
  10.5 92.3 %copy-start.9 = (bf16[32,256]{1,0:T(8,128)(2,1)S(1)}, bf16[32,256]{1,0:T(8,128)(2,1)}, u32[]{:S(2)}) copy-start(bf16[32,256]{1,0:T(8,128)(2,1)} %param.13) | copy-start | bytes 49156
  22.3 12.2 %collective-permute-start = (bf16[4,448,128]{2,1,0:T(8,128)(2,1)S(1)}, bf16[4,448,128]{2,1,0:T(8,128)(2,1)S(1)}, u32[]{:S(2)}, u32[]{:S(2)}) collective-permute-start(bf16[4,448,128]{2,1,0:T(8,128)(2,1)S(1)} %all_to_all.30.refs_0_), channel_id=1, source_target_pairs={{0,64},{64,128},{128,192},{192,256},{256,320},{320,384},{384,448},... | collective-permute-start | bytes 1376264 | tf_op jit(solution)/shard_map/ppermute | solution.py:189
  26.9 11.8 %collective-permute-start.1 = (bf16[4,448,128]{2,1,0:T(8,128)(2,1)S(1)}, bf16[4,448,128]{2,1,0:T(8,128)(2,1)S(1)}, u32[]{:S(2)}, u32[]{:S(2)}) collective-permute-start(bf16[4,448,128]{2,1,0:T(8,128)(2,1)S(1)} %all_to_all.30.refs_0_), channel_id=1, source_target_pairs={{64,0},{128,64},{192,128},{256,192},{320,256},{384,320},{448,384},... | collective-permute-start | bytes 1376264 | tf_op jit(solution)/shard_map/ppermute | solution.py:190
  38.7 14.6 %collective-permute-start.2 = (bf16[4,448,128]{2,1,0:T(8,128)(2,1)S(1)}, bf16[4,448,128]{2,1,0:T(8,128)(2,1)S(1)}, u32[]{:S(2)}, u32[]{:S(2)}) collective-permute-start(bf16[4,448,128]{2,1,0:T(8,128)(2,1)S(1)} %collective-permute-done.refs_1_), channel_id=1, source_target_pairs={{64,128},{128,192},{192,256},{256,320},{320,384},{384,448},{65,129... | collective-permute-start | bytes 1376264 | tf_op jit(solution)/shard_map/ppermute | solution.py:189
  39.4 15.5 %collective-permute-start.3 = (bf16[4,448,128]{2,1,0:T(8,128)(2,1)S(1)}, bf16[4,448,128]{2,1,0:T(8,128)(2,1)S(1)}, u32[]{:S(2)}, u32[]{:S(2)}) collective-permute-start(bf16[4,448,128]{2,1,0:T(8,128)(2,1)S(1)} %collective-permute-done.1.refs_8_), channel_id=1, source_target_pairs={{64,0},{128,64},{192,128},{256,192},{320,256},{384,320},{65,1},{12... | collective-permute-start | bytes 1376264 | tf_op jit(solution)/shard_map/ppermute | solution.py:190
  54.9 2.0 collective-permute-start.4
  55.6 16.8 %collective-permute-start.6 = (bf16[4,448,128]{2,1,0:T(8,128)(2,1)S(1)}, bf16[4,448,128]{2,1,0:T(8,128)(2,1)S(1)}, u32[]{:S(2)}, u32[]{:S(2)}) collective-permute-start(bf16[4,448,128]{2,1,0:T(8,128)(2,1)S(1)} %collective-permute-done.3.refs_9_), channel_id=1, source_target_pairs={{64,0},{128,64},{192,128},{256,192},{320,256},{65,1},{129,65},{193... | collective-permute-start | bytes 1376264 | tf_op jit(solution)/shard_map/ppermute | solution.py:190
  56.9 16.8 %collective-permute-start.5 = (bf16[4,448,128]{2,1,0:T(8,128)(2,1)S(1)}, bf16[4,448,128]{2,1,0:T(8,128)(2,1)S(1)}, u32[]{:S(2)}, u32[]{:S(2)}) collective-permute-start(bf16[4,448,128]{2,1,0:T(8,128)(2,1)S(1)} %collective-permute-done.4.refs_3_), channel_id=1, source_target_pairs={{192,256},{256,320},{320,384},{384,448},{193,257},{257,321},{321,3... | collective-permute-start | bytes 1376264 | tf_op jit(solution)/shard_map/ppermute | solution.py:189
  72.4 16.7 %collective-permute-start.8 = (bf16[4,448,128]{2,1,0:T(8,128)(2,1)S(1)}, bf16[4,448,128]{2,1,0:T(8,128)(2,1)S(1)}, u32[]{:S(2)}, u32[]{:S(2)}) collective-permute-start(bf16[4,448,128]{2,1,0:T(8,128)(2,1)S(1)} %collective-permute-done.6.refs_10_), channel_id=1, source_target_pairs={{64,0},{128,64},{192,128},{256,192},{65,1},{129,65},{193,129},{257... | collective-permute-start | bytes 1376264 | tf_op jit(solution)/shard_map/ppermute | solution.py:190
  73.7 17.5 %collective-permute-start.7 = (bf16[4,448,128]{2,1,0:T(8,128)(2,1)S(1)}, bf16[4,448,128]{2,1,0:T(8,128)(2,1)}, u32[]{:S(2)}, u32[]{:S(2)}) collective-permute-start(bf16[4,448,128]{2,1,0:T(8,128)(2,1)S(1)} %collective-permute-done.5.refs_4_), channel_id=1, source_target_pairs={{256,320},{320,384},{384,448},{257,321},{321,385},{385,449},{258,3... | collective-permute-start | bytes 1376264 | tf_op jit(solution)/shard_map/ppermute | solution.py:189
  75.2 0.8 copy-start.1
  89.1 12.4 %collective-permute-start.10 = (bf16[4,448,128]{2,1,0:T(8,128)(2,1)S(1)}, bf16[4,448,128]{2,1,0:T(8,128)(2,1)}, u32[]{:S(2)}, u32[]{:S(2)}) collective-permute-start(bf16[4,448,128]{2,1,0:T(8,128)(2,1)S(1)} %collective-permute-done.8.refs_11_), channel_id=1, source_target_pairs={{64,0},{128,64},{192,128},{65,1},{129,65},{193,129},{66,2},{130,66... | collective-permute-start | bytes 1376264 | tf_op jit(solution)/shard_map/ppermute | solution.py:190
  90.4 0.8 copy-start.3
  91.2 11.7 %collective-permute-start.9 = (bf16[4,448,128]{2,1,0:T(8,128)(2,1)}, bf16[4,448,128]{2,1,0:T(8,128)(2,1)}, u32[]{:S(2)}, u32[]{:S(2)}) collective-permute-start(bf16[4,448,128]{2,1,0:T(8,128)(2,1)} %collective-permute-done.7.refs_5_), channel_id=1, source_target_pairs={{320,384},{384,448},{321,385},{385,449},{322,386},{386,450},{323,3... | collective-permute-start | bytes 1376264 | tf_op jit(solution)/shard_map/ppermute | solution.py:189
  101.5 12.1 %collective-permute-start.11 = (bf16[4,448,128]{2,1,0:T(8,128)(2,1)}, bf16[4,448,128]{2,1,0:T(8,128)(2,1)}, u32[]{:S(2)}, u32[]{:S(2)}) collective-permute-start(bf16[4,448,128]{2,1,0:T(8,128)(2,1)} %collective-permute-done.10.refs_12_), channel_id=1, source_target_pairs={{64,0},{128,64},{65,1},{129,65},{66,2},{130,66},{67,3},{131,67},{6... | collective-permute-start | bytes 1376264 | tf_op jit(solution)/shard_map/ppermute | solution.py:190
  113.6 15.1 %collective-permute-start.12 = (bf16[4,448,128]{2,1,0:T(8,128)(2,1)}, bf16[4,448,128]{2,1,0:T(8,128)(2,1)}, u32[]{:S(2)}, u32[]{:S(2)}) collective-permute-start(bf16[4,448,128]{2,1,0:T(8,128)(2,1)} %collective-permute-done.9.refs_6_), channel_id=1, source_target_pairs={{384,448},{385,449},{386,450},{387,451},{388,452},{389,453},{390,4... | collective-permute-start | bytes 1376264 | tf_op jit(solution)/shard_map/ppermute | solution.py:189
  115.1 13.6 %collective-permute-start.13 = (bf16[4,448,128]{2,1,0:T(8,128)(2,1)}, bf16[4,448,128]{2,1,0:T(8,128)(2,1)}, u32[]{:S(2)}, u32[]{:S(2)}) collective-permute-start(bf16[4,448,128]{2,1,0:T(8,128)(2,1)} %collective-permute-done.11.refs_13_), channel_id=1, source_target_pairs={{64,0},{65,1},{66,2},{67,3},{68,4},{69,5},{70,6},{71,7},{72,8},{73... | collective-permute-start | bytes 1376264 | tf_op jit(solution)/shard_map/ppermute | solution.py:190
  130.3 25.8 %all-to-all-start.2 = ((f32[32,8,512]{2,1,0:T(8,128)}), f32[32,8,512]{2,1,0:T(8,128)}, u32[]{:S(2)}, u32[]{:S(2)}) async-start(f32[32,8,512]{2,1,0:T(8,128)} %broadcast_in_dim.44), calls=%async_computation.2 | async-start | bytes 1048576 | tf_op jit(solution)/shard_map/all_to_all | solution.py:88
  139.6 1.0 copy-start.2
  140.7 1.0 copy-start.4
  156.2 19.1 %all-to-all-start.3 = ((f32[32,2,2048]{2,1,0:T(2,128)}), f32[32,2,2048]{2,1,0:T(2,128)S(1)}, u32[]{:S(2)}, u32[]{:S(2)}) async-start(f32[32,2,2048]{2,1,0:T(2,128)} %layer.1), calls=%async_computation.3 | async-start | bytes 1048576 | tf_op jit(solution)/shard_map/all_to_all | solution.py:282
  176.9 23.8 %all-to-all-start.4 = ((f32[16,12,128]{2,1,0:T(8,128)}), f32[16,12,128]{2,1,0:T(8,128)S(1)}, u32[]{:S(2)}, u32[]{:S(2)}) async-start(f32[16,12,128]{2,1,0:T(8,128)} %broadcast_in_dim.48), calls=%async_computation.4 | async-start | bytes 262144 | tf_op jit(solution)/shard_map/all_to_all | solution.py:88
  201.7 21.3 %all-to-all-start.5 = ((bf16[32,96,128]{2,1,0:T(8,128)(2,1)}), bf16[32,96,128]{2,1,0:T(8,128)(2,1)S(1)}, u32[]{:S(2)}, u32[]{:S(2)}) async-start(bf16[32,96,128]{2,1,0:T(8,128)(2,1)} %broadcast_in_dim.49), calls=%async_computation.5 | async-start | bytes 1572864 | tf_op jit(solution)/shard_map/all_to_all | solution.py:88
Sparse Core Ops, SparseCore 0:
  9.7 93.9 all-gather.5
  129.5 61.8 all-gather.7

commit v8 on v6

--- a/solution.py
+++ b/solution.py
@@ -266,15 +266,14 @@
             out = tie(out, chain.ups[-1])
             out, query_rows = exchange_z(out, queries)
         if s == 6:
+            shared = share_plane(out, query_rows)
             chain.after(out, plane_tokens)
-    shared = share_plane(out, query_rows)
-    out = tie(out, chain.ups[-1], chain.downs[-1])
-    out = share(out, PLANE, Y * X * C)
+            out = tie(out, chain.ups[-1])
+            out = share(out, PLANE, Y * X * C)
+    out = out.reshape(Y, rank, -1).transpose(1, 0, 2).reshape(rank, -1)
 
     place = jnp.stack([z]).astype(jnp.int32)
     in_part = layer(place, factor, chain.blocks(), plane_tokens)
-    in_part, out = lax.optimization_barrier((in_part, out))
-    out = out.reshape(Y, rank, -1).transpose(1, 0, 2).reshape(rank, -1)
     in_proj = lax.all_to_all(in_part, PLANE, 0, 0, tiled=True)
     in_proj = in_proj.sum(0)
 

time: 230 us -> 221 us (0.961)
  waiting for transfers between devices: 99.8 us -> 94.4 us
  starting transfers between devices: 54.6 us -> 50.7 us
    ppermute x7, waiting for transfers between devices: 52.5 us -> 45.5 us  [step(): lax.ppermute(down, 'zl', [(z, z - 1) for z in range(1, ZL + 1 - s)])]
  transfers between devices with their start and end apart: 21 -> 21, of which waited for: 10 -> 11; matrix products, arithmetic and copies ran while one was open for 4% -> 4% of each run, Pallas kernels for 6% -> 7%
where the time goes in v8:
time: 221 us; the launch traced here: 219 us
  waiting for transfers between devices  94.4 us (43%)
  starting transfers between devices  50.7 us (23%)
  blocking collectives  23.7 us (11%)
  Pallas kernels  23.5 us (11%)
  between operations  13.8 us (6%)
  local copies, waits for them, and re-layouts  10.8 us (5%)
    ppermute x7, waiting for transfers between devices, step(): lax.ppermute(down, 'zl', [(z, z - 1) for z in range(1, ZL + 1 - s)])  45.5 us
    all_to_all x3, waiting for transfers between devices, share(): lax.all_to_all(jnp.broadcast_to(x[None], (count,) + x.shape), axes, 0, 0,...  23.8 us
    all_to_all x3, starting transfers between devices, share(): lax.all_to_all(jnp.broadcast_to(x[None], (count,) + x.shape), axes, 0, 0,...  14.8 us
    pallas_call x1, Pallas kernels, layer(): pl.pallas_call(layer_kernel, out_shape=jax.ShapeDtypeStruct((rank // 2, 2...  14.7 us
    all_gather x1, blocking collectives, exchange_z(): got = lax.all_gather(sent, 'zh')  12.3 us
    all_to_all x1, waiting for transfers between devices, shards(): in_proj = lax.all_to_all(in_part, PLANE, 0, 0, tiled=True)  12.1 us
    ppermute x7, starting transfers between devices, step(): lax.ppermute(up, 'zl', [(z, z + 1) for z in range(s - 1, ZL - 1)])  11.7 us
    all_to_all x1, blocking collectives, shards(): chain = Chain(lax.all_to_all(quarters, 'y', 0, 0, tiled=True))  11.4 us
  transfers between devices with their start and end apart: 21, of which 11 were waited for; matrix products, arithmetic and copies ran while one was open for 4% of the time, Pallas kernels for 7%

profile of v8, /device:TPU:1, one launch (start us, length us, event | category | flops | bytes accessed | tf_op | source)
XLA Modules:
  0.0 219.4 jit_solution(1321818115696810189)
XLA Ops:
  6.5 3.1 %constant_dynamic-slice_fusion = bf16[240,4096]{1,0:T(8,128)(2,1)} fusion(bf16[480,4096]{1,0:T(8,128)(2,1)} %param.7, s32[]{:T(128)S(6)} %select_n.55), kind=kLoop, calls=%fused_computation.35 | loop fusion | bytes 3932164 | tf_op jit(solution)/shard_map/dynamic_slice | solution.py:250
  9.6 0.0 all-gather.6.cloned.1.call-update
  9.7 0.0 copy-start.3
  9.7 0.9 copy-done.1
  10.6 0.2 copy.14
  10.8 0.2 copy.13
  11.0 11.4 %all_to_all.30.refs_0_ = bf16[4,448,128]{2,1,0:T(8,128)(2,1)S(1)} all-to-all(bf16[4,448,128]{2,1,0:T(8,128)(2,1)S(1)} %pad_maximum_fusion), channel_id=1, replica_groups=mesh['zl'=8,'y'=4,'x'=4,'zh'=2,'c'=2] {'y'}, dimensions={0} | all-to-all | bytes 917504 | tf_op jit(solution)/shard_map/all_to_all | solution.py:257
  22.4 4.5 %collective-permute-start = (bf16[4,448,128]{2,1,0:T(8,128)(2,1)S(1)}, bf16[4,448,128]{2,1,0:T(8,128)(2,1)S(1)}, u32[]{:S(2)}, u32[]{:S(2)}) collective-permute-start(bf16[4,448,128]{2,1,0:T(8,128)(2,1)S(1)} %all_to_all.30.refs_0_), channel_id=1, source_target_pairs={{0,64},{64,128},{128,192},{192,256},{256,320},{320,384},{384,448},... | collective-permute-start | bytes 1376264 | tf_op jit(solution)/shard_map/ppermute | solution.py:189
  26.9 1.3 collective-permute-start.2
  28.2 6.3 %collective-permute-done.refs_1_ = bf16[4,448,128]{2,1,0:T(8,128)(2,1)S(1)} collective-permute-done((bf16[4,448,128]{2,1,0:T(8,128)(2,1)S(1)}, bf16[4,448,128]{2,1,0:T(8,128)(2,1)S(1)}, u32[]{:S(2)}, u32[]{:S(2)}) %collective-permute-start) | collective-permute-done | bytes 458784 | tf_op jit(solution)/shard_map/ppermute | solution.py:189
  34.5 0.7 collective-permute-start.1
  35.2 3.6 %collective-permute-done.2.refs_8_ = bf16[4,448,128]{2,1,0:T(8,128)(2,1)S(1)} collective-permute-done((bf16[4,448,128]{2,1,0:T(8,128)(2,1)S(1)}, bf16[4,448,128]{2,1,0:T(8,128)(2,1)S(1)}, u32[]{:S(2)}, u32[]{:S(2)}) %collective-permute-start.2) | collective-permute-done | bytes 458784 | tf_op jit(solution)/shard_map/ppermute | solution.py:190
  38.8 1.3 collective-permute-start.4
  40.1 0.0 collective-permute-done.1.refs_2_
  40.1 0.7 collective-permute-start.3
  40.8 9.3 %collective-permute-done.4.refs_9_ = bf16[4,448,128]{2,1,0:T(8,128)(2,1)S(1)} collective-permute-done((bf16[4,448,128]{2,1,0:T(8,128)(2,1)S(1)}, bf16[4,448,128]{2,1,0:T(8,128)(2,1)S(1)}, u32[]{:S(2)}, u32[]{:S(2)}) %collective-permute-start.4) | collective-permute-done | bytes 458784 | tf_op jit(solution)/shard_map/ppermute | solution.py:190
  50.1 1.3 collective-permute-start.6
  51.4 0.0 collective-permute-done.3.refs_3_
  51.4 1.4 collective-permute-start.5
  52.9 9.7 %collective-permute-done.6.refs_10_ = bf16[4,448,128]{2,1,0:T(8,128)(2,1)S(1)} collective-permute-done((bf16[4,448,128]{2,1,0:T(8,128)(2,1)S(1)}, bf16[4,448,128]{2,1,0:T(8,128)(2,1)S(1)}, u32[]{:S(2)}, u32[]{:S(2)}) %collective-permute-start.6) | collective-permute-done | bytes 458784 | tf_op jit(solution)/shard_map/ppermute | solution.py:190
  62.6 1.3 collective-permute-start.8
  63.9 0.0 collective-permute-done.5.refs_4_
  63.9 1.4 collective-permute-start.7
  65.3 7.4 %collective-permute-done.8.refs_11_ = bf16[4,448,128]{2,1,0:T(8,128)(2,1)} collective-permute-done((bf16[4,448,128]{2,1,0:T(8,128)(2,1)S(1)}, bf16[4,448,128]{2,1,0:T(8,128)(2,1)}, u32[]{:S(2)}, u32[]{:S(2)}) %collective-permute-start.8) | collective-permute-done | bytes 458784 | tf_op jit(solution)/shard_map/ppermute | solution.py:190
  72.8 1.3 collective-permute-start.10
  74.1 1.0 pad.9
  75.0 0.9 convolution_bitcast_fusion
  75.9 9.4 %all-to-all-start.1 = ((f32[8,8,512]{2,1,0:T(8,128)}), f32[8,8,512]{2,1,0:T(8,128)S(1)}, u32[]{:S(2)}, u32[]{:S(2)}) async-start(f32[8,8,512]{2,1,0:T(8,128)} %convolution_bitcast_fusion), calls=%async_computation.1 | async-start | bytes 262144 | tf_op jit(solution)/shard_map/all_to_all | solution.py:263
  85.3 5.3 %all-to-all-done.1 = f32[8,8,512]{2,1,0:T(8,128)S(1)} async-done(((f32[8,8,512]{2,1,0:T(8,128)}), f32[8,8,512]{2,1,0:T(8,128)S(1)}, u32[]{:S(2)}, u32[]{:S(2)}) %all-to-all-start.1) | async-done | bytes 131104 | tf_op jit(solution)/shard_map/all_to_all | solution.py:263
  90.6 1.5 collective-permute-start.9
  92.1 1.3 collective-permute-start.12
  93.4 12.3 %all-gather = bf16[64,512]{1,0:T(8,128)(2,1)S(1)} all-gather(bf16[32,512]{1,0:T(8,128)(2,1)S(1)} %pad_maximum_fusion.2), channel_id=2, replica_groups=mesh['zl'=8,'y'=4,'x'=4,'zh'=2,'c'=2] {'zh'}, dimensions={0}, use_global_device_ids=true | all-gather | bytes 98304 | tf_op jit(solution)/shard_map/all_gather | solution.py:222
  105.7 0.6 pad_maximum_fusion.1
  106.3 0.0 all-gather.8.cloned.1.call-update
  106.4 0.0 collective-permute-done.9.refs_6_
  106.4 0.0 all-gather.6.cloned.1.call-done
  106.4 1.5 collective-permute-start.11
  107.9 1.3 collective-permute-start.13
  109.2 0.1 dynamic-slice_bitcast_fusion.1
  109.3 0.9 broadcast_in_dim.46
  110.2 6.2 %all-to-all-start.3 = ((f32[32,8,512]{2,1,0:T(8,128)}), f32[32,8,512]{2,1,0:T(8,128)}, u32[]{:S(2)}, u32[]{:S(2)}) async-start(f32[32,8,512]{2,1,0:T(8,128)} %broadcast_in_dim.46), calls=%async_computation.3 | async-start | bytes 1048576 | tf_op jit(solution)/shard_map/all_to_all | solution.py:88
  116.3 15.4 %collective-permute-done.13.refs_14_ = bf16[4,448,128]{2,1,0:T(8,128)(2,1)} collective-permute-done((bf16[4,448,128]{2,1,0:T(8,128)(2,1)}, bf16[4,448,128]{2,1,0:T(8,128)(2,1)}, u32[]{:S(2)}, u32[]{:S(2)}) %collective-permute-start.13) | collective-permute-done | bytes 458784 | tf_op jit(solution)/shard_map/ppermute | solution.py:190
  131.7 14.7 %layer.1 = f32[32,2,2048]{2,1,0:T(2,128)} custom-call(s32[1]{0:T(128)} %bitcast.place_ref, bf16[64,256]{1,0:T(8,128)(2,1)S(1)} %pad.8.factor_ref, bf16[4,448,128]{2,1,0:T(8,128)(2,1)S(1)} %all_to_all.30.refs_0_, bf16[4,448,128]{2,1,0:T(8,128)(2,1)S(1)} %collective-permute-done.refs_1_, bf16[4,448,128]{2,1,0:T(8,128)(2,1)S(1)} %collective-permute-done.1.refs_2_, ...), custom_call_target="tpu_custom_call" | custom-call | flops 7046430720 | bytes 19398656 | tf_op jit(solution)/shard_map/layer/pallas_call | solution.py:154
  146.5 0.0 all-to-all-done.3
  146.5 5.9 %all-to-all-start.2 = ((f32[32,2,2048]{2,1,0:T(2,128)}), f32[32,2,2048]{2,1,0:T(2,128)S(1)}, u32[]{:S(2)}, u32[]{:S(2)}) async-start(f32[32,2,2048]{2,1,0:T(2,128)} %layer.1), calls=%async_computation.2 | async-start | bytes 1048576 | tf_op jit(solution)/shard_map/all_to_all | solution.py:277
  152.4 1.1 copy.17
  153.5 12.1 %all-to-all-done.2 = f32[32,2,2048]{2,1,0:T(2,128)S(1)} async-done(((f32[32,2,2048]{2,1,0:T(2,128)}), f32[32,2,2048]{2,1,0:T(2,128)S(1)}, u32[]{:S(2)}, u32[]{:S(2)}) %all-to-all-start.2) | async-done | bytes 524320 | tf_op jit(solution)/shard_map/all_to_all | solution.py:277
  165.6 0.2 reduce_sum.38
  165.8 0.1 broadcast_select_fusion
  165.9 0.1 select_n.57
  166.0 0.5 convolution_multiply_fusion
  166.5 0.1 broadcast_in_dim.47
  166.6 0.7 broadcast_in_dim.48
  167.3 3.5 %all-to-all-start.4 = ((f32[16,12,128]{2,1,0:T(8,128)}), f32[16,12,128]{2,1,0:T(8,128)S(1)}, u32[]{:S(2)}, u32[]{:S(2)}) async-start(f32[16,12,128]{2,1,0:T(8,128)} %broadcast_in_dim.48), calls=%async_computation.4 | async-start | bytes 262144 | tf_op jit(solution)/shard_map/all_to_all | solution.py:88
  170.8 1.4 all-gather.8.cloned.1.call-done
  172.2 11.2 %all-to-all-done.4 = f32[16,12,128]{2,1,0:T(8,128)S(1)} async-done(((f32[16,12,128]{2,1,0:T(8,128)}), f32[16,12,128]{2,1,0:T(8,128)S(1)}, u32[]{:S(2)}, u32[]{:S(2)}) %all-to-all-start.4) | async-done | bytes 98336 | tf_op jit(solution)/shard_map/all_to_all | solution.py:88
  183.4 1.0 broadcast_in_dim.49
  184.4 5.1 %all-to-all-start.5 = ((bf16[32,96,128]{2,1,0:T(8,128)(2,1)}), bf16[32,96,128]{2,1,0:T(8,128)(2,1)S(1)}, u32[]{:S(2)}, u32[]{:S(2)}) async-start(bf16[32,96,128]{2,1,0:T(8,128)(2,1)} %broadcast_in_dim.49), calls=%async_computation.5 | async-start | bytes 1572864 | tf_op jit(solution)/shard_map/all_to_all | solution.py:88
  189.5 1.0 dynamic-slice_bitcast_fusion
  190.6 0.1 reshape.112
  190.7 0.3 copy.16
  190.9 0.2 reshape.113.queries_ref
  191.1 12.6 %all-to-all-done.5.features_ref = bf16[32,96,128]{2,1,0:T(8,128)(2,1)S(1)} async-done(((bf16[32,96,128]{2,1,0:T(8,128)(2,1)}), bf16[32,96,128]{2,1,0:T(8,128)(2,1)S(1)}, u32[]{:S(2)}, u32[]{:S(2)}) %all-to-all-start.5) | async-done | bytes 786464 | tf_op jit(solution)/shard_map/all_to_all | solution.py:88
  203.7 8.8 %solve.1 = f32[32,96]{1,0:T(8,128)} custom-call(bf16[32,96,128]{2,1,0:T(8,128)(2,1)S(1)} %all-to-all-done.5.features_ref, bf16[32,4096]{1,0:T(8,128)(2,1)S(1)} %reshape.113.queries_ref), custom_call_target="tpu_custom_call" | custom-call | tf_op jit(solution)/shard_map/solve/pallas_call | solution.py:79
  (28 shorter events, 0.2 us)
Async XLA Ops:
  6.5 102.6 %copy-start = (bf16[896,64]{0,1:T(8,128)(2,1)S(1)}, bf16[896,64]{0,1:T(8,128)(2,1)}, u32[]{:S(2)}) copy-start(bf16[896,64]{0,1:T(8,128)(2,1)} %param.11) | copy-start | bytes 344068
  6.5 99.9 %all-gather.6.cloned.1.call-start = ((), (), s32[]{:S(2)}) async-start(), calls=%async_computation.6 | async-start | bytes 17694720 | tf_op jit(solution)/shard_map/all_gather | solution.py:251
  9.6 0.9 copy-start.1
  9.6 1.1 copy-start.2
  9.7 65.4 %copy-start.3 = (bf16[256,64]{0,1:T(8,128)(2,1)S(1)}, bf16[256,64]{0,1:T(8,128)(2,1)}, u32[]{:S(2)}) copy-start(bf16[256,64]{0,1:T(8,128)(2,1)} %param.12) | copy-start | bytes 98308
  10.6 74.7 %copy-start.4 = (bf16[32,256]{1,0:T(8,128)(2,1)S(1)}, bf16[32,256]{1,0:T(8,128)(2,1)}, u32[]{:S(2)}) copy-start(bf16[32,256]{1,0:T(8,128)(2,1)} %param.13) | copy-start | bytes 49156
  22.4 12.2 %collective-permute-start = (bf16[4,448,128]{2,1,0:T(8,128)(2,1)S(1)}, bf16[4,448,128]{2,1,0:T(8,128)(2,1)S(1)}, u32[]{:S(2)}, u32[]{:S(2)}) collective-permute-start(bf16[4,448,128]{2,1,0:T(8,128)(2,1)S(1)} %all_to_all.30.refs_0_), channel_id=1, source_target_pairs={{0,64},{64,128},{128,192},{192,256},{256,320},{320,384},{384,448},... | collective-permute-start | bytes 1376264 | tf_op jit(solution)/shard_map/ppermute | solution.py:189
  26.9 11.9 %collective-permute-start.2 = (bf16[4,448,128]{2,1,0:T(8,128)(2,1)S(1)}, bf16[4,448,128]{2,1,0:T(8,128)(2,1)S(1)}, u32[]{:S(2)}, u32[]{:S(2)}) collective-permute-start(bf16[4,448,128]{2,1,0:T(8,128)(2,1)S(1)} %all_to_all.30.refs_0_), channel_id=1, source_target_pairs={{64,0},{128,64},{192,128},{256,192},{320,256},{384,320},{448,384},... | collective-permute-start | bytes 1376264 | tf_op jit(solution)/shard_map/ppermute | solution.py:190
  34.5 5.6 %collective-permute-start.1 = (bf16[4,448,128]{2,1,0:T(8,128)(2,1)S(1)}, bf16[4,448,128]{2,1,0:T(8,128)(2,1)S(1)}, u32[]{:S(2)}, u32[]{:S(2)}) collective-permute-start(bf16[4,448,128]{2,1,0:T(8,128)(2,1)S(1)} %collective-permute-done.refs_1_), channel_id=1, source_target_pairs={{64,128},{128,192},{192,256},{256,320},{320,384},{384,448},{65,129... | collective-permute-start | bytes 1376264 | tf_op jit(solution)/shard_map/ppermute | solution.py:189
  38.8 11.3 %collective-permute-start.4 = (bf16[4,448,128]{2,1,0:T(8,128)(2,1)S(1)}, bf16[4,448,128]{2,1,0:T(8,128)(2,1)S(1)}, u32[]{:S(2)}, u32[]{:S(2)}) collective-permute-start(bf16[4,448,128]{2,1,0:T(8,128)(2,1)S(1)} %collective-permute-done.2.refs_8_), channel_id=1, source_target_pairs={{64,0},{128,64},{192,128},{256,192},{320,256},{384,320},{65,1},{12... | collective-permute-start | bytes 1376264 | tf_op jit(solution)/shard_map/ppermute | solution.py:190
  40.1 11.3 %collective-permute-start.3 = (bf16[4,448,128]{2,1,0:T(8,128)(2,1)S(1)}, bf16[4,448,128]{2,1,0:T(8,128)(2,1)S(1)}, u32[]{:S(2)}, u32[]{:S(2)}) collective-permute-start(bf16[4,448,128]{2,1,0:T(8,128)(2,1)S(1)} %collective-permute-done.1.refs_2_), channel_id=1, source_target_pairs={{128,192},{192,256},{256,320},{320,384},{384,448},{129,193},{193,2... | collective-permute-start | bytes 1376264 | tf_op jit(solution)/shard_map/ppermute | solution.py:189
  50.1 12.5 %collective-permute-start.6 = (bf16[4,448,128]{2,1,0:T(8,128)(2,1)S(1)}, bf16[4,448,128]{2,1,0:T(8,128)(2,1)S(1)}, u32[]{:S(2)}, u32[]{:S(2)}) collective-permute-start(bf16[4,448,128]{2,1,0:T(8,128)(2,1)S(1)} %collective-permute-done.4.refs_9_), channel_id=1, source_target_pairs={{64,0},{128,64},{192,128},{256,192},{320,256},{65,1},{129,65},{193... | collective-permute-start | bytes 1376264 | tf_op jit(solution)/shard_map/ppermute | solution.py:190
  51.4 12.5 %collective-permute-start.5 = (bf16[4,448,128]{2,1,0:T(8,128)(2,1)S(1)}, bf16[4,448,128]{2,1,0:T(8,128)(2,1)}, u32[]{:S(2)}, u32[]{:S(2)}) collective-permute-start(bf16[4,448,128]{2,1,0:T(8,128)(2,1)S(1)} %collective-permute-done.3.refs_3_), channel_id=1, source_target_pairs={{192,256},{256,320},{320,384},{384,448},{193,257},{257,321},{321,3... | collective-permute-start | bytes 1376264 | tf_op jit(solution)/shard_map/ppermute | solution.py:189
  62.6 10.2 %collective-permute-start.8 = (bf16[4,448,128]{2,1,0:T(8,128)(2,1)S(1)}, bf16[4,448,128]{2,1,0:T(8,128)(2,1)}, u32[]{:S(2)}, u32[]{:S(2)}) collective-permute-start(bf16[4,448,128]{2,1,0:T(8,128)(2,1)S(1)} %collective-permute-done.6.refs_10_), channel_id=1, source_target_pairs={{64,0},{128,64},{192,128},{256,192},{65,1},{129,65},{193,129},{257... | collective-permute-start | bytes 1376264 | tf_op jit(solution)/shard_map/ppermute | solution.py:190
  63.9 26.7 %collective-permute-start.7 = (bf16[4,448,128]{2,1,0:T(8,128)(2,1)}, bf16[4,448,128]{2,1,0:T(8,128)(2,1)}, u32[]{:S(2)}, u32[]{:S(2)}) collective-permute-start(bf16[4,448,128]{2,1,0:T(8,128)(2,1)} %collective-permute-done.5.refs_4_), channel_id=1, source_target_pairs={{256,320},{320,384},{384,448},{257,321},{321,385},{385,449},{258,3... | collective-permute-start | bytes 1376264 | tf_op jit(solution)/shard_map/ppermute | solution.py:189
  72.8 19.3 %collective-permute-start.10 = (bf16[4,448,128]{2,1,0:T(8,128)(2,1)}, bf16[4,448,128]{2,1,0:T(8,128)(2,1)}, u32[]{:S(2)}, u32[]{:S(2)}) collective-permute-start(bf16[4,448,128]{2,1,0:T(8,128)(2,1)} %collective-permute-done.8.refs_11_), channel_id=1, source_target_pairs={{64,0},{128,64},{192,128},{65,1},{129,65},{193,129},{66,2},{130,66... | collective-permute-start | bytes 1376264 | tf_op jit(solution)/shard_map/ppermute | solution.py:190
  75.9 14.7 %all-to-all-start.1 = ((f32[8,8,512]{2,1,0:T(8,128)}), f32[8,8,512]{2,1,0:T(8,128)S(1)}, u32[]{:S(2)}, u32[]{:S(2)}) async-start(f32[8,8,512]{2,1,0:T(8,128)} %convolution_bitcast_fusion), calls=%async_computation.1 | async-start | bytes 262144 | tf_op jit(solution)/shard_map/all_to_all | solution.py:263
  85.3 86.9 %all-gather.8.cloned.1.call-start = ((), (), s32[]{:S(2)}) async-start(), calls=%async_computation.7 | async-start | bytes 1622016 | tf_op jit(solution)/shard_map/all_gather | solution.py:235
  90.6 15.8 %collective-permute-start.9 = (bf16[4,448,128]{2,1,0:T(8,128)(2,1)}, bf16[4,448,128]{2,1,0:T(8,128)(2,1)}, u32[]{:S(2)}, u32[]{:S(2)}) collective-permute-start(bf16[4,448,128]{2,1,0:T(8,128)(2,1)} %collective-permute-done.7.refs_5_), channel_id=1, source_target_pairs={{320,384},{384,448},{321,385},{385,449},{322,386},{386,450},{323,3... | collective-permute-start | bytes 1376264 | tf_op jit(solution)/shard_map/ppermute | solution.py:189
  92.1 15.8 %collective-permute-start.12 = (bf16[4,448,128]{2,1,0:T(8,128)(2,1)}, bf16[4,448,128]{2,1,0:T(8,128)(2,1)}, u32[]{:S(2)}, u32[]{:S(2)}) collective-permute-start(bf16[4,448,128]{2,1,0:T(8,128)(2,1)} %collective-permute-done.10.refs_12_), channel_id=1, source_target_pairs={{64,0},{128,64},{65,1},{129,65},{66,2},{130,66},{67,3},{131,67},{6... | collective-permute-start | bytes 1376264 | tf_op jit(solution)/shard_map/ppermute | solution.py:190
  106.4 9.9 %collective-permute-start.11 = (bf16[4,448,128]{2,1,0:T(8,128)(2,1)}, bf16[4,448,128]{2,1,0:T(8,128)(2,1)}, u32[]{:S(2)}, u32[]{:S(2)}) collective-permute-start(bf16[4,448,128]{2,1,0:T(8,128)(2,1)} %collective-permute-done.9.refs_6_), channel_id=1, source_target_pairs={{384,448},{385,449},{386,450},{387,451},{388,452},{389,453},{390,4... | collective-permute-start | bytes 1376264 | tf_op jit(solution)/shard_map/ppermute | solution.py:189
  107.9 23.9 %collective-permute-start.13 = (bf16[4,448,128]{2,1,0:T(8,128)(2,1)}, bf16[4,448,128]{2,1,0:T(8,128)(2,1)}, u32[]{:S(2)}, u32[]{:S(2)}) collective-permute-start(bf16[4,448,128]{2,1,0:T(8,128)(2,1)} %collective-permute-done.12.refs_13_), channel_id=1, source_target_pairs={{64,0},{65,1},{66,2},{67,3},{68,4},{69,5},{70,6},{71,7},{72,8},{73... | collective-permute-start | bytes 1376264 | tf_op jit(solution)/shard_map/ppermute | solution.py:190
  110.2 36.3 %all-to-all-start.3 = ((f32[32,8,512]{2,1,0:T(8,128)}), f32[32,8,512]{2,1,0:T(8,128)}, u32[]{:S(2)}, u32[]{:S(2)}) async-start(f32[32,8,512]{2,1,0:T(8,128)} %broadcast_in_dim.46), calls=%async_computation.3 | async-start | bytes 1048576 | tf_op jit(solution)/shard_map/all_to_all | solution.py:88
  146.5 19.1 %all-to-all-start.2 = ((f32[32,2,2048]{2,1,0:T(2,128)}), f32[32,2,2048]{2,1,0:T(2,128)S(1)}, u32[]{:S(2)}, u32[]{:S(2)}) async-start(f32[32,2,2048]{2,1,0:T(2,128)} %layer.1), calls=%async_computation.2 | async-start | bytes 1048576 | tf_op jit(solution)/shard_map/all_to_all | solution.py:277
  167.3 16.1 %all-to-all-start.4 = ((f32[16,12,128]{2,1,0:T(8,128)}), f32[16,12,128]{2,1,0:T(8,128)S(1)}, u32[]{:S(2)}, u32[]{:S(2)}) async-start(f32[16,12,128]{2,1,0:T(8,128)} %broadcast_in_dim.48), calls=%async_computation.4 | async-start | bytes 262144 | tf_op jit(solution)/shard_map/all_to_all | solution.py:88
  184.4 19.3 %all-to-all-start.5 = ((bf16[32,96,128]{2,1,0:T(8,128)(2,1)}), bf16[32,96,128]{2,1,0:T(8,128)(2,1)S(1)}, u32[]{:S(2)}, u32[]{:S(2)}) async-start(bf16[32,96,128]{2,1,0:T(8,128)(2,1)} %broadcast_in_dim.49), calls=%async_computation.5 | async-start | bytes 1572864 | tf_op jit(solution)/shard_map/all_to_all | solution.py:88
Sparse Core Ops, SparseCore 0:
  9.8 93.9 all-gather.5
  106.9 65.2 all-gather.7

commit v9 on v8

--- a/solution.py
+++ b/solution.py
@@ -98,13 +98,17 @@
     hidden = blocks[0].shape[1] // 2
     half = all_tokens.shape[1]
 
+    parts, pieces = token_sems.shape
+
     def token_copies(p):
-        for c in range(2):
+        for c in range(pieces):
             yield pltpu.make_async_copy(
-                all_tokens.at[2 * p + c], tokens.at[p, pl.ds(c * half, half)], token_sems.at[p, c]
+                all_tokens.at[pieces * p + c],
+                tokens.at[p, pl.ds(c * half, half)],
+                token_sems.at[p, c],
             )
 
-    for p in range(Y):
+    for p in range(parts):
         for copy in token_copies(p):
             copy.start()
 
@@ -137,13 +141,16 @@
             preferred_element_type=jnp.float32,
         )
         space = jnp.zeros((proj.shape[0], 256 - half), jnp.float32)
-        proj = jnp.concatenate([proj[:, :half], space, proj[:, half:], space], axis=1)
-        lanes = pl.ds(pl.multiple_of(p * 512, 512), 512)
+        spread = []
+        for c in range(pieces):
+            spread += [proj[:, c * half : (c + 1) * half], space]
+        proj = jnp.concatenate(spread, axis=1)
+        lanes = pl.ds(pl.multiple_of(p * (256 * pieces), 256), 256 * pieces)
         for d in range(out_ref.shape[0]):
             out_ref[d, :, lanes] = proj[2 * d : 2 * d + 2]
         return carry
 
-    lax.fori_loop(0, Y, part, 0)
+    lax.fori_loop(0, parts, part, 0)
 
 
 def layer(place, factor, blocks, tokens):
@@ -160,8 +167,8 @@
         out_specs=vmem,
         scratch_shapes=[
             pltpu.VMEM((depth, 512), jnp.bfloat16),
-            pltpu.VMEM((Y, 2 * half, depth), jnp.bfloat16),
-            pltpu.SemaphoreType.DMA((Y, 2)),
+            pltpu.VMEM((Y // 2, 4 * half, depth), jnp.bfloat16),
+            pltpu.SemaphoreType.DMA((Y // 2, 4)),
         ],
         compiler_params=pltpu.CompilerParams(vmem_limit_bytes=38 * 2**20),
         cost_estimate=pl.CostEstimate(

time: 221 us -> 221 us (level)
  no operation moved by 1% of the time
where the time goes in v9:
time: 221 us; the launch traced here: 220 us
  waiting for transfers between devices  94.5 us (43%)
  starting transfers between devices  50.7 us (23%)
  Pallas kernels  23.9 us (11%)
  blocking collectives  23.7 us (11%)
  between operations  13.8 us (6%)
  local copies, waits for them, and re-layouts  10.8 us (5%)
    ppermute x7, waiting for transfers between devices, step(): lax.ppermute(down, 'zl', [(z, z - 1) for z in range(1, ZL + 1 - s)])  45.5 us
    all_to_all x3, waiting for transfers between devices, share(): lax.all_to_all(jnp.broadcast_to(x[None], (count,) + x.shape), axes, 0, 0,...  24.1 us
    pallas_call x1, Pallas kernels, layer(): pl.pallas_call(layer_kernel, out_shape=jax.ShapeDtypeStruct((rank // 2, 2...  15.1 us
    all_to_all x3, starting transfers between devices, share(): lax.all_to_all(jnp.broadcast_to(x[None], (count,) + x.shape), axes, 0, 0,...  14.7 us
    all_gather x1, blocking collectives, exchange_z(): got = lax.all_gather(sent, 'zh')  12.3 us
    all_to_all x1, waiting for transfers between devices, shards(): in_proj = lax.all_to_all(in_part, PLANE, 0, 0, tiled=True)  12.3 us
    ppermute x7, starting transfers between devices, step(): lax.ppermute(up, 'zl', [(z, z + 1) for z in range(s - 1, ZL - 1)])  11.7 us
    all_to_all x1, blocking collectives, shards(): chain = Chain(lax.all_to_all(quarters, 'y', 0, 0, tiled=True))  11.4 us
  transfers between devices with their start and end apart: 21, of which 11 were waited for; matrix products, arithmetic and copies ran while one was open for 4% of the time, Pallas kernels for 7%

profile of v9, /device:TPU:1, one launch (start us, length us, event | category | flops | bytes accessed | tf_op | source)
XLA Modules:
  0.0 219.8 jit_solution(14506138503787545455)
XLA Ops:
  6.5 3.1 %constant_dynamic-slice_fusion = bf16[240,4096]{1,0:T(8,128)(2,1)} fusion(bf16[480,4096]{1,0:T(8,128)(2,1)} %param.7, s32[]{:T(128)S(6)} %select_n.55), kind=kLoop, calls=%fused_computation.35 | loop fusion | bytes 3932164 | tf_op jit(solution)/shard_map/dynamic_slice | solution.py:257
  9.6 0.0 all-gather.6.cloned.1.call-update
  9.7 0.0 copy-start.3
  9.7 0.9 copy-done.1
  10.6 0.2 copy.14
  10.8 0.2 copy.13
  11.0 11.4 %all_to_all.30.refs_0_ = bf16[4,448,128]{2,1,0:T(8,128)(2,1)S(1)} all-to-all(bf16[4,448,128]{2,1,0:T(8,128)(2,1)S(1)} %pad_maximum_fusion), channel_id=1, replica_groups=mesh['zl'=8,'y'=4,'x'=4,'zh'=2,'c'=2] {'y'}, dimensions={0} | all-to-all | bytes 917504 | tf_op jit(solution)/shard_map/all_to_all | solution.py:264
  22.4 4.5 %collective-permute-start = (bf16[4,448,128]{2,1,0:T(8,128)(2,1)S(1)}, bf16[4,448,128]{2,1,0:T(8,128)(2,1)S(1)}, u32[]{:S(2)}, u32[]{:S(2)}) collective-permute-start(bf16[4,448,128]{2,1,0:T(8,128)(2,1)S(1)} %all_to_all.30.refs_0_), channel_id=1, source_target_pairs={{0,64},{64,128},{128,192},{192,256},{256,320},{320,384},{384,448},... | collective-permute-start | bytes 1376264 | tf_op jit(solution)/shard_map/ppermute | solution.py:196
  26.9 1.3 collective-permute-start.2
  28.2 6.3 %collective-permute-done.refs_1_ = bf16[4,448,128]{2,1,0:T(8,128)(2,1)S(1)} collective-permute-done((bf16[4,448,128]{2,1,0:T(8,128)(2,1)S(1)}, bf16[4,448,128]{2,1,0:T(8,128)(2,1)S(1)}, u32[]{:S(2)}, u32[]{:S(2)}) %collective-permute-start) | collective-permute-done | bytes 458784 | tf_op jit(solution)/shard_map/ppermute | solution.py:196
  34.5 0.7 collective-permute-start.1
  35.2 3.6 %collective-permute-done.2.refs_8_ = bf16[4,448,128]{2,1,0:T(8,128)(2,1)S(1)} collective-permute-done((bf16[4,448,128]{2,1,0:T(8,128)(2,1)S(1)}, bf16[4,448,128]{2,1,0:T(8,128)(2,1)S(1)}, u32[]{:S(2)}, u32[]{:S(2)}) %collective-permute-start.2) | collective-permute-done | bytes 458784 | tf_op jit(solution)/shard_map/ppermute | solution.py:197
  38.8 1.3 collective-permute-start.4
  40.1 0.7 collective-permute-start.3
  40.8 9.3 %collective-permute-done.4.refs_9_ = bf16[4,448,128]{2,1,0:T(8,128)(2,1)S(1)} collective-permute-done((bf16[4,448,128]{2,1,0:T(8,128)(2,1)S(1)}, bf16[4,448,128]{2,1,0:T(8,128)(2,1)S(1)}, u32[]{:S(2)}, u32[]{:S(2)}) %collective-permute-start.4) | collective-permute-done | bytes 458784 | tf_op jit(solution)/shard_map/ppermute | solution.py:197
  50.1 1.3 collective-permute-start.6
  51.4 0.0 collective-permute-done.3.refs_3_
  51.4 1.4 collective-permute-start.5
  52.9 9.7 %collective-permute-done.6.refs_10_ = bf16[4,448,128]{2,1,0:T(8,128)(2,1)S(1)} collective-permute-done((bf16[4,448,128]{2,1,0:T(8,128)(2,1)S(1)}, bf16[4,448,128]{2,1,0:T(8,128)(2,1)S(1)}, u32[]{:S(2)}, u32[]{:S(2)}) %collective-permute-start.6) | collective-permute-done | bytes 458784 | tf_op jit(solution)/shard_map/ppermute | solution.py:197
  62.6 1.3 collective-permute-start.8
  63.9 0.0 collective-permute-done.5.refs_4_
  63.9 1.4 collective-permute-start.7
  65.3 7.4 %collective-permute-done.8.refs_11_ = bf16[4,448,128]{2,1,0:T(8,128)(2,1)} collective-permute-done((bf16[4,448,128]{2,1,0:T(8,128)(2,1)S(1)}, bf16[4,448,128]{2,1,0:T(8,128)(2,1)}, u32[]{:S(2)}, u32[]{:S(2)}) %collective-permute-start.8) | collective-permute-done | bytes 458784 | tf_op jit(solution)/shard_map/ppermute | solution.py:197
  72.8 1.3 collective-permute-start.10
  74.1 1.0 pad.9
  75.0 0.9 convolution_bitcast_fusion
  75.9 9.4 %all-to-all-start.1 = ((f32[8,8,512]{2,1,0:T(8,128)}), f32[8,8,512]{2,1,0:T(8,128)S(1)}, u32[]{:S(2)}, u32[]{:S(2)}) async-start(f32[8,8,512]{2,1,0:T(8,128)} %convolution_bitcast_fusion), calls=%async_computation.1 | async-start | bytes 262144 | tf_op jit(solution)/shard_map/all_to_all | solution.py:270
  85.3 5.3 %all-to-all-done.1 = f32[8,8,512]{2,1,0:T(8,128)S(1)} async-done(((f32[8,8,512]{2,1,0:T(8,128)}), f32[8,8,512]{2,1,0:T(8,128)S(1)}, u32[]{:S(2)}, u32[]{:S(2)}) %all-to-all-start.1) | async-done | bytes 131104 | tf_op jit(solution)/shard_map/all_to_all | solution.py:270
  90.6 0.0 collective-permute-done.7.refs_5_
  90.6 1.5 collective-permute-start.9
  92.1 0.0 collective-permute-done.10.refs_12_
  92.1 1.3 collective-permute-start.12
  93.4 12.3 %all-gather = bf16[64,512]{1,0:T(8,128)(2,1)S(1)} all-gather(bf16[32,512]{1,0:T(8,128)(2,1)S(1)} %pad_maximum_fusion.2), channel_id=2, replica_groups=mesh['zl'=8,'y'=4,'x'=4,'zh'=2,'c'=2] {'zh'}, dimensions={0}, use_global_device_ids=true | all-gather | bytes 98304 | tf_op jit(solution)/shard_map/all_gather | solution.py:229
  105.7 0.6 pad_maximum_fusion.1
  106.3 0.0 all-gather.8.cloned.1.call-update
  106.4 0.0 collective-permute-done.9.refs_6_
  106.4 0.0 all-gather.6.cloned.1.call-done
  106.4 1.5 collective-permute-start.11
  107.9 1.3 collective-permute-start.13
  109.2 0.1 dynamic-slice_bitcast_fusion.1
  109.3 0.9 broadcast_in_dim.46
  110.2 6.2 %all-to-all-start.3 = ((f32[32,8,512]{2,1,0:T(8,128)}), f32[32,8,512]{2,1,0:T(8,128)}, u32[]{:S(2)}, u32[]{:S(2)}) async-start(f32[32,8,512]{2,1,0:T(8,128)} %broadcast_in_dim.46), calls=%async_computation.3 | async-start | bytes 1048576 | tf_op jit(solution)/shard_map/all_to_all | solution.py:88
  116.3 15.4 %collective-permute-done.13.refs_14_ = bf16[4,448,128]{2,1,0:T(8,128)(2,1)} collective-permute-done((bf16[4,448,128]{2,1,0:T(8,128)(2,1)}, bf16[4,448,128]{2,1,0:T(8,128)(2,1)}, u32[]{:S(2)}, u32[]{:S(2)}) %collective-permute-start.13) | collective-permute-done | bytes 458784 | tf_op jit(solution)/shard_map/ppermute | solution.py:197
  131.7 15.1 %layer.1 = f32[32,2,2048]{2,1,0:T(2,128)} custom-call(s32[1]{0:T(128)} %bitcast.place_ref, bf16[64,256]{1,0:T(8,128)(2,1)S(1)} %pad.8.factor_ref, bf16[4,448,128]{2,1,0:T(8,128)(2,1)S(1)} %all_to_all.30.refs_0_, bf16[4,448,128]{2,1,0:T(8,128)(2,1)S(1)} %collective-permute-done.refs_1_, bf16[4,448,128]{2,1,0:T(8,128)(2,1)S(1)} %collective-permute-done.1.refs_2_, ...), custom_call_target="tpu_custom_call" | custom-call | flops 7046430720 | bytes 19398656 | tf_op jit(solution)/shard_map/layer/pallas_call | solution.py:161
  146.8 5.9 %all-to-all-start.2 = ((f32[32,2,2048]{2,1,0:T(2,128)}), f32[32,2,2048]{2,1,0:T(2,128)S(1)}, u32[]{:S(2)}, u32[]{:S(2)}) async-start(f32[32,2,2048]{2,1,0:T(2,128)} %layer.1), calls=%async_computation.2 | async-start | bytes 1048576 | tf_op jit(solution)/shard_map/all_to_all | solution.py:284
  152.8 1.1 copy.17
  153.9 12.3 %all-to-all-done.2 = f32[32,2,2048]{2,1,0:T(2,128)S(1)} async-done(((f32[32,2,2048]{2,1,0:T(2,128)}), f32[32,2,2048]{2,1,0:T(2,128)S(1)}, u32[]{:S(2)}, u32[]{:S(2)}) %all-to-all-start.2) | async-done | bytes 524320 | tf_op jit(solution)/shard_map/all_to_all | solution.py:284
  166.1 0.2 reduce_sum.38
  166.3 0.1 broadcast_select_fusion
  166.4 0.1 select_n.57
  166.6 0.5 convolution_multiply_fusion
  167.1 0.1 broadcast_in_dim.47
  167.2 0.7 broadcast_in_dim.48
  167.8 3.5 %all-to-all-start.4 = ((f32[16,12,128]{2,1,0:T(8,128)}), f32[16,12,128]{2,1,0:T(8,128)S(1)}, u32[]{:S(2)}, u32[]{:S(2)}) async-start(f32[16,12,128]{2,1,0:T(8,128)} %broadcast_in_dim.48), calls=%async_computation.4 | async-start | bytes 262144 | tf_op jit(solution)/shard_map/all_to_all | solution.py:88
  171.3 1.0 all-gather.8.cloned.1.call-done
  172.3 11.5 %all-to-all-done.4 = f32[16,12,128]{2,1,0:T(8,128)S(1)} async-done(((f32[16,12,128]{2,1,0:T(8,128)}), f32[16,12,128]{2,1,0:T(8,128)S(1)}, u32[]{:S(2)}, u32[]{:S(2)}) %all-to-all-start.4) | async-done | bytes 98336 | tf_op jit(solution)/shard_map/all_to_all | solution.py:88
  183.9 1.0 broadcast_in_dim.49
  184.9 5.0 %all-to-all-start.5 = ((bf16[32,96,128]{2,1,0:T(8,128)(2,1)}), bf16[32,96,128]{2,1,0:T(8,128)(2,1)S(1)}, u32[]{:S(2)}, u32[]{:S(2)}) async-start(bf16[32,96,128]{2,1,0:T(8,128)(2,1)} %broadcast_in_dim.49), calls=%async_computation.5 | async-start | bytes 1572864 | tf_op jit(solution)/shard_map/all_to_all | solution.py:88
  189.9 1.0 dynamic-slice_bitcast_fusion
  191.0 0.1 reshape.112
  191.1 0.3 copy.16
  191.4 0.2 reshape.113.queries_ref
  191.6 12.6 %all-to-all-done.5.features_ref = bf16[32,96,128]{2,1,0:T(8,128)(2,1)S(1)} async-done(((bf16[32,96,128]{2,1,0:T(8,128)(2,1)}), bf16[32,96,128]{2,1,0:T(8,128)(2,1)S(1)}, u32[]{:S(2)}, u32[]{:S(2)}) %all-to-all-start.5) | async-done | bytes 786464 | tf_op jit(solution)/shard_map/all_to_all | solution.py:88
  204.2 8.8 %solve.1 = f32[32,96]{1,0:T(8,128)} custom-call(bf16[32,96,128]{2,1,0:T(8,128)(2,1)S(1)} %all-to-all-done.5.features_ref, bf16[32,4096]{1,0:T(8,128)(2,1)S(1)} %reshape.113.queries_ref), custom_call_target="tpu_custom_call" | custom-call | tf_op jit(solution)/shard_map/solve/pallas_call | solution.py:79
  (28 shorter events, 0.2 us)
Async XLA Ops:
  6.5 102.6 %copy-start = (bf16[896,64]{0,1:T(8,128)(2,1)S(1)}, bf16[896,64]{0,1:T(8,128)(2,1)}, u32[]{:S(2)}) copy-start(bf16[896,64]{0,1:T(8,128)(2,1)} %param.11) | copy-start | bytes 344068
  6.5 99.9 %all-gather.6.cloned.1.call-start = ((), (), s32[]{:S(2)}) async-start(), calls=%async_computation.6 | async-start | bytes 17694720 | tf_op jit(solution)/shard_map/all_gather | solution.py:258
  9.6 0.9 copy-start.1
  9.6 1.1 copy-start.2
  9.7 65.4 %copy-start.3 = (bf16[256,64]{0,1:T(8,128)(2,1)S(1)}, bf16[256,64]{0,1:T(8,128)(2,1)}, u32[]{:S(2)}) copy-start(bf16[256,64]{0,1:T(8,128)(2,1)} %param.12) | copy-start | bytes 98308
  10.6 74.7 %copy-start.4 = (bf16[32,256]{1,0:T(8,128)(2,1)S(1)}, bf16[32,256]{1,0:T(8,128)(2,1)}, u32[]{:S(2)}) copy-start(bf16[32,256]{1,0:T(8,128)(2,1)} %param.13) | copy-start | bytes 49156
  22.4 12.2 %collective-permute-start = (bf16[4,448,128]{2,1,0:T(8,128)(2,1)S(1)}, bf16[4,448,128]{2,1,0:T(8,128)(2,1)S(1)}, u32[]{:S(2)}, u32[]{:S(2)}) collective-permute-start(bf16[4,448,128]{2,1,0:T(8,128)(2,1)S(1)} %all_to_all.30.refs_0_), channel_id=1, source_target_pairs={{0,64},{64,128},{128,192},{192,256},{256,320},{320,384},{384,448},... | collective-permute-start | bytes 1376264 | tf_op jit(solution)/shard_map/ppermute | solution.py:196
  26.9 11.9 %collective-permute-start.2 = (bf16[4,448,128]{2,1,0:T(8,128)(2,1)S(1)}, bf16[4,448,128]{2,1,0:T(8,128)(2,1)S(1)}, u32[]{:S(2)}, u32[]{:S(2)}) collective-permute-start(bf16[4,448,128]{2,1,0:T(8,128)(2,1)S(1)} %all_to_all.30.refs_0_), channel_id=1, source_target_pairs={{64,0},{128,64},{192,128},{256,192},{320,256},{384,320},{448,384},... | collective-permute-start | bytes 1376264 | tf_op jit(solution)/shard_map/ppermute | solution.py:197
  34.5 5.6 %collective-permute-start.1 = (bf16[4,448,128]{2,1,0:T(8,128)(2,1)S(1)}, bf16[4,448,128]{2,1,0:T(8,128)(2,1)S(1)}, u32[]{:S(2)}, u32[]{:S(2)}) collective-permute-start(bf16[4,448,128]{2,1,0:T(8,128)(2,1)S(1)} %collective-permute-done.refs_1_), channel_id=1, source_target_pairs={{64,128},{128,192},{192,256},{256,320},{320,384},{384,448},{65,129... | collective-permute-start | bytes 1376264 | tf_op jit(solution)/shard_map/ppermute | solution.py:196
  38.8 11.3 %collective-permute-start.4 = (bf16[4,448,128]{2,1,0:T(8,128)(2,1)S(1)}, bf16[4,448,128]{2,1,0:T(8,128)(2,1)S(1)}, u32[]{:S(2)}, u32[]{:S(2)}) collective-permute-start(bf16[4,448,128]{2,1,0:T(8,128)(2,1)S(1)} %collective-permute-done.2.refs_8_), channel_id=1, source_target_pairs={{64,0},{128,64},{192,128},{256,192},{320,256},{384,320},{65,1},{12... | collective-permute-start | bytes 1376264 | tf_op jit(solution)/shard_map/ppermute | solution.py:197
  40.1 11.3 %collective-permute-start.3 = (bf16[4,448,128]{2,1,0:T(8,128)(2,1)S(1)}, bf16[4,448,128]{2,1,0:T(8,128)(2,1)S(1)}, u32[]{:S(2)}, u32[]{:S(2)}) collective-permute-start(bf16[4,448,128]{2,1,0:T(8,128)(2,1)S(1)} %collective-permute-done.1.refs_2_), channel_id=1, source_target_pairs={{128,192},{192,256},{256,320},{320,384},{384,448},{129,193},{193,2... | collective-permute-start | bytes 1376264 | tf_op jit(solution)/shard_map/ppermute | solution.py:196
  50.1 12.5 %collective-permute-start.6 = (bf16[4,448,128]{2,1,0:T(8,128)(2,1)S(1)}, bf16[4,448,128]{2,1,0:T(8,128)(2,1)S(1)}, u32[]{:S(2)}, u32[]{:S(2)}) collective-permute-start(bf16[4,448,128]{2,1,0:T(8,128)(2,1)S(1)} %collective-permute-done.4.refs_9_), channel_id=1, source_target_pairs={{64,0},{128,64},{192,128},{256,192},{320,256},{65,1},{129,65},{193... | collective-permute-start | bytes 1376264 | tf_op jit(solution)/shard_map/ppermute | solution.py:197
  51.4 12.5 %collective-permute-start.5 = (bf16[4,448,128]{2,1,0:T(8,128)(2,1)S(1)}, bf16[4,448,128]{2,1,0:T(8,128)(2,1)}, u32[]{:S(2)}, u32[]{:S(2)}) collective-permute-start(bf16[4,448,128]{2,1,0:T(8,128)(2,1)S(1)} %collective-permute-done.3.refs_3_), channel_id=1, source_target_pairs={{192,256},{256,320},{320,384},{384,448},{193,257},{257,321},{321,3... | collective-permute-start | bytes 1376264 | tf_op jit(solution)/shard_map/ppermute | solution.py:196
  62.6 10.2 %collective-permute-start.8 = (bf16[4,448,128]{2,1,0:T(8,128)(2,1)S(1)}, bf16[4,448,128]{2,1,0:T(8,128)(2,1)}, u32[]{:S(2)}, u32[]{:S(2)}) collective-permute-start(bf16[4,448,128]{2,1,0:T(8,128)(2,1)S(1)} %collective-permute-done.6.refs_10_), channel_id=1, source_target_pairs={{64,0},{128,64},{192,128},{256,192},{65,1},{129,65},{193,129},{257... | collective-permute-start | bytes 1376264 | tf_op jit(solution)/shard_map/ppermute | solution.py:197
  63.9 26.7 %collective-permute-start.7 = (bf16[4,448,128]{2,1,0:T(8,128)(2,1)}, bf16[4,448,128]{2,1,0:T(8,128)(2,1)}, u32[]{:S(2)}, u32[]{:S(2)}) collective-permute-start(bf16[4,448,128]{2,1,0:T(8,128)(2,1)} %collective-permute-done.5.refs_4_), channel_id=1, source_target_pairs={{256,320},{320,384},{384,448},{257,321},{321,385},{385,449},{258,3... | collective-permute-start | bytes 1376264 | tf_op jit(solution)/shard_map/ppermute | solution.py:196
  72.8 19.3 %collective-permute-start.10 = (bf16[4,448,128]{2,1,0:T(8,128)(2,1)}, bf16[4,448,128]{2,1,0:T(8,128)(2,1)}, u32[]{:S(2)}, u32[]{:S(2)}) collective-permute-start(bf16[4,448,128]{2,1,0:T(8,128)(2,1)} %collective-permute-done.8.refs_11_), channel_id=1, source_target_pairs={{64,0},{128,64},{192,128},{65,1},{129,65},{193,129},{66,2},{130,66... | collective-permute-start | bytes 1376264 | tf_op jit(solution)/shard_map/ppermute | solution.py:197
  75.9 14.7 %all-to-all-start.1 = ((f32[8,8,512]{2,1,0:T(8,128)}), f32[8,8,512]{2,1,0:T(8,128)S(1)}, u32[]{:S(2)}, u32[]{:S(2)}) async-start(f32[8,8,512]{2,1,0:T(8,128)} %convolution_bitcast_fusion), calls=%async_computation.1 | async-start | bytes 262144 | tf_op jit(solution)/shard_map/all_to_all | solution.py:270
  85.3 87.1 %all-gather.8.cloned.1.call-start = ((), (), s32[]{:S(2)}) async-start(), calls=%async_computation.7 | async-start | bytes 1622016 | tf_op jit(solution)/shard_map/all_gather | solution.py:242
  90.6 15.8 %collective-permute-start.9 = (bf16[4,448,128]{2,1,0:T(8,128)(2,1)}, bf16[4,448,128]{2,1,0:T(8,128)(2,1)}, u32[]{:S(2)}, u32[]{:S(2)}) collective-permute-start(bf16[4,448,128]{2,1,0:T(8,128)(2,1)} %collective-permute-done.7.refs_5_), channel_id=1, source_target_pairs={{320,384},{384,448},{321,385},{385,449},{322,386},{386,450},{323,3... | collective-permute-start | bytes 1376264 | tf_op jit(solution)/shard_map/ppermute | solution.py:196
  92.1 15.8 %collective-permute-start.12 = (bf16[4,448,128]{2,1,0:T(8,128)(2,1)}, bf16[4,448,128]{2,1,0:T(8,128)(2,1)}, u32[]{:S(2)}, u32[]{:S(2)}) collective-permute-start(bf16[4,448,128]{2,1,0:T(8,128)(2,1)} %collective-permute-done.10.refs_12_), channel_id=1, source_target_pairs={{64,0},{128,64},{65,1},{129,65},{66,2},{130,66},{67,3},{131,67},{6... | collective-permute-start | bytes 1376264 | tf_op jit(solution)/shard_map/ppermute | solution.py:197
  106.4 9.9 %collective-permute-start.11 = (bf16[4,448,128]{2,1,0:T(8,128)(2,1)}, bf16[4,448,128]{2,1,0:T(8,128)(2,1)}, u32[]{:S(2)}, u32[]{:S(2)}) collective-permute-start(bf16[4,448,128]{2,1,0:T(8,128)(2,1)} %collective-permute-done.9.refs_6_), channel_id=1, source_target_pairs={{384,448},{385,449},{386,450},{387,451},{388,452},{389,453},{390,4... | collective-permute-start | bytes 1376264 | tf_op jit(solution)/shard_map/ppermute | solution.py:196
  107.9 23.9 %collective-permute-start.13 = (bf16[4,448,128]{2,1,0:T(8,128)(2,1)}, bf16[4,448,128]{2,1,0:T(8,128)(2,1)}, u32[]{:S(2)}, u32[]{:S(2)}) collective-permute-start(bf16[4,448,128]{2,1,0:T(8,128)(2,1)} %collective-permute-done.12.refs_13_), channel_id=1, source_target_pairs={{64,0},{65,1},{66,2},{67,3},{68,4},{69,5},{70,6},{71,7},{72,8},{73... | collective-permute-start | bytes 1376264 | tf_op jit(solution)/shard_map/ppermute | solution.py:197
  110.2 36.7 %all-to-all-start.3 = ((f32[32,8,512]{2,1,0:T(8,128)}), f32[32,8,512]{2,1,0:T(8,128)}, u32[]{:S(2)}, u32[]{:S(2)}) async-start(f32[32,8,512]{2,1,0:T(8,128)} %broadcast_in_dim.46), calls=%async_computation.3 | async-start | bytes 1048576 | tf_op jit(solution)/shard_map/all_to_all | solution.py:88
  146.8 19.3 %all-to-all-start.2 = ((f32[32,2,2048]{2,1,0:T(2,128)}), f32[32,2,2048]{2,1,0:T(2,128)S(1)}, u32[]{:S(2)}, u32[]{:S(2)}) async-start(f32[32,2,2048]{2,1,0:T(2,128)} %layer.1), calls=%async_computation.2 | async-start | bytes 1048576 | tf_op jit(solution)/shard_map/all_to_all | solution.py:284
  167.8 16.0 %all-to-all-start.4 = ((f32[16,12,128]{2,1,0:T(8,128)}), f32[16,12,128]{2,1,0:T(8,128)S(1)}, u32[]{:S(2)}, u32[]{:S(2)}) async-start(f32[16,12,128]{2,1,0:T(8,128)} %broadcast_in_dim.48), calls=%async_computation.4 | async-start | bytes 262144 | tf_op jit(solution)/shard_map/all_to_all | solution.py:88
  184.9 19.3 %all-to-all-start.5 = ((bf16[32,96,128]{2,1,0:T(8,128)(2,1)}), bf16[32,96,128]{2,1,0:T(8,128)(2,1)S(1)}, u32[]{:S(2)}, u32[]{:S(2)}) async-start(bf16[32,96,128]{2,1,0:T(8,128)(2,1)} %broadcast_in_dim.49), calls=%async_computation.5 | async-start | bytes 1572864 | tf_op jit(solution)/shard_map/all_to_all | solution.py:88
Sparse Core Ops, SparseCore 0:
  9.8 93.9 all-gather.5
  106.9 65.3 all-gather.7

commit v10 on v7

--- a/solution.py
+++ b/solution.py
@@ -264,10 +264,11 @@
     out = out_partial(out_grad, out_factor).reshape(X * C, rank // (X * C), -1)
     for s in range(1, ZL):
         chain.step()
-        if s == 2:
+        if s == 1:
+            out = tie(out, chain.ups[-1])
             out = lax.all_to_all(out, ("x", "c"), 0, 0, tiled=True).sum(0)
-        if s < 3:
-            out = chain.join(out)
+        if s == 5:
+            chain.after(out)
         if s == 6:
             out = chain.join(out)
         if s == 7:

time: 240 us -> 230 us (0.958)
  waiting for transfers between devices: 94.7 us -> 88.2 us
  starting transfers between devices: 55.4 us -> 52.7 us
  local copies, waits for them, and re-layouts: 13.4 us -> 10.8 us
    ppermute x7, waiting for transfers between devices: 53.4 us -> 46.5 us  [step(): lax.ppermute(down, 'zl', [(z, z - 1) for z in range(1, ZL + 1 - s)])]
    unnamed x20 -> x10, local copies, waits for them, and re-layouts: 4.45 us -> 0.87 us
    all_to_all x3, starting transfers between devices: 27.9 us -> 24.4 us  [share(): lax.all_to_all(jnp.broadcast_to(x[None], (count,) + x.shape), axes, 0, 0,...]
where the time goes in v10:
time: 230 us; the launch traced here: 229 us
  waiting for transfers between devices  88.2 us (38%)
  starting transfers between devices  52.7 us (23%)
  blocking collectives  38.2 us (17%)
  Pallas kernels  23.5 us (10%)
  between operations  13.8 us (6%)
  local copies, waits for them, and re-layouts  10.8 us (5%)
    ppermute x7, waiting for transfers between devices, step(): lax.ppermute(down, 'zl', [(z, z - 1) for z in range(1, ZL + 1 - s)])  46.5 us
    all_to_all x3, starting transfers between devices, share(): lax.all_to_all(jnp.broadcast_to(x[None], (count,) + x.shape), axes, 0, 0,...  24.4 us
    all_to_all x3, waiting for transfers between devices, share(): lax.all_to_all(jnp.broadcast_to(x[None], (count,) + x.shape), axes, 0, 0,...  21.4 us
    pallas_call x1, Pallas kernels, layer(): pl.pallas_call(layer_kernel, out_shape=jax.ShapeDtypeStruct((rank // 2, 2...  14.7 us
    all_to_all x1, blocking collectives, shards(): out = lax.all_to_all(out, ('x', 'c'), 0, 0, tiled=True).sum(0)  14.5 us
    all_gather x1, blocking collectives, exchange_z(): got = lax.all_gather(sent, 'zh')  12.3 us
    ppermute x7, starting transfers between devices, step(): lax.ppermute(up, 'zl', [(z, z + 1) for z in range(s - 1, ZL - 1)])  11.7 us
    all_to_all x1, blocking collectives, shards(): chain = Chain(lax.all_to_all(quarters, 'y', 0, 0, tiled=True))  11.4 us
  transfers between devices with their start and end apart: 20, of which 11 were waited for; matrix products, arithmetic and copies ran while one was open for 3% of the time, Pallas kernels for 6%

profile of v10, /device:TPU:1, one launch (start us, length us, event | category | flops | bytes accessed | tf_op | source)
XLA Modules:
  0.0 228.9 jit_solution(11899367479339170278)
XLA Ops:
  6.5 3.1 %constant_dynamic-slice_fusion = bf16[240,4096]{1,0:T(8,128)(2,1)} fusion(bf16[480,4096]{1,0:T(8,128)(2,1)} %param.7, s32[]{:T(128)S(6)} %select_n.55), kind=kLoop, calls=%fused_computation.35 | loop fusion | bytes 3932164 | tf_op jit(solution)/shard_map/dynamic_slice | solution.py:256
  9.6 0.0 all-gather.6.cloned.1.call-update
  9.6 0.0 copy-start.3
  9.6 0.0 all-gather.8.cloned.1.call-start
  9.7 0.8 copy-done.1
  10.5 0.2 copy.14
  10.7 0.2 copy.13
  10.9 11.4 %all_to_all.30.refs_0_ = bf16[4,448,128]{2,1,0:T(8,128)(2,1)S(1)} all-to-all(bf16[4,448,128]{2,1,0:T(8,128)(2,1)S(1)} %pad_maximum_fusion), channel_id=1, replica_groups=mesh['zl'=8,'y'=4,'x'=4,'zh'=2,'c'=2] {'y'}, dimensions={0} | all-to-all | bytes 917504 | tf_op jit(solution)/shard_map/all_to_all | solution.py:263
  22.3 4.5 %collective-permute-start = (bf16[4,448,128]{2,1,0:T(8,128)(2,1)S(1)}, bf16[4,448,128]{2,1,0:T(8,128)(2,1)S(1)}, u32[]{:S(2)}, u32[]{:S(2)}) collective-permute-start(bf16[4,448,128]{2,1,0:T(8,128)(2,1)S(1)} %all_to_all.30.refs_0_), channel_id=1, source_target_pairs={{0,64},{64,128},{128,192},{192,256},{256,320},{320,384},{384,448},... | collective-permute-start | bytes 1376264 | tf_op jit(solution)/shard_map/ppermute | solution.py:189
  26.9 1.3 collective-permute-start.2
  28.2 6.3 %collective-permute-done.refs_1_ = bf16[4,448,128]{2,1,0:T(8,128)(2,1)S(1)} collective-permute-done((bf16[4,448,128]{2,1,0:T(8,128)(2,1)S(1)}, bf16[4,448,128]{2,1,0:T(8,128)(2,1)S(1)}, u32[]{:S(2)}, u32[]{:S(2)}) %collective-permute-start) | collective-permute-done | bytes 458784 | tf_op jit(solution)/shard_map/ppermute | solution.py:189
  34.5 0.7 collective-permute-start.1
  35.2 3.6 %collective-permute-done.2.refs_8_ = bf16[4,448,128]{2,1,0:T(8,128)(2,1)S(1)} collective-permute-done((bf16[4,448,128]{2,1,0:T(8,128)(2,1)S(1)}, bf16[4,448,128]{2,1,0:T(8,128)(2,1)S(1)}, u32[]{:S(2)}, u32[]{:S(2)}) %collective-permute-start.2) | collective-permute-done | bytes 458784 | tf_op jit(solution)/shard_map/ppermute | solution.py:190
  38.8 1.3 collective-permute-start.4
  40.1 0.0 collective-permute-done.1.refs_2_
  40.1 0.7 collective-permute-start.3
  40.8 9.3 %collective-permute-done.4.refs_9_ = bf16[4,448,128]{2,1,0:T(8,128)(2,1)S(1)} collective-permute-done((bf16[4,448,128]{2,1,0:T(8,128)(2,1)S(1)}, bf16[4,448,128]{2,1,0:T(8,128)(2,1)S(1)}, u32[]{:S(2)}, u32[]{:S(2)}) %collective-permute-start.4) | collective-permute-done | bytes 458784 | tf_op jit(solution)/shard_map/ppermute | solution.py:190
  50.1 1.3 collective-permute-start.6
  51.4 1.4 collective-permute-start.5
  52.8 9.7 %collective-permute-done.6.refs_10_ = bf16[4,448,128]{2,1,0:T(8,128)(2,1)S(1)} collective-permute-done((bf16[4,448,128]{2,1,0:T(8,128)(2,1)S(1)}, bf16[4,448,128]{2,1,0:T(8,128)(2,1)S(1)}, u32[]{:S(2)}, u32[]{:S(2)}) %collective-permute-start.6) | collective-permute-done | bytes 458784 | tf_op jit(solution)/shard_map/ppermute | solution.py:190
  62.6 1.3 collective-permute-start.8
  63.8 0.0 collective-permute-done.5.refs_4_
  63.9 1.5 collective-permute-start.7
  65.3 7.4 %collective-permute-done.8.refs_11_ = bf16[4,448,128]{2,1,0:T(8,128)(2,1)} collective-permute-done((bf16[4,448,128]{2,1,0:T(8,128)(2,1)S(1)}, bf16[4,448,128]{2,1,0:T(8,128)(2,1)}, u32[]{:S(2)}, u32[]{:S(2)}) %collective-permute-start.8) | collective-permute-done | bytes 458784 | tf_op jit(solution)/shard_map/ppermute | solution.py:190
  72.7 1.3 collective-permute-start.10
  74.0 1.0 pad.9
  75.0 0.2 convolution_bitcast_fusion
  75.2 14.5 %all_to_all.31 = f32[8,8,512]{2,1,0:T(8,128)S(1)} all-to-all(f32[8,8,512]{2,1,0:T(8,128)S(1)} %convolution_bitcast_fusion), channel_id=1, replica_groups=mesh['zl'=8,'y'=4,'x'=4,'zh'=2,'c'=2] {'x','c'}, dimensions={0} | all-to-all | bytes 262144 | tf_op jit(solution)/shard_map/all_to_all | solution.py:269
  89.7 0.0 collective-permute-done.7.refs_5_
  89.7 1.5 collective-permute-start.9
  91.2 1.3 collective-permute-start.11
  92.5 0.0 collective-permute-done.9.refs_6_
  92.5 14.0 %collective-permute-done.11.refs_13_ = bf16[4,448,128]{2,1,0:T(8,128)(2,1)} collective-permute-done((bf16[4,448,128]{2,1,0:T(8,128)(2,1)}, bf16[4,448,128]{2,1,0:T(8,128)(2,1)}, u32[]{:S(2)}, u32[]{:S(2)}) %collective-permute-start.11) | collective-permute-done | bytes 458784 | tf_op jit(solution)/shard_map/ppermute | solution.py:190
  106.5 1.4 collective-permute-start.12
  107.9 1.3 collective-permute-start.13
  109.3 12.3 %all-gather = bf16[64,512]{1,0:T(8,128)(2,1)S(1)} all-gather(bf16[32,512]{1,0:T(8,128)(2,1)S(1)} %pad_maximum_fusion.2), channel_id=2, replica_groups=mesh['zl'=8,'y'=4,'x'=4,'zh'=2,'c'=2] {'zh'}, dimensions={0}, use_global_device_ids=true | all-gather | bytes 98304 | tf_op jit(solution)/shard_map/all_gather | solution.py:228
  121.6 2.5 %collective-permute-done.13.refs_14_ = bf16[4,448,128]{2,1,0:T(8,128)(2,1)} collective-permute-done((bf16[4,448,128]{2,1,0:T(8,128)(2,1)}, bf16[4,448,128]{2,1,0:T(8,128)(2,1)}, u32[]{:S(2)}, u32[]{:S(2)}) %collective-permute-start.13) | collective-permute-done | bytes 458784 | tf_op jit(solution)/shard_map/ppermute | solution.py:190
  124.2 0.6 pad_maximum_fusion.1
  124.8 0.0 all-gather.8.cloned.1.call-update
  124.8 0.1 dynamic-slice_bitcast_fusion.1
  124.9 0.9 broadcast_in_dim.44
  125.8 6.6 %all-to-all-start.2 = ((f32[32,8,512]{2,1,0:T(8,128)}), f32[32,8,512]{2,1,0:T(8,128)}, u32[]{:S(2)}, u32[]{:S(2)}) async-start(f32[32,8,512]{2,1,0:T(8,128)} %broadcast_in_dim.44), calls=%async_computation.2 | async-start | bytes 1048576 | tf_op jit(solution)/shard_map/all_to_all | solution.py:88
  132.4 0.0 all-gather.6.cloned.1.call-done
  132.4 14.7 %layer.1 = f32[32,2,2048]{2,1,0:T(2,128)} custom-call(s32[1]{0:T(128)} %bitcast.place_ref, bf16[64,256]{1,0:T(8,128)(2,1)S(1)} %pad.8.factor_ref, bf16[4,448,128]{2,1,0:T(8,128)(2,1)S(1)} %all_to_all.30.refs_0_, bf16[4,448,128]{2,1,0:T(8,128)(2,1)S(1)} %collective-permute-done.refs_1_, bf16[4,448,128]{2,1,0:T(8,128)(2,1)S(1)} %collective-permute-done.1.refs_2_, ...), custom_call_target="tpu_custom_call" | custom-call | flops 7046430720 | bytes 19398656 | tf_op jit(solution)/shard_map/layer/pallas_call | solution.py:154
  147.1 7.5 %all-to-all-start.3 = ((f32[32,2,2048]{2,1,0:T(2,128)}), f32[32,2,2048]{2,1,0:T(2,128)S(1)}, u32[]{:S(2)}, u32[]{:S(2)}) async-start(f32[32,2,2048]{2,1,0:T(2,128)} %layer.1), calls=%async_computation.3 | async-start | bytes 1048576 | tf_op jit(solution)/shard_map/all_to_all | solution.py:283
  154.7 1.1 copy.17
  155.8 10.4 %all-to-all-done.3 = f32[32,2,2048]{2,1,0:T(2,128)S(1)} async-done(((f32[32,2,2048]{2,1,0:T(2,128)}), f32[32,2,2048]{2,1,0:T(2,128)S(1)}, u32[]{:S(2)}, u32[]{:S(2)}) %all-to-all-start.3) | async-done | bytes 524320 | tf_op jit(solution)/shard_map/all_to_all | solution.py:283
  166.2 0.2 reduce_sum.38
  166.4 0.1 broadcast_select_fusion
  166.5 0.1 select_n.57
  166.6 0.5 convolution_multiply_fusion
  167.1 0.1 broadcast_in_dim.47
  167.2 0.7 broadcast_in_dim.48
  167.9 11.2 %all-to-all-start.4 = ((f32[16,12,128]{2,1,0:T(8,128)}), f32[16,12,128]{2,1,0:T(8,128)S(1)}, u32[]{:S(2)}, u32[]{:S(2)}) async-start(f32[16,12,128]{2,1,0:T(8,128)} %broadcast_in_dim.48), calls=%async_computation.4 | async-start | bytes 262144 | tf_op jit(solution)/shard_map/all_to_all | solution.py:88
  179.1 3.5 %all-gather.8.cloned.1.call-done = bf16[1536,512]{1,0:T(8,128)(2,1)} async-done(((bf16[48,512]{1,0:T(8,128)(2,1)}), bf16[1536,512]{1,0:T(8,128)(2,1)}) %all-gather.8.cloned.1.call-update) | async-done | bytes 1572880 | tf_op jit(solution)/shard_map/all_gather | solution.py:241
  182.5 8.7 %all-to-all-done.4 = f32[16,12,128]{2,1,0:T(8,128)S(1)} async-done(((f32[16,12,128]{2,1,0:T(8,128)}), f32[16,12,128]{2,1,0:T(8,128)S(1)}, u32[]{:S(2)}, u32[]{:S(2)}) %all-to-all-start.4) | async-done | bytes 98336 | tf_op jit(solution)/shard_map/all_to_all | solution.py:88
  191.2 1.0 broadcast_in_dim.49
  192.2 6.7 %all-to-all-start.5 = ((bf16[32,96,128]{2,1,0:T(8,128)(2,1)}), bf16[32,96,128]{2,1,0:T(8,128)(2,1)S(1)}, u32[]{:S(2)}, u32[]{:S(2)}) async-start(bf16[32,96,128]{2,1,0:T(8,128)(2,1)} %broadcast_in_dim.49), calls=%async_computation.5 | async-start | bytes 1572864 | tf_op jit(solution)/shard_map/all_to_all | solution.py:88
  198.9 1.0 dynamic-slice_bitcast_fusion
  200.0 0.1 reshape.120
  200.1 0.3 copy.16
  200.3 0.2 reshape.121.queries_ref
  200.5 12.7 %all-to-all-done.5.features_ref = bf16[32,96,128]{2,1,0:T(8,128)(2,1)S(1)} async-done(((bf16[32,96,128]{2,1,0:T(8,128)(2,1)}), bf16[32,96,128]{2,1,0:T(8,128)(2,1)S(1)}, u32[]{:S(2)}, u32[]{:S(2)}) %all-to-all-start.5) | async-done | bytes 786464 | tf_op jit(solution)/shard_map/all_to_all | solution.py:88
  213.2 8.8 %solve.1 = f32[32,96]{1,0:T(8,128)} custom-call(bf16[32,96,128]{2,1,0:T(8,128)(2,1)S(1)} %all-to-all-done.5.features_ref, bf16[32,4096]{1,0:T(8,128)(2,1)S(1)} %reshape.121.queries_ref), custom_call_target="tpu_custom_call" | custom-call | tf_op jit(solution)/shard_map/solve/pallas_call | solution.py:79
  (29 shorter events, 0.2 us)
Async XLA Ops:
  6.5 118.3 %copy-start = (bf16[896,64]{0,1:T(8,128)(2,1)S(1)}, bf16[896,64]{0,1:T(8,128)(2,1)}, u32[]{:S(2)}) copy-start(bf16[896,64]{0,1:T(8,128)(2,1)} %param.11) | copy-start | bytes 344068
  6.5 125.8 %all-gather.6.cloned.1.call-start = ((), (), s32[]{:S(2)}) async-start(), calls=%async_computation.6 | async-start | bytes 17694720 | tf_op jit(solution)/shard_map/all_gather | solution.py:257
  9.6 0.9 copy-start.1
  9.6 1.1 copy-start.2
  9.6 65.4 %copy-start.3 = (bf16[256,64]{0,1:T(8,128)(2,1)S(1)}, bf16[256,64]{0,1:T(8,128)(2,1)}, u32[]{:S(2)}) copy-start(bf16[256,64]{0,1:T(8,128)(2,1)} %param.12) | copy-start | bytes 98308
  9.6 172.9 %all-gather.8.cloned.1.call-start = ((), (), s32[]{:S(2)}) async-start(), calls=%async_computation.7 | async-start | bytes 1622016 | tf_op jit(solution)/shard_map/all_gather | solution.py:241
  10.5 82.0 %copy-start.4 = (bf16[32,256]{1,0:T(8,128)(2,1)S(1)}, bf16[32,256]{1,0:T(8,128)(2,1)}, u32[]{:S(2)}) copy-start(bf16[32,256]{1,0:T(8,128)(2,1)} %param.13) | copy-start | bytes 49156
  22.3 12.2 %collective-permute-start = (bf16[4,448,128]{2,1,0:T(8,128)(2,1)S(1)}, bf16[4,448,128]{2,1,0:T(8,128)(2,1)S(1)}, u32[]{:S(2)}, u32[]{:S(2)}) collective-permute-start(bf16[4,448,128]{2,1,0:T(8,128)(2,1)S(1)} %all_to_all.30.refs_0_), channel_id=1, source_target_pairs={{0,64},{64,128},{128,192},{192,256},{256,320},{320,384},{384,448},... | collective-permute-start | bytes 1376264 | tf_op jit(solution)/shard_map/ppermute | solution.py:189
  26.9 11.9 %collective-permute-start.2 = (bf16[4,448,128]{2,1,0:T(8,128)(2,1)S(1)}, bf16[4,448,128]{2,1,0:T(8,128)(2,1)S(1)}, u32[]{:S(2)}, u32[]{:S(2)}) collective-permute-start(bf16[4,448,128]{2,1,0:T(8,128)(2,1)S(1)} %all_to_all.30.refs_0_), channel_id=1, source_target_pairs={{64,0},{128,64},{192,128},{256,192},{320,256},{384,320},{448,384},... | collective-permute-start | bytes 1376264 | tf_op jit(solution)/shard_map/ppermute | solution.py:190
  34.5 5.6 %collective-permute-start.1 = (bf16[4,448,128]{2,1,0:T(8,128)(2,1)S(1)}, bf16[4,448,128]{2,1,0:T(8,128)(2,1)S(1)}, u32[]{:S(2)}, u32[]{:S(2)}) collective-permute-start(bf16[4,448,128]{2,1,0:T(8,128)(2,1)S(1)} %collective-permute-done.refs_1_), channel_id=1, source_target_pairs={{64,128},{128,192},{192,256},{256,320},{320,384},{384,448},{65,129... | collective-permute-start | bytes 1376264 | tf_op jit(solution)/shard_map/ppermute | solution.py:189
  38.8 11.3 %collective-permute-start.4 = (bf16[4,448,128]{2,1,0:T(8,128)(2,1)S(1)}, bf16[4,448,128]{2,1,0:T(8,128)(2,1)S(1)}, u32[]{:S(2)}, u32[]{:S(2)}) collective-permute-start(bf16[4,448,128]{2,1,0:T(8,128)(2,1)S(1)} %collective-permute-done.2.refs_8_), channel_id=1, source_target_pairs={{64,0},{128,64},{192,128},{256,192},{320,256},{384,320},{65,1},{12... | collective-permute-start | bytes 1376264 | tf_op jit(solution)/shard_map/ppermute | solution.py:190
  40.1 11.3 %collective-permute-start.3 = (bf16[4,448,128]{2,1,0:T(8,128)(2,1)S(1)}, bf16[4,448,128]{2,1,0:T(8,128)(2,1)S(1)}, u32[]{:S(2)}, u32[]{:S(2)}) collective-permute-start(bf16[4,448,128]{2,1,0:T(8,128)(2,1)S(1)} %collective-permute-done.1.refs_2_), channel_id=1, source_target_pairs={{128,192},{192,256},{256,320},{320,384},{384,448},{129,193},{193,2... | collective-permute-start | bytes 1376264 | tf_op jit(solution)/shard_map/ppermute | solution.py:189
  50.1 12.5 %collective-permute-start.6 = (bf16[4,448,128]{2,1,0:T(8,128)(2,1)S(1)}, bf16[4,448,128]{2,1,0:T(8,128)(2,1)S(1)}, u32[]{:S(2)}, u32[]{:S(2)}) collective-permute-start(bf16[4,448,128]{2,1,0:T(8,128)(2,1)S(1)} %collective-permute-done.4.refs_9_), channel_id=1, source_target_pairs={{64,0},{128,64},{192,128},{256,192},{320,256},{65,1},{129,65},{193... | collective-permute-start | bytes 1376264 | tf_op jit(solution)/shard_map/ppermute | solution.py:190
  51.4 12.5 %collective-permute-start.5 = (bf16[4,448,128]{2,1,0:T(8,128)(2,1)S(1)}, bf16[4,448,128]{2,1,0:T(8,128)(2,1)}, u32[]{:S(2)}, u32[]{:S(2)}) collective-permute-start(bf16[4,448,128]{2,1,0:T(8,128)(2,1)S(1)} %collective-permute-done.3.refs_3_), channel_id=1, source_target_pairs={{192,256},{256,320},{320,384},{384,448},{193,257},{257,321},{321,3... | collective-permute-start | bytes 1376264 | tf_op jit(solution)/shard_map/ppermute | solution.py:189
  62.6 10.2 %collective-permute-start.8 = (bf16[4,448,128]{2,1,0:T(8,128)(2,1)S(1)}, bf16[4,448,128]{2,1,0:T(8,128)(2,1)}, u32[]{:S(2)}, u32[]{:S(2)}) collective-permute-start(bf16[4,448,128]{2,1,0:T(8,128)(2,1)S(1)} %collective-permute-done.6.refs_10_), channel_id=1, source_target_pairs={{64,0},{128,64},{192,128},{256,192},{65,1},{129,65},{193,129},{257... | collective-permute-start | bytes 1376264 | tf_op jit(solution)/shard_map/ppermute | solution.py:190
  63.9 25.9 %collective-permute-start.7 = (bf16[4,448,128]{2,1,0:T(8,128)(2,1)}, bf16[4,448,128]{2,1,0:T(8,128)(2,1)}, u32[]{:S(2)}, u32[]{:S(2)}) collective-permute-start(bf16[4,448,128]{2,1,0:T(8,128)(2,1)} %collective-permute-done.5.refs_4_), channel_id=1, source_target_pairs={{256,320},{320,384},{384,448},{257,321},{321,385},{385,449},{258,3... | collective-permute-start | bytes 1376264 | tf_op jit(solution)/shard_map/ppermute | solution.py:189
  72.7 18.5 %collective-permute-start.10 = (bf16[4,448,128]{2,1,0:T(8,128)(2,1)}, bf16[4,448,128]{2,1,0:T(8,128)(2,1)}, u32[]{:S(2)}, u32[]{:S(2)}) collective-permute-start(bf16[4,448,128]{2,1,0:T(8,128)(2,1)} %collective-permute-done.8.refs_11_), channel_id=1, source_target_pairs={{64,0},{128,64},{192,128},{65,1},{129,65},{193,129},{66,2},{130,66... | collective-permute-start | bytes 1376264 | tf_op jit(solution)/shard_map/ppermute | solution.py:190
  89.7 2.8 %collective-permute-start.9 = (bf16[4,448,128]{2,1,0:T(8,128)(2,1)}, bf16[4,448,128]{2,1,0:T(8,128)(2,1)}, u32[]{:S(2)}, u32[]{:S(2)}) collective-permute-start(bf16[4,448,128]{2,1,0:T(8,128)(2,1)} %collective-permute-done.7.refs_5_), channel_id=1, source_target_pairs={{320,384},{384,448},{321,385},{385,449},{322,386},{386,450},{323,3... | collective-permute-start | bytes 1376264 | tf_op jit(solution)/shard_map/ppermute | solution.py:189
  91.2 15.3 %collective-permute-start.11 = (bf16[4,448,128]{2,1,0:T(8,128)(2,1)}, bf16[4,448,128]{2,1,0:T(8,128)(2,1)}, u32[]{:S(2)}, u32[]{:S(2)}) collective-permute-start(bf16[4,448,128]{2,1,0:T(8,128)(2,1)} %collective-permute-done.10.refs_12_), channel_id=1, source_target_pairs={{64,0},{128,64},{65,1},{129,65},{66,2},{130,66},{67,3},{131,67},{6... | collective-permute-start | bytes 1376264 | tf_op jit(solution)/shard_map/ppermute | solution.py:190
  106.5 15.1 %collective-permute-start.12 = (bf16[4,448,128]{2,1,0:T(8,128)(2,1)}, bf16[4,448,128]{2,1,0:T(8,128)(2,1)}, u32[]{:S(2)}, u32[]{:S(2)}) collective-permute-start(bf16[4,448,128]{2,1,0:T(8,128)(2,1)} %collective-permute-done.9.refs_6_), channel_id=1, source_target_pairs={{384,448},{385,449},{386,450},{387,451},{388,452},{389,453},{390,4... | collective-permute-start | bytes 1376264 | tf_op jit(solution)/shard_map/ppermute | solution.py:189
  107.9 16.2 %collective-permute-start.13 = (bf16[4,448,128]{2,1,0:T(8,128)(2,1)}, bf16[4,448,128]{2,1,0:T(8,128)(2,1)}, u32[]{:S(2)}, u32[]{:S(2)}) collective-permute-start(bf16[4,448,128]{2,1,0:T(8,128)(2,1)} %collective-permute-done.11.refs_13_), channel_id=1, source_target_pairs={{64,0},{65,1},{66,2},{67,3},{68,4},{69,5},{70,6},{71,7},{72,8},{73... | collective-permute-start | bytes 1376264 | tf_op jit(solution)/shard_map/ppermute | solution.py:190
  125.8 21.3 %all-to-all-start.2 = ((f32[32,8,512]{2,1,0:T(8,128)}), f32[32,8,512]{2,1,0:T(8,128)}, u32[]{:S(2)}, u32[]{:S(2)}) async-start(f32[32,8,512]{2,1,0:T(8,128)} %broadcast_in_dim.44), calls=%async_computation.2 | async-start | bytes 1048576 | tf_op jit(solution)/shard_map/all_to_all | solution.py:88
  147.1 19.1 %all-to-all-start.3 = ((f32[32,2,2048]{2,1,0:T(2,128)}), f32[32,2,2048]{2,1,0:T(2,128)S(1)}, u32[]{:S(2)}, u32[]{:S(2)}) async-start(f32[32,2,2048]{2,1,0:T(2,128)} %layer.1), calls=%async_computation.3 | async-start | bytes 1048576 | tf_op jit(solution)/shard_map/all_to_all | solution.py:283
  167.9 23.3 %all-to-all-start.4 = ((f32[16,12,128]{2,1,0:T(8,128)}), f32[16,12,128]{2,1,0:T(8,128)S(1)}, u32[]{:S(2)}, u32[]{:S(2)}) async-start(f32[16,12,128]{2,1,0:T(8,128)} %broadcast_in_dim.48), calls=%async_computation.4 | async-start | bytes 262144 | tf_op jit(solution)/shard_map/all_to_all | solution.py:88
  192.2 21.0 %all-to-all-start.5 = ((bf16[32,96,128]{2,1,0:T(8,128)(2,1)}), bf16[32,96,128]{2,1,0:T(8,128)(2,1)S(1)}, u32[]{:S(2)}, u32[]{:S(2)}) async-start(bf16[32,96,128]{2,1,0:T(8,128)(2,1)} %broadcast_in_dim.49), calls=%async_computation.5 | async-start | bytes 1572864 | tf_op jit(solution)/shard_map/all_to_all | solution.py:88
Sparse Core Ops, SparseCore 0:
  9.7 93.9 all-gather.5
  124.9 57.5 all-gather.7

commit v11 on v8

--- a/solution.py
+++ b/solution.py
@@ -261,10 +261,12 @@
         if s == 1:
             out = tie(out, chain.ups[-1])
             out = lax.all_to_all(out, ("x", "c"), 0, 0, tiled=True).sum(0)
-        if s == 5:
+        if s == 4:
             chain.after(out)
             out = tie(out, chain.ups[-1])
             out, query_rows = exchange_z(out, queries)
+        if s == 5:
+            chain.after(out, query_rows)
         if s == 6:
             shared = share_plane(out, query_rows)
             chain.after(out, plane_tokens)

time: 221 us -> 223 us (level)
    all_gather x1, waiting for transfers between devices: 0.02 us -> 5.85 us  [shards(): plane_tokens = lax.all_gather(mine, ('y', 'c'))]
    ppermute x7, waiting for transfers between devices: 45.5 us -> 40.5 us  [step(): lax.ppermute(down, 'zl', [(z, z - 1) for z in range(1, ZL + 1 - s)])]
where the time goes in v11:
time: 223 us; the launch traced here: 222 us
  waiting for transfers between devices  95.3 us (43%)
  starting transfers between devices  52.3 us (23%)
  blocking collectives  23.7 us (11%)
  Pallas kernels  23.5 us (11%)
  between operations  13.8 us (6%)
  local copies, waits for them, and re-layouts  10.8 us (5%)
    ppermute x7, waiting for transfers between devices, step(): lax.ppermute(down, 'zl', [(z, z - 1) for z in range(1, ZL + 1 - s)])  40.5 us
    all_to_all x3, waiting for transfers between devices, share(): lax.all_to_all(jnp.broadcast_to(x[None], (count,) + x.shape), axes, 0, 0,...  24.9 us
    all_to_all x3, starting transfers between devices, share(): lax.all_to_all(jnp.broadcast_to(x[None], (count,) + x.shape), axes, 0, 0,...  16 us
    pallas_call x1, Pallas kernels, layer(): pl.pallas_call(layer_kernel, out_shape=jax.ShapeDtypeStruct((rank // 2, 2...  14.7 us
    all_gather x1, blocking collectives, exchange_z(): got = lax.all_gather(sent, 'zh')  12.3 us
    all_to_all x1, waiting for transfers between devices, shards(): in_proj = lax.all_to_all(in_part, PLANE, 0, 0, tiled=True)  12.3 us
    ppermute x7, starting transfers between devices, step(): lax.ppermute(up, 'zl', [(z, z + 1) for z in range(s - 1, ZL - 1)])  11.7 us
    all_to_all x1, blocking collectives, shards(): chain = Chain(lax.all_to_all(quarters, 'y', 0, 0, tiled=True))  11.4 us
  transfers between devices with their start and end apart: 21, of which 11 were waited for; matrix products, arithmetic and copies ran while one was open for 4% of the time, Pallas kernels for 7%

profile of v11, /device:TPU:1, one launch (start us, length us, event | category | flops | bytes accessed | tf_op | source)
XLA Modules:
  0.0 221.9 jit_solution(7635503352243244512)
XLA Ops:
  6.5 3.1 %constant_dynamic-slice_fusion = bf16[240,4096]{1,0:T(8,128)(2,1)} fusion(bf16[480,4096]{1,0:T(8,128)(2,1)} %param.7, s32[]{:T(128)S(6)} %select_n.55), kind=kLoop, calls=%fused_computation.35 | loop fusion | bytes 3932164 | tf_op jit(solution)/shard_map/dynamic_slice | solution.py:250
  9.6 0.0 all-gather.6.cloned.1.call-update
  9.7 0.0 copy-start.3
  9.7 0.9 copy-done.1
  10.6 0.2 copy.14
  10.8 0.2 copy.13
  11.0 11.4 %all_to_all.30.refs_0_ = bf16[4,448,128]{2,1,0:T(8,128)(2,1)S(1)} all-to-all(bf16[4,448,128]{2,1,0:T(8,128)(2,1)S(1)} %pad_maximum_fusion), channel_id=1, replica_groups=mesh['zl'=8,'y'=4,'x'=4,'zh'=2,'c'=2] {'y'}, dimensions={0} | all-to-all | bytes 917504 | tf_op jit(solution)/shard_map/all_to_all | solution.py:257
  22.4 4.5 %collective-permute-start = (bf16[4,448,128]{2,1,0:T(8,128)(2,1)S(1)}, bf16[4,448,128]{2,1,0:T(8,128)(2,1)S(1)}, u32[]{:S(2)}, u32[]{:S(2)}) collective-permute-start(bf16[4,448,128]{2,1,0:T(8,128)(2,1)S(1)} %all_to_all.30.refs_0_), channel_id=1, source_target_pairs={{0,64},{64,128},{128,192},{192,256},{256,320},{320,384},{384,448},... | collective-permute-start | bytes 1376264 | tf_op jit(solution)/shard_map/ppermute | solution.py:189
  26.9 1.3 collective-permute-start.2
  28.2 6.3 %collective-permute-done.refs_1_ = bf16[4,448,128]{2,1,0:T(8,128)(2,1)S(1)} collective-permute-done((bf16[4,448,128]{2,1,0:T(8,128)(2,1)S(1)}, bf16[4,448,128]{2,1,0:T(8,128)(2,1)S(1)}, u32[]{:S(2)}, u32[]{:S(2)}) %collective-permute-start) | collective-permute-done | bytes 458784 | tf_op jit(solution)/shard_map/ppermute | solution.py:189
  34.5 0.7 collective-permute-start.1
  35.2 3.6 %collective-permute-done.2.refs_8_ = bf16[4,448,128]{2,1,0:T(8,128)(2,1)S(1)} collective-permute-done((bf16[4,448,128]{2,1,0:T(8,128)(2,1)S(1)}, bf16[4,448,128]{2,1,0:T(8,128)(2,1)S(1)}, u32[]{:S(2)}, u32[]{:S(2)}) %collective-permute-start.2) | collective-permute-done | bytes 458784 | tf_op jit(solution)/shard_map/ppermute | solution.py:190
  38.8 1.3 collective-permute-start.4
  40.1 0.0 collective-permute-done.1.refs_2_
  40.1 0.7 collective-permute-start.3
  40.8 9.3 %collective-permute-done.4.refs_9_ = bf16[4,448,128]{2,1,0:T(8,128)(2,1)S(1)} collective-permute-done((bf16[4,448,128]{2,1,0:T(8,128)(2,1)S(1)}, bf16[4,448,128]{2,1,0:T(8,128)(2,1)S(1)}, u32[]{:S(2)}, u32[]{:S(2)}) %collective-permute-start.4) | collective-permute-done | bytes 458784 | tf_op jit(solution)/shard_map/ppermute | solution.py:190
  50.1 1.3 collective-permute-start.6
  51.4 0.0 collective-permute-done.3.refs_3_
  51.4 1.4 collective-permute-start.5
  52.9 9.7 %collective-permute-done.6.refs_10_ = bf16[4,448,128]{2,1,0:T(8,128)(2,1)S(1)} collective-permute-done((bf16[4,448,128]{2,1,0:T(8,128)(2,1)S(1)}, bf16[4,448,128]{2,1,0:T(8,128)(2,1)S(1)}, u32[]{:S(2)}, u32[]{:S(2)}) %collective-permute-start.6) | collective-permute-done | bytes 458784 | tf_op jit(solution)/shard_map/ppermute | solution.py:190
  62.6 1.3 collective-permute-start.8
  63.9 1.0 pad.9
  64.9 0.9 convolution_bitcast_fusion
  65.7 8.4 %all-to-all-start.1 = ((f32[8,8,512]{2,1,0:T(8,128)}), f32[8,8,512]{2,1,0:T(8,128)S(1)}, u32[]{:S(2)}, u32[]{:S(2)}) async-start(f32[8,8,512]{2,1,0:T(8,128)} %convolution_bitcast_fusion), calls=%async_computation.1 | async-start | bytes 262144 | tf_op jit(solution)/shard_map/all_to_all | solution.py:263
  74.1 5.3 %all-to-all-done.1 = f32[8,8,512]{2,1,0:T(8,128)S(1)} async-done(((f32[8,8,512]{2,1,0:T(8,128)}), f32[8,8,512]{2,1,0:T(8,128)S(1)}, u32[]{:S(2)}, u32[]{:S(2)}) %all-to-all-start.1) | async-done | bytes 131104 | tf_op jit(solution)/shard_map/all_to_all | solution.py:263
  79.4 1.5 collective-permute-start.7
  80.9 1.3 collective-permute-start.10
  82.2 12.3 %all-gather = bf16[64,512]{1,0:T(8,128)(2,1)S(1)} all-gather(bf16[32,512]{1,0:T(8,128)(2,1)S(1)} %pad_maximum_fusion.2), channel_id=2, replica_groups=mesh['zl'=8,'y'=4,'x'=4,'zh'=2,'c'=2] {'zh'}, dimensions={0}, use_global_device_ids=true | all-gather | bytes 98304 | tf_op jit(solution)/shard_map/all_gather | solution.py:222
  94.5 1.5 collective-permute-start.9
  96.0 0.0 collective-permute-done.10.refs_12_
  96.0 1.3 collective-permute-start.12
  97.3 0.6 pad_maximum_fusion.1
  97.9 0.0 all-gather.8.cloned.1.call-update
  97.9 0.0 collective-permute-done.9.refs_6_
  97.9 5.8 %all-gather.6.cloned.1.call-done = bf16[1920,4096]{1,0:T(8,128)(2,1)} async-done(((bf16[240,4096]{1,0:T(8,128)(2,1)}), bf16[1920,4096]{1,0:T(8,128)(2,1)}) %all-gather.6.cloned.1.call-update) | async-done | bytes 15728656 | tf_op jit(solution)/shard_map/all_gather | solution.py:251
  103.8 1.4 collective-permute-start.11
  105.2 14.9 %collective-permute-done.12.refs_13_ = bf16[4,448,128]{2,1,0:T(8,128)(2,1)} collective-permute-done((bf16[4,448,128]{2,1,0:T(8,128)(2,1)}, bf16[4,448,128]{2,1,0:T(8,128)(2,1)}, u32[]{:S(2)}, u32[]{:S(2)}) %collective-permute-start.12) | collective-permute-done | bytes 458784 | tf_op jit(solution)/shard_map/ppermute | solution.py:190
  120.1 1.3 collective-permute-start.13
  121.4 0.1 dynamic-slice_bitcast_fusion.1
  121.5 0.9 broadcast_in_dim.46
  122.4 6.5 %all-to-all-start.3 = ((f32[32,8,512]{2,1,0:T(8,128)}), f32[32,8,512]{2,1,0:T(8,128)}, u32[]{:S(2)}, u32[]{:S(2)}) async-start(f32[32,8,512]{2,1,0:T(8,128)} %broadcast_in_dim.46), calls=%async_computation.3 | async-start | bytes 1048576 | tf_op jit(solution)/shard_map/all_to_all | solution.py:88
  128.9 0.0 collective-permute-done.11.refs_7_
  128.9 3.0 %collective-permute-done.13.refs_14_ = bf16[4,448,128]{2,1,0:T(8,128)(2,1)} collective-permute-done((bf16[4,448,128]{2,1,0:T(8,128)(2,1)}, bf16[4,448,128]{2,1,0:T(8,128)(2,1)}, u32[]{:S(2)}, u32[]{:S(2)}) %collective-permute-start.13) | collective-permute-done | bytes 458784 | tf_op jit(solution)/shard_map/ppermute | solution.py:190
  132.0 14.7 %layer.1 = f32[32,2,2048]{2,1,0:T(2,128)} custom-call(s32[1]{0:T(128)} %bitcast.place_ref, bf16[64,256]{1,0:T(8,128)(2,1)S(1)} %pad.8.factor_ref, bf16[4,448,128]{2,1,0:T(8,128)(2,1)S(1)} %all_to_all.30.refs_0_, bf16[4,448,128]{2,1,0:T(8,128)(2,1)S(1)} %collective-permute-done.refs_1_, bf16[4,448,128]{2,1,0:T(8,128)(2,1)S(1)} %collective-permute-done.1.refs_2_, ...), custom_call_target="tpu_custom_call" | custom-call | flops 7046430720 | bytes 19398656 | tf_op jit(solution)/shard_map/layer/pallas_call | solution.py:154
  146.7 7.3 %all-to-all-start.2 = ((f32[32,2,2048]{2,1,0:T(2,128)}), f32[32,2,2048]{2,1,0:T(2,128)S(1)}, u32[]{:S(2)}, u32[]{:S(2)}) async-start(f32[32,2,2048]{2,1,0:T(2,128)} %layer.1), calls=%async_computation.2 | async-start | bytes 1048576 | tf_op jit(solution)/shard_map/all_to_all | solution.py:279
  154.1 1.1 copy.17
  155.2 12.3 %all-to-all-done.2 = f32[32,2,2048]{2,1,0:T(2,128)S(1)} async-done(((f32[32,2,2048]{2,1,0:T(2,128)}), f32[32,2,2048]{2,1,0:T(2,128)S(1)}, u32[]{:S(2)}, u32[]{:S(2)}) %all-to-all-start.2) | async-done | bytes 524320 | tf_op jit(solution)/shard_map/all_to_all | solution.py:279
  167.4 0.2 reduce_sum.38
  167.6 0.1 broadcast_select_fusion
  167.7 0.1 select_n.57
  167.9 0.5 convolution_multiply_fusion
  168.4 0.1 broadcast_in_dim.47
  168.5 0.7 broadcast_in_dim.48
  169.1 3.5 %all-to-all-start.4 = ((f32[16,12,128]{2,1,0:T(8,128)}), f32[16,12,128]{2,1,0:T(8,128)S(1)}, u32[]{:S(2)}, u32[]{:S(2)}) async-start(f32[16,12,128]{2,1,0:T(8,128)} %broadcast_in_dim.48), calls=%async_computation.4 | async-start | bytes 262144 | tf_op jit(solution)/shard_map/all_to_all | solution.py:88
  172.6 0.0 all-gather.8.cloned.1.call-done
  172.7 12.3 %all-to-all-done.4 = f32[16,12,128]{2,1,0:T(8,128)S(1)} async-done(((f32[16,12,128]{2,1,0:T(8,128)}), f32[16,12,128]{2,1,0:T(8,128)S(1)}, u32[]{:S(2)}, u32[]{:S(2)}) %all-to-all-start.4) | async-done | bytes 98336 | tf_op jit(solution)/shard_map/all_to_all | solution.py:88
  185.0 1.0 broadcast_in_dim.49
  186.0 5.9 %all-to-all-start.5 = ((bf16[32,96,128]{2,1,0:T(8,128)(2,1)}), bf16[32,96,128]{2,1,0:T(8,128)(2,1)S(1)}, u32[]{:S(2)}, u32[]{:S(2)}) async-start(bf16[32,96,128]{2,1,0:T(8,128)(2,1)} %broadcast_in_dim.49), calls=%async_computation.5 | async-start | bytes 1572864 | tf_op jit(solution)/shard_map/all_to_all | solution.py:88
  192.0 1.0 dynamic-slice_bitcast_fusion
  193.0 0.1 reshape.116
  193.1 0.3 copy.16
  193.4 0.2 reshape.117.queries_ref
  193.6 12.6 %all-to-all-done.5.features_ref = bf16[32,96,128]{2,1,0:T(8,128)(2,1)S(1)} async-done(((bf16[32,96,128]{2,1,0:T(8,128)(2,1)}), bf16[32,96,128]{2,1,0:T(8,128)(2,1)S(1)}, u32[]{:S(2)}, u32[]{:S(2)}) %all-to-all-start.5) | async-done | bytes 786464 | tf_op jit(solution)/shard_map/all_to_all | solution.py:88
  206.2 8.8 %solve.1 = f32[32,96]{1,0:T(8,128)} custom-call(bf16[32,96,128]{2,1,0:T(8,128)(2,1)S(1)} %all-to-all-done.5.features_ref, bf16[32,4096]{1,0:T(8,128)(2,1)S(1)} %reshape.117.queries_ref), custom_call_target="tpu_custom_call" | custom-call | tf_op jit(solution)/shard_map/solve/pallas_call | solution.py:79
  (28 shorter events, 0.2 us)
Async XLA Ops:
  6.5 114.9 %copy-start = (bf16[896,64]{0,1:T(8,128)(2,1)S(1)}, bf16[896,64]{0,1:T(8,128)(2,1)}, u32[]{:S(2)}) copy-start(bf16[896,64]{0,1:T(8,128)(2,1)} %param.11) | copy-start | bytes 344068
  6.5 97.3 %all-gather.6.cloned.1.call-start = ((), (), s32[]{:S(2)}) async-start(), calls=%async_computation.6 | async-start | bytes 17694720 | tf_op jit(solution)/shard_map/all_gather | solution.py:251
  9.6 0.9 copy-start.1
  9.6 1.1 copy-start.2
  9.7 55.2 %copy-start.3 = (bf16[256,64]{0,1:T(8,128)(2,1)S(1)}, bf16[256,64]{0,1:T(8,128)(2,1)}, u32[]{:S(2)}) copy-start(bf16[256,64]{0,1:T(8,128)(2,1)} %param.12) | copy-start | bytes 98308
  10.6 63.5 %copy-start.4 = (bf16[32,256]{1,0:T(8,128)(2,1)S(1)}, bf16[32,256]{1,0:T(8,128)(2,1)}, u32[]{:S(2)}) copy-start(bf16[32,256]{1,0:T(8,128)(2,1)} %param.13) | copy-start | bytes 49156
  22.4 12.2 %collective-permute-start = (bf16[4,448,128]{2,1,0:T(8,128)(2,1)S(1)}, bf16[4,448,128]{2,1,0:T(8,128)(2,1)S(1)}, u32[]{:S(2)}, u32[]{:S(2)}) collective-permute-start(bf16[4,448,128]{2,1,0:T(8,128)(2,1)S(1)} %all_to_all.30.refs_0_), channel_id=1, source_target_pairs={{0,64},{64,128},{128,192},{192,256},{256,320},{320,384},{384,448},... | collective-permute-start | bytes 1376264 | tf_op jit(solution)/shard_map/ppermute | solution.py:189
  26.9 11.9 %collective-permute-start.2 = (bf16[4,448,128]{2,1,0:T(8,128)(2,1)S(1)}, bf16[4,448,128]{2,1,0:T(8,128)(2,1)S(1)}, u32[]{:S(2)}, u32[]{:S(2)}) collective-permute-start(bf16[4,448,128]{2,1,0:T(8,128)(2,1)S(1)} %all_to_all.30.refs_0_), channel_id=1, source_target_pairs={{64,0},{128,64},{192,128},{256,192},{320,256},{384,320},{448,384},... | collective-permute-start | bytes 1376264 | tf_op jit(solution)/shard_map/ppermute | solution.py:190
  34.5 5.6 %collective-permute-start.1 = (bf16[4,448,128]{2,1,0:T(8,128)(2,1)S(1)}, bf16[4,448,128]{2,1,0:T(8,128)(2,1)S(1)}, u32[]{:S(2)}, u32[]{:S(2)}) collective-permute-start(bf16[4,448,128]{2,1,0:T(8,128)(2,1)S(1)} %collective-permute-done.refs_1_), channel_id=1, source_target_pairs={{64,128},{128,192},{192,256},{256,320},{320,384},{384,448},{65,129... | collective-permute-start | bytes 1376264 | tf_op jit(solution)/shard_map/ppermute | solution.py:189
  38.8 11.3 %collective-permute-start.4 = (bf16[4,448,128]{2,1,0:T(8,128)(2,1)S(1)}, bf16[4,448,128]{2,1,0:T(8,128)(2,1)S(1)}, u32[]{:S(2)}, u32[]{:S(2)}) collective-permute-start(bf16[4,448,128]{2,1,0:T(8,128)(2,1)S(1)} %collective-permute-done.2.refs_8_), channel_id=1, source_target_pairs={{64,0},{128,64},{192,128},{256,192},{320,256},{384,320},{65,1},{12... | collective-permute-start | bytes 1376264 | tf_op jit(solution)/shard_map/ppermute | solution.py:190
  40.1 11.3 %collective-permute-start.3 = (bf16[4,448,128]{2,1,0:T(8,128)(2,1)S(1)}, bf16[4,448,128]{2,1,0:T(8,128)(2,1)S(1)}, u32[]{:S(2)}, u32[]{:S(2)}) collective-permute-start(bf16[4,448,128]{2,1,0:T(8,128)(2,1)S(1)} %collective-permute-done.1.refs_2_), channel_id=1, source_target_pairs={{128,192},{192,256},{256,320},{320,384},{384,448},{129,193},{193,2... | collective-permute-start | bytes 1376264 | tf_op jit(solution)/shard_map/ppermute | solution.py:189
  50.1 12.5 %collective-permute-start.6 = (bf16[4,448,128]{2,1,0:T(8,128)(2,1)S(1)}, bf16[4,448,128]{2,1,0:T(8,128)(2,1)S(1)}, u32[]{:S(2)}, u32[]{:S(2)}) collective-permute-start(bf16[4,448,128]{2,1,0:T(8,128)(2,1)S(1)} %collective-permute-done.4.refs_9_), channel_id=1, source_target_pairs={{64,0},{128,64},{192,128},{256,192},{320,256},{65,1},{129,65},{193... | collective-permute-start | bytes 1376264 | tf_op jit(solution)/shard_map/ppermute | solution.py:190
  51.4 28.0 %collective-permute-start.5 = (bf16[4,448,128]{2,1,0:T(8,128)(2,1)S(1)}, bf16[4,448,128]{2,1,0:T(8,128)(2,1)}, u32[]{:S(2)}, u32[]{:S(2)}) collective-permute-start(bf16[4,448,128]{2,1,0:T(8,128)(2,1)S(1)} %collective-permute-done.3.refs_3_), channel_id=1, source_target_pairs={{192,256},{256,320},{320,384},{384,448},{193,257},{257,321},{321,3... | collective-permute-start | bytes 1376264 | tf_op jit(solution)/shard_map/ppermute | solution.py:189
  62.6 18.3 %collective-permute-start.8 = (bf16[4,448,128]{2,1,0:T(8,128)(2,1)S(1)}, bf16[4,448,128]{2,1,0:T(8,128)(2,1)}, u32[]{:S(2)}, u32[]{:S(2)}) collective-permute-start(bf16[4,448,128]{2,1,0:T(8,128)(2,1)S(1)} %collective-permute-done.6.refs_10_), channel_id=1, source_target_pairs={{64,0},{128,64},{192,128},{256,192},{65,1},{129,65},{193,129},{257... | collective-permute-start | bytes 1376264 | tf_op jit(solution)/shard_map/ppermute | solution.py:190
  65.7 13.7 %all-to-all-start.1 = ((f32[8,8,512]{2,1,0:T(8,128)}), f32[8,8,512]{2,1,0:T(8,128)S(1)}, u32[]{:S(2)}, u32[]{:S(2)}) async-start(f32[8,8,512]{2,1,0:T(8,128)} %convolution_bitcast_fusion), calls=%async_computation.1 | async-start | bytes 262144 | tf_op jit(solution)/shard_map/all_to_all | solution.py:263
  74.1 98.6 %all-gather.8.cloned.1.call-start = ((), (), s32[]{:S(2)}) async-start(), calls=%async_computation.7 | async-start | bytes 1622016 | tf_op jit(solution)/shard_map/all_gather | solution.py:235
  79.4 15.1 %collective-permute-start.7 = (bf16[4,448,128]{2,1,0:T(8,128)(2,1)}, bf16[4,448,128]{2,1,0:T(8,128)(2,1)}, u32[]{:S(2)}, u32[]{:S(2)}) collective-permute-start(bf16[4,448,128]{2,1,0:T(8,128)(2,1)} %collective-permute-done.5.refs_4_), channel_id=1, source_target_pairs={{256,320},{320,384},{384,448},{257,321},{321,385},{385,449},{258,3... | collective-permute-start | bytes 1376264 | tf_op jit(solution)/shard_map/ppermute | solution.py:189
  80.9 15.1 %collective-permute-start.10 = (bf16[4,448,128]{2,1,0:T(8,128)(2,1)}, bf16[4,448,128]{2,1,0:T(8,128)(2,1)}, u32[]{:S(2)}, u32[]{:S(2)}) collective-permute-start(bf16[4,448,128]{2,1,0:T(8,128)(2,1)} %collective-permute-done.8.refs_11_), channel_id=1, source_target_pairs={{64,0},{128,64},{192,128},{65,1},{129,65},{193,129},{66,2},{130,66... | collective-permute-start | bytes 1376264 | tf_op jit(solution)/shard_map/ppermute | solution.py:190
  94.5 3.4 %collective-permute-start.9 = (bf16[4,448,128]{2,1,0:T(8,128)(2,1)}, bf16[4,448,128]{2,1,0:T(8,128)(2,1)}, u32[]{:S(2)}, u32[]{:S(2)}) collective-permute-start(bf16[4,448,128]{2,1,0:T(8,128)(2,1)} %collective-permute-done.7.refs_5_), channel_id=1, source_target_pairs={{320,384},{384,448},{321,385},{385,449},{322,386},{386,450},{323,3... | collective-permute-start | bytes 1376264 | tf_op jit(solution)/shard_map/ppermute | solution.py:189
  96.0 24.1 %collective-permute-start.12 = (bf16[4,448,128]{2,1,0:T(8,128)(2,1)}, bf16[4,448,128]{2,1,0:T(8,128)(2,1)}, u32[]{:S(2)}, u32[]{:S(2)}) collective-permute-start(bf16[4,448,128]{2,1,0:T(8,128)(2,1)} %collective-permute-done.10.refs_12_), channel_id=1, source_target_pairs={{64,0},{128,64},{65,1},{129,65},{66,2},{130,66},{67,3},{131,67},{6... | collective-permute-start | bytes 1376264 | tf_op jit(solution)/shard_map/ppermute | solution.py:190
  103.8 25.1 %collective-permute-start.11 = (bf16[4,448,128]{2,1,0:T(8,128)(2,1)}, bf16[4,448,128]{2,1,0:T(8,128)(2,1)}, u32[]{:S(2)}, u32[]{:S(2)}) collective-permute-start(bf16[4,448,128]{2,1,0:T(8,128)(2,1)} %collective-permute-done.9.refs_6_), channel_id=1, source_target_pairs={{384,448},{385,449},{386,450},{387,451},{388,452},{389,453},{390,4... | collective-permute-start | bytes 1376264 | tf_op jit(solution)/shard_map/ppermute | solution.py:189
  120.1 11.9 %collective-permute-start.13 = (bf16[4,448,128]{2,1,0:T(8,128)(2,1)}, bf16[4,448,128]{2,1,0:T(8,128)(2,1)}, u32[]{:S(2)}, u32[]{:S(2)}) collective-permute-start(bf16[4,448,128]{2,1,0:T(8,128)(2,1)} %collective-permute-done.12.refs_13_), channel_id=1, source_target_pairs={{64,0},{65,1},{66,2},{67,3},{68,4},{69,5},{70,6},{71,7},{72,8},{73... | collective-permute-start | bytes 1376264 | tf_op jit(solution)/shard_map/ppermute | solution.py:190
  122.4 24.3 %all-to-all-start.3 = ((f32[32,8,512]{2,1,0:T(8,128)}), f32[32,8,512]{2,1,0:T(8,128)}, u32[]{:S(2)}, u32[]{:S(2)}) async-start(f32[32,8,512]{2,1,0:T(8,128)} %broadcast_in_dim.46), calls=%async_computation.3 | async-start | bytes 1048576 | tf_op jit(solution)/shard_map/all_to_all | solution.py:88
  146.7 20.7 %all-to-all-start.2 = ((f32[32,2,2048]{2,1,0:T(2,128)}), f32[32,2,2048]{2,1,0:T(2,128)S(1)}, u32[]{:S(2)}, u32[]{:S(2)}) async-start(f32[32,2,2048]{2,1,0:T(2,128)} %layer.1), calls=%async_computation.2 | async-start | bytes 1048576 | tf_op jit(solution)/shard_map/all_to_all | solution.py:279
  169.1 15.9 %all-to-all-start.4 = ((f32[16,12,128]{2,1,0:T(8,128)}), f32[16,12,128]{2,1,0:T(8,128)S(1)}, u32[]{:S(2)}, u32[]{:S(2)}) async-start(f32[16,12,128]{2,1,0:T(8,128)} %broadcast_in_dim.48), calls=%async_computation.4 | async-start | bytes 262144 | tf_op jit(solution)/shard_map/all_to_all | solution.py:88
  186.0 20.2 %all-to-all-start.5 = ((bf16[32,96,128]{2,1,0:T(8,128)(2,1)}), bf16[32,96,128]{2,1,0:T(8,128)(2,1)S(1)}, u32[]{:S(2)}, u32[]{:S(2)}) async-start(bf16[32,96,128]{2,1,0:T(8,128)(2,1)} %broadcast_in_dim.49), calls=%async_computation.5 | async-start | bytes 1572864 | tf_op jit(solution)/shard_map/all_to_all | solution.py:88
Sparse Core Ops, SparseCore 0:
  9.8 93.9 all-gather.5
  106.9 62.6 all-gather.7
